TPU v7x, 512 devices: a whole 4x4x16 slice. The times are simulated.
512 devices in a mesh: dp: 8 (over x, z_hi), ctx: 64 (over y, z_lo, core).
Axes of the slice: x: 4, y: 4, z: 16 (z_hi: 2, z_lo: 8; z = z_hi * 8 + z_lo), core: 2. Of those that a mesh axis runs over, the one named last changes fastest.
Arguments:
- inputs: float32 [8, 2048, 8192], P('dp', None, 'ctx'), may hold values from -6 to 6
- grad_out: float32 [8, 2048, 8192], P('dp', None, 'ctx'), may hold values from -6 to 6
- filters: float32 [2048, 8192], P(('dp', 'ctx')), may hold values from -0.0625 to 0.0625
Outputs:
- input_grad: float32 [8, 2048, 8192], P('dp', None, 'ctx')
- filter_grad: float32 [2048, 8192], P(('dp', 'ctx'))
All inputs are finite; a program needn't handle non-finite values.
Results may differ from a plain program's by a relative error of at most 0.000098.
Values sent between devices are 32-bit elements; how exact they have to be, the bound alone decides.
No kernel may reach another device: no remote copies, remote signals or barrier semaphores. Data moves between devices by JAX's collectives and lax.ppermute only.
A program may use at most 64 MiB of HBM per device.

v0:
```python
import math

import jax
import jax.numpy as jnp
from jax import lax
from jax.sharding import PartitionSpec as P


def dft_tables(seq_length):
    inner_size = 128
    padded_size = 2 * seq_length
    outer_size = padded_size // inner_size
    signal_rows = seq_length // inner_size
    freq_count = outer_size // 2 + 1
    two_pi = 2.0 * math.pi
    order_rows = jnp.arange(signal_rows, dtype=jnp.int32)
    order_freq = jnp.arange(freq_count, dtype=jnp.int32)
    order_inner = jnp.arange(inner_size, dtype=jnp.int32)
    angle_outer = (
        two_pi
        / outer_size
        * (order_rows[:, None] * order_freq[None, :] % outer_size).astype(jnp.float32)
    )
    cos_outer = jnp.cos(angle_outer)
    sin_outer = jnp.sin(angle_outer)
    first_table = jnp.concatenate([cos_outer, -sin_outer], axis=1)
    weights = jnp.where((order_freq == 0) | (order_freq == freq_count - 1), 1.0, 2.0).astype(
        jnp.float32
    )
    last_table = jnp.concatenate(
        [(cos_outer * weights[None, :]).T, (-sin_outer * weights[None, :]).T], axis=0
    )
    angle_inner = (
        two_pi
        / inner_size
        * (order_inner[:, None] * order_inner[None, :] % inner_size).astype(jnp.float32)
    )
    cos_inner = jnp.cos(angle_inner)
    sin_inner = jnp.sin(angle_inner)
    forward_block = jnp.concatenate(
        [
            jnp.concatenate([cos_inner, -sin_inner], axis=1),
            jnp.concatenate([sin_inner, cos_inner], axis=1),
        ],
        axis=0,
    )
    inverse_block = jnp.concatenate(
        [
            jnp.concatenate([cos_inner, sin_inner], axis=1),
            jnp.concatenate([-sin_inner, cos_inner], axis=1),
        ],
        axis=0,
    )
    angle_turn = (
        two_pi
        / padded_size
        * (order_freq[:, None] * order_inner[None, :] % padded_size).astype(jnp.float32)
    )
    return (
        first_table,
        last_table,
        forward_block,
        inverse_block,
        jnp.cos(angle_turn),
        jnp.sin(angle_turn),
        freq_count,
        signal_rows,
        padded_size,
    )


def forward_spectrum(signal, tables):
    (
        first_table,
        last_table,
        forward_block,
        inverse_block,
        cos_turn,
        sin_turn,
        freq_count,
        signal_rows,
        padded_size,
    ) = tables
    highest = lax.Precision.HIGHEST
    row_count = signal.shape[0]
    shaped = signal.reshape(row_count, signal_rows, 128)
    first = jnp.einsum("man,ak->mkn", shaped, first_table, precision=highest)
    first_real = first[:, :freq_count]
    first_imag = first[:, freq_count:]
    turned = jnp.concatenate(
        [
            first_real * cos_turn + first_imag * sin_turn,
            first_imag * cos_turn - first_real * sin_turn,
        ],
        axis=-1,
    )
    return jnp.einsum("mkn,nj->mkj", turned, forward_block, precision=highest)


def inverse_signal(spec_real, spec_imag, tables):
    (
        first_table,
        last_table,
        forward_block,
        inverse_block,
        cos_turn,
        sin_turn,
        freq_count,
        signal_rows,
        padded_size,
    ) = tables
    highest = lax.Precision.HIGHEST
    row_count = spec_real.shape[0]
    stacked = jnp.concatenate([spec_real, spec_imag], axis=-1)
    middle = jnp.einsum("mkj,jn->mkn", stacked, inverse_block, precision=highest)
    middle_real = middle[..., :128]
    middle_imag = middle[..., 128:]
    back = jnp.concatenate(
        [
            middle_real * cos_turn - middle_imag * sin_turn,
            middle_imag * cos_turn + middle_real * sin_turn,
        ],
        axis=1,
    )
    result = jnp.einsum("mkn,ka->man", back, last_table, precision=highest)
    return (result / padded_size).reshape(row_count, -1)


def shards(inputs, grad_out, filters):
    dp_count = lax.axis_size("dp")
    ctx_count = lax.axis_size("ctx")
    seq_local, channel_count, local_tokens = inputs.shape
    owned_channels = channel_count // (dp_count * ctx_count)
    seq_length = local_tokens * ctx_count
    tables = dft_tables(seq_length)
    freq_count = tables[6]
    split_shape = (seq_local, dp_count, ctx_count, owned_channels, local_tokens)
    split_input = inputs.reshape(split_shape)
    split_grad = grad_out.reshape(split_shape)
    norm_factor = 1.0 / math.sqrt(seq_local * dp_count * seq_length)
    moved_input, moved_grad = (
        lax.all_to_all(split_input, "ctx", split_axis=2, concat_axis=4, tiled=True),
        lax.all_to_all(split_grad, "ctx", split_axis=2, concat_axis=4, tiled=True),
    )
    channels = dp_count * owned_channels
    filter_rows = lax.all_gather(filters, "dp", axis=0, tiled=True)
    spec_shape = (seq_local, channels, freq_count, 256)
    input_spec = forward_spectrum(
        moved_input.reshape(seq_local * channels, seq_length), tables
    ).reshape(spec_shape)
    grad_spec = forward_spectrum(
        moved_grad.reshape(seq_local * channels, seq_length), tables
    ).reshape(spec_shape)
    filter_spec = forward_spectrum(filter_rows, tables)[None]
    input_real = input_spec[..., :128]
    input_imag = input_spec[..., 128:]
    grad_real = grad_spec[..., :128]
    grad_imag = grad_spec[..., 128:]
    filter_real = filter_spec[..., :128]
    filter_imag = filter_spec[..., 128:]
    product_real = grad_real * filter_real + grad_imag * filter_imag
    product_imag = grad_imag * filter_real - grad_real * filter_imag
    input_part = inverse_signal(
        product_real.reshape(seq_local * channels, freq_count, 128),
        product_imag.reshape(seq_local * channels, freq_count, 128),
        tables,
    )
    corr_real = jnp.sum(grad_real * input_real + grad_imag * input_imag, axis=0)
    corr_imag = jnp.sum(grad_imag * input_real - grad_real * input_imag, axis=0)
    filter_part = inverse_signal(corr_real, corr_imag, tables) * norm_factor
    leaving = input_part.reshape(seq_local, dp_count, 1, owned_channels, seq_length)
    returned = lax.all_to_all(leaving, "ctx", split_axis=4, concat_axis=2, tiled=True)
    summed = lax.psum_scatter(
        filter_part.reshape(dp_count, owned_channels, seq_length),
        "dp",
        scatter_dimension=0,
        tiled=True,
    )
    filter_grad = summed.reshape(owned_channels, seq_length)
    input_grad = returned.reshape(seq_local, channel_count, local_tokens)
    return (input_grad, filter_grad)


def solution(mesh):
    placed = (P("dp", None, "ctx"), P("dp", None, "ctx"), P(("dp", "ctx"), None))
    return jax.shard_map(
        shards,
        mesh=mesh,
        in_specs=placed,
        out_specs=(P("dp", None, "ctx"), P(("dp", "ctx"), None)),
        check_vma=False,
    )
```

profile of v0, /device:TPU:6, one launch (start us, length us, event | category | flops | bytes accessed | tf_op | source)
XLA Modules:
  0.0 564.4 jit_solution(7946573195563729075)
XLA Ops:
  7.2 2.5 copy.18
  9.7 16.3 %all-to-all-start = ((f32[1,8,64,4,128]{4,3,1,0,2:T(4,128)}), f32[1,8,64,4,128]{4,3,1,0,2:T(4,128)S(1)}, u32[]{:S(2)}, u32[]{:S(2)}) async-start(f32[1,8,64,4,128]{4,3,1,0,2:T(4,128)} %copy.18), calls=%async_computation | async-start | bytes 2097152 | tf_op jit(solution)/shard_map/all_to_all | solution.py:143
  27.3 50.1 %all-to-all-done = f32[1,8,64,4,128]{4,3,1,0,2:T(4,128)S(1)} async-done(((f32[1,8,64,4,128]{4,3,1,0,2:T(4,128)}), f32[1,8,64,4,128]{4,3,1,0,2:T(4,128)S(1)}, u32[]{:S(2)}, u32[]{:S(2)}) %all-to-all-start) | async-done | bytes 1048608 | tf_op jit(solution)/shard_map/all_to_all | solution.py:143
  77.4 8.3 %all-to-all-start.2 = ((f32[1,8,64,4,128]{4,3,1,0,2:T(4,128)}), f32[1,8,64,4,128]{4,3,1,0,2:T(4,128)}, u32[]{:S(2)}, u32[]{:S(2)}) async-start(f32[1,8,64,4,128]{4,3,1,0,2:T(4,128)} %copy.22), calls=%async_computation.2 | async-start | bytes 2097152 | tf_op jit(solution)/shard_map/all_to_all | solution.py:142
  88.7 99.1 %all-gather.3.cloned.1.call-done = f32[8,4,8192]{2,1,0:T(4,128)} async-done(((f32[1,4,8192]{2,1,0:T(4,128)}), f32[8,4,8192]{2,1,0:T(4,128)}) %all-gather.3.cloned.1.call-update) | async-done | bytes 1048592 | tf_op jit(solution)/shard_map/all_gather | solution.py:146
  189.8 2.0 convolution_bitcast_fusion.1
  192.4 3.4 convolution_bitcast_fusion.2
  197.7 2.0 convolution_bitcast_fusion
  200.7 2.3 fusion.31
  202.9 2.1 fusion.34
  205.0 2.1 fusion.28
  207.9 2.1 fusion.8
  210.0 2.1 fusion.16
  212.9 2.4 fusion.46
  217.0 10.7 %copy.20 = f32[1,8,1,4,8192]{1,3,2,0,4:T(4,128)} copy(f32[1,8,1,4,8192]{4,3,1,2,0:T(4,128)S(1)} %reshape_reshape.10) | data formatting | bytes 2097152 | tf_op jit(solution)/shard_map/reshape;reshape | solution.py:171
  227.7 22.0 %reshape.102 = f32[64,1,4096]{2,1,0:T(1,128)} reshape(f32[8192,1,1,4,8]{4,3,2,1,0:T(4,128)} %bitcast.65) | data formatting | bytes 2097152
  249.7 5.7 %all-to-all-start.1 = ((f32[64,1,4096]{2,1,0:T(1,128)}), f32[64,1,4096]{2,1,0:T(1,128)S(1)}, u32[]{:S(2)}, u32[]{:S(2)}) async-start(f32[64,1,4096]{2,1,0:T(1,128)} %reshape.102), calls=%async_computation.1 | async-start | bytes 2097152 | tf_op jit(solution)/shard_map/all_to_all | solution.py:172
  255.4 2.4 fusion.40
  257.8 2.6 mul.580
  261.8 255.4 %all-reduce.3.cloned.1.call-done = f32[8,4,8192]{2,1,0:T(4,128)} async-done(((f32[8,4,8192]{2,1,0:T(4,128)}), f32[8,4,8192]{2,1,0:T(4,128)}) %all-reduce.3.cloned.1.call-update) | async-done | bytes 1048592
  517.2 2.2 dynamic-slice_bitcast_fusion
  519.9 3.3 reduce
  523.2 21.2 %reshape.103 = f32[8192,1,1,4,8]{4,3,2,1,0:T(4,128)} reshape(f32[64,4096]{1,0:T(8,128)S(1)} %reduce) | data formatting | bytes 2097152
  544.4 13.0 %copy.21 = f32[1,8,64,1,4,128]{5,4,2,1,3,0:T(4,128)} copy(f32[1,8,64,1,4,128]{1,4,5,2,3,0:T(4,128)} %bitcast.66) | data formatting | bytes 2097152 | tf_op jit(solution)/shard_map/all_to_all | solution.py:172
  (38 shorter events, 14.7 us)
Async XLA Ops:
  9.7 16.3 %copy-start.3 = (f32[1,2048,128]{2,1,0:T(8,128)S(1)}, f32[1,2048,128]{2,1,0:T(8,128)}, u32[]{:S(2)}) copy-start(f32[1,2048,128]{2,1,0:T(8,128)} %param.3) | copy-start | bytes 3145732
  9.7 67.7 %all-to-all-start = ((f32[1,8,64,4,128]{4,3,1,0,2:T(4,128)}), f32[1,8,64,4,128]{4,3,1,0,2:T(4,128)S(1)}, u32[]{:S(2)}, u32[]{:S(2)}) async-start(f32[1,8,64,4,128]{4,3,1,0,2:T(4,128)} %copy.18), calls=%async_computation | async-start | bytes 2097152 | tf_op jit(solution)/shard_map/all_to_all | solution.py:143
  77.4 9.5 %copy-start.1 = (f32[1,8,64,4,128]{4,3,1,0,2:T(4,128)}, f32[1,8,64,4,128]{4,3,1,0,2:T(4,128)S(1)}, u32[]{:S(2)}) copy-start(f32[1,8,64,4,128]{4,3,1,0,2:T(4,128)S(1)} %all-to-all-done) | copy-start | bytes 3145732
  77.4 118.4 %all-to-all-start.2 = ((f32[1,8,64,4,128]{4,3,1,0,2:T(4,128)}), f32[1,8,64,4,128]{4,3,1,0,2:T(4,128)}, u32[]{:S(2)}, u32[]{:S(2)}) async-start(f32[1,8,64,4,128]{4,3,1,0,2:T(4,128)} %copy.22), calls=%async_computation.2 | async-start | bytes 2097152 | tf_op jit(solution)/shard_map/all_to_all | solution.py:142
  85.7 102.1 %all-gather.3.cloned.1.call-start = ((), (), s32[]{:S(2)}) async-start(), calls=%async_computation.3 | async-start | bytes 1179648 | tf_op jit(solution)/shard_map/all_gather | solution.py:146
  189.7 2.0 copy-start.2
  197.6 2.1 copy-start
  197.7 2.1 copy-start.4
  197.7 2.1 copy-start.5
  212.1 0.8 copy-start.6
  212.1 0.8 copy-start.7
  249.7 269.7 %all-to-all-start.1 = ((f32[64,1,4096]{2,1,0:T(1,128)}), f32[64,1,4096]{2,1,0:T(1,128)S(1)}, u32[]{:S(2)}, u32[]{:S(2)}) async-start(f32[64,1,4096]{2,1,0:T(1,128)} %reshape.102), calls=%async_computation.1 | async-start | bytes 2097152 | tf_op jit(solution)/shard_map/all_to_all | solution.py:172
  255.4 261.8 %all-reduce.3.cloned.1.call-start = ((), (), s32[]{:S(2)}) async-start(), calls=%async_computation.4 | async-start | bytes 2097152
Sparse Core Ops, SparseCore 0:
  89.8 98.0 all-gather.2
  260.6 256.5 all-reduce.2
where the time goes:
time: 569 us; the launch traced here: 564 us
  waiting for transfers between devices  405 us (71%)
  local copies, waits for them, and re-layouts  83.7 us (15%)
  starting transfers between devices  30.8 us (5%)
  matrix products  22.9 us (4%)
  between operations  14.5 us (3%)
  other arithmetic  7.71 us (1%)
    unnamed x3, waiting for transfers between devices  256 us
    all_gather x1, waiting for transfers between devices, shards(): filter_rows = lax.all_gather(filters, 'dp', axis=0, tiled=True)  99.1 us
    all_to_all x1, waiting for transfers between devices, shards(): lax.all_to_all(split_grad, 'ctx', split_axis=2, concat_axis=4, tiled=True)  50.1 us
    unnamed x19, local copies, waits for them, and re-layouts  44.8 us
    all_to_all x1, starting transfers between devices, shards(): lax.all_to_all(split_grad, 'ctx', split_axis=2, concat_axis=4, tiled=True)  16.3 us
    all_to_all x2, local copies, waits for them, and re-layouts, shards(): lax.all_to_all(leaving, 'ctx', split_axis=4, concat_axis=2, tiled=True)  13.5 us
    another operation x2, local copies, waits for them, and re-layouts, shards(): input_part.reshape(seq_local, dp_count, 1, owned_channels, seq_length)  12.4 us
  transfers between devices with their start and end apart: 5, of which 3 were waited for; matrix products, arithmetic and copies ran while one was open for 4% of the time, Pallas kernels for 0%

commit v1 on v0

v1 whole, which is shorter than its diff:
```python
import math

import jax
import jax.numpy as jnp
import numpy as np
from jax import lax
from jax.experimental import pallas as pl
from jax.experimental.pallas import tpu as pltpu
from jax.sharding import Mesh
from jax.sharding import PartitionSpec as P

INNER = 128
HIGH = lax.Precision.HIGH


def dft_tables(seq_length):
    padded = 2 * seq_length
    outer = padded // INNER
    rows = seq_length // INNER
    freqs = outer // 2 + 1
    row, freq, inner = np.arange(rows), np.arange(freqs), np.arange(INNER)
    angle = 2.0 * np.pi / outer * (row[:, None] * freq[None, :] % outer)
    cos_outer, sin_outer = np.cos(angle), np.sin(angle)
    first = np.concatenate([cos_outer, -sin_outer], axis=1)
    weights = np.where((freq == 0) | (freq == freqs - 1), 1.0, 2.0) / padded
    last = np.concatenate([cos_outer * weights, -sin_outer * weights], axis=1)
    angle = 2.0 * np.pi / INNER * (inner[:, None] * inner[None, :] % INNER)
    cos_inner, sin_inner = np.cos(angle), np.sin(angle)
    forward = np.block([[cos_inner, -sin_inner], [sin_inner, cos_inner]])
    inverse = np.block([[cos_inner, sin_inner], [-sin_inner, cos_inner]])
    angle = 2.0 * np.pi / padded * (freq[:, None] * inner[None, :] % padded)
    return [
        np.asarray(t, np.float32)
        for t in (first, last, forward, inverse, np.cos(angle), np.sin(angle))
    ]


def forward_spectrum(signal, first_table, tables, form):
    _, _, forward, _, cos_turn, sin_turn = tables
    freqs = cos_turn.shape[0]
    first = jnp.einsum(form, signal, first_table, precision=HIGH)
    real, imag = first[:, :, :freqs], first[:, :, freqs:]
    turned = jnp.concatenate(
        [real * cos_turn + imag * sin_turn, imag * cos_turn - real * sin_turn], axis=-1
    )
    return jnp.einsum("bhkn,nj->bhkj", turned, forward, precision=HIGH)


def inverse_signal(real, imag, last_table, tables, form):
    _, _, _, inverse, cos_turn, sin_turn = tables
    stacked = jnp.concatenate([real, imag], axis=-1)
    middle = jnp.einsum("bhkj,jn->bhkn", stacked, inverse, precision=HIGH)
    middle_real, middle_imag = middle[..., :INNER], middle[..., INNER:]
    back = jnp.concatenate(
        [
            middle_real * cos_turn - middle_imag * sin_turn,
            middle_imag * cos_turn + middle_real * sin_turn,
        ],
        axis=2,
    )
    return jnp.einsum(form, back, last_table, precision=HIGH)


def pack_kernel(half, grad, tokens, blocks):
    _, _, y, z, _, _ = tokens.shape
    own, far = half[0], 1 - half[0]
    for i in range(y):
        for k in range(z):
            for n, array in enumerate((grad, tokens)):
                blocks[i, k, 0, n] = array[:, own, i, k]
                blocks[i, k, 1, n] = array[:, far, i, z - 1 - k]


def unpack_kernel(half, blocks, tokens):
    _, _, y, z, _, _ = tokens.shape
    own, far = half[0], 1 - half[0]
    for i in range(y):
        for k in range(z):
            tokens[:, own, i, k] = blocks[i, k, 0]
            tokens[:, far, i, z - 1 - k] = blocks[i, k, 1]


def moving(kernel, half, arrays, shape):
    whole = pl.BlockSpec(memory_space=pltpu.VMEM)
    size = 8 * math.prod(shape)
    return pl.pallas_call(
        kernel,
        out_shape=jax.ShapeDtypeStruct(shape, jnp.float32),
        in_specs=[pl.BlockSpec(memory_space=pltpu.SMEM)] + [whole] * len(arrays),
        out_specs=whole,
        cost_estimate=pl.CostEstimate(flops=0, bytes_accessed=size, transcendentals=0),
    )(half, *arrays)


def shards(inputs, grad_out, filters):
    x, h, y, z, c = (lax.axis_size(a) for a in ("x", "zh", "y", "zl", "c"))
    at_x, half, at_c = (lax.axis_index(a) for a in ("x", "zh", "c"))
    _, channels, block = inputs.shape
    j = channels // (x * h * y * z * c)
    seq_length = filters.shape[1]
    rows = y * z * c
    tables = dft_tables(seq_length)
    norm = 1.0 / math.sqrt(x * h * seq_length)
    first, last = jnp.asarray(tables[0]), jnp.asarray(tables[1]).T
    place = half.reshape(1).astype(jnp.int32)
    whole_shape = (x, h, y, z, c * j, INNER)
    block_shape = (rows, x, c * j, INNER)

    def exchange(blocks):
        return lax.all_to_all(blocks, ("y", "zl", "c"), 0, 0, tiled=True)

    swap = [(0, 1), (1, 0)]
    facing = []
    for i in range(h * z):
        facing += [(c * i, c * i), (c * i + 1, c * (h * z - 1 - i) + 1)]
    along_x = lambda v, s: lax.ppermute(v, "x", [(i, (i + s) % x) for i in range(x)])

    both = moving(
        pack_kernel,
        place,
        [grad_out.reshape(whole_shape), inputs.reshape(whole_shape)],
        (y, z, c, 2, x, c * j, INNER),
    )
    both = exchange(both.reshape(rows, 2, x, c * j, INNER))

    sibling = lax.ppermute(filters, "c", swap)
    tile = jnp.where(
        at_c == 0,
        jnp.concatenate([filters, sibling]),
        jnp.concatenate([sibling, filters]),
    )
    tile = lax.ppermute(tile, ("zh", "zl", "c"), facing)
    tiles = jnp.stack([tile] + [along_x(tile, x - s) for s in range(1, x)])
    tiles = jnp.roll(tiles, at_x, axis=0)
    filter_spec = forward_spectrum(
        tiles.reshape(x, c * j, rows, INNER), first, tables, "xham,ak->xhkm"
    )
    filter_real, filter_imag = filter_spec[..., :INNER], filter_spec[..., INNER:]

    grad_spec = forward_spectrum(both[:, 0], first, tables, "axhm,ak->xhkm")
    grad_real, grad_imag = grad_spec[..., :INNER], grad_spec[..., INNER:]
    input_part = inverse_signal(
        grad_real * filter_real + grad_imag * filter_imag,
        grad_imag * filter_real - grad_real * filter_imag,
        last,
        tables,
        "xhkm,ka->axhm",
    )
    returned = exchange(input_part)

    input_spec = forward_spectrum(both[:, 1], first, tables, "axhm,ak->xhkm")
    input_real, input_imag = input_spec[..., :INNER], input_spec[..., INNER:]
    filter_part = inverse_signal(
        grad_real * input_real + grad_imag * input_imag,
        grad_imag * input_real - grad_real * input_imag,
        last,
        tables,
        "xhkm,ka->xham",
    )
    parts = jnp.roll(filter_part.reshape(x, c, j, seq_length) * norm, -at_x, axis=0)
    part = parts[0] + sum(along_x(parts[s], s) for s in range(1, x))
    part = lax.ppermute(part, ("zh", "zl", "c"), facing)
    kept = lax.dynamic_index_in_dim(part, at_c, 0, keepdims=False)
    sent = lax.dynamic_index_in_dim(part, 1 - at_c, 0, keepdims=False)
    filter_grad = kept + lax.ppermute(sent, "c", swap)

    blocks = returned.reshape(y, z, c, x, c * j, INNER)
    input_grad = moving(unpack_kernel, place, [blocks], whole_shape)
    return (input_grad.reshape(1, channels, block), filter_grad)


def solution(mesh):
    count = mesh.devices.size
    devices = mesh.devices.reshape(4, 2, 4, count // 64, 2)
    fine = Mesh(devices, ("x", "zh", "y", "zl", "c"))
    tokens = P(("x", "zh"), None, ("y", "zl", "c"))
    owners = P(("x", "zh", "y", "zl", "c"), None)
    return jax.shard_map(
        shards,
        mesh=fine,
        in_specs=(tokens, tokens, owners),
        out_specs=(tokens, owners),
        check_vma=False,
    )
```

time: 569 us -> 225 us (0.40)
  waiting for transfers between devices: 405 us -> 126 us
  local copies, waits for them, and re-layouts: 83.7 us -> 8.25 us
  starting transfers between devices: 30.8 us -> 62.7 us
  between operations: 14.5 us -> 1.1 us
  matrix products: 22.9 us -> 11.5 us
    unnamed x3 -> x0, waiting for transfers between devices: 256 us -> none
    all_gather x1 -> x0, waiting for transfers between devices: 99.1 us -> none  [shards(): filter_rows = lax.all_gather(filters, 'dp', axis=0, tiled=True)]
    all_to_all x3 -> x2, waiting for transfers between devices: 50.1 us -> 113 us  [exchange(): return lax.all_to_all(blocks, ('y', 'zl', 'c'), 0, 0, tiled=True)]
    unnamed x19 -> x22, local copies, waits for them, and re-layouts: 44.8 us -> 2.62 us
    ppermute x0 -> x10, starting transfers between devices: none -> 31.8 us  [the longest x6 17.8 us: shards(): lax.ppermute(v, 'x', [(i, (i + s) % x) for i in range(x)])]
    all_to_all x4 -> x0, local copies, waits for them, and re-layouts: 16 us -> none  [the longest x2 13.5 us: shards(): lax.all_to_all(leaving, 'ctx', split_axis=4, concat_axis=2, tiled=True)]
    ppermute x0 -> x10, waiting for transfers between devices: none -> 13.1 us  [the longest x6 10.7 us: shards(): lax.ppermute(v, 'x', [(i, (i + s) % x) for i in range(x)])]
    another operation x2 -> x0, local copies, waits for them, and re-layouts: 12.4 us -> none  [shards(): input_part.reshape(seq_local, dp_count, 1, owned_channels, seq_length)]
  transfers between devices with their start and end apart: 5 -> 12, of which waited for: 3 -> 5; matrix products, arithmetic and copies ran while one was open for 4% -> 3% of each run, Pallas kernels for 0% -> 1%
where the time goes in v1:
time: 225 us; the launch traced here: 222 us
  waiting for transfers between devices  126 us (56%)
  starting transfers between devices  62.7 us (28%)
  matrix products  11.5 us (5%)
  local copies, waits for them, and re-layouts  8.25 us (4%)
  other arithmetic  6.98 us (3%)
  Pallas kernels  5.25 us (2%)
    all_to_all x2, waiting for transfers between devices, exchange(): return lax.all_to_all(blocks, ('y', 'zl', 'c'), 0, 0, tiled=True)  113 us
    all_to_all x2, starting transfers between devices, exchange(): return lax.all_to_all(blocks, ('y', 'zl', 'c'), 0, 0, tiled=True)  30.9 us
    ppermute x6, starting transfers between devices, shards(): lax.ppermute(v, 'x', [(i, (i + s) % x) for i in range(x)])  17.8 us
    ppermute x1, starting transfers between devices, shards(): filter_grad = kept + lax.ppermute(sent, 'c', swap)  10.7 us
    ppermute x6, waiting for transfers between devices, shards(): lax.ppermute(v, 'x', [(i, (i + s) % x) for i in range(x)])  10.7 us
    pallas_call x2, Pallas kernels, moving(): pl.pallas_call(kernel, out_shape=jax.ShapeDtypeStruct(shape, jnp.float32)...  5.25 us
  transfers between devices with their start and end apart: 12, of which 5 were waited for; matrix products, arithmetic and copies ran while one was open for 3% of the time, Pallas kernels for 1%

profile of v1, /device:TPU:6, one launch (start us, length us, event | category | flops | bytes accessed | tf_op | source)
XLA Modules:
  0.0 221.7 jit_solution(17704268568793201642)
XLA Ops:
  0.6 1.9 collective-permute-start
  2.6 1.5 collective-permute-done
  5.9 3.0 %shard_map.131 = f32[4,8,2,2,4,8,128]{6,5,4,3,2,1,0:T(8,128)} custom-call(s32[1]{0:T(128)} %bitcast.half, f32[4,2,4,8,8,128]{5,4,3,2,1,0:T(8,128)} %bitcast.79, f32[4,2,4,8,8,128]{5,4,3,2,1,0:T(8,128)} %bitcast.80), custom_call_target="tpu_custom_call" | custom-call | bytes 4194304 | tf_op jit(solution)/shard_map/pallas_call | solution.py:86
  8.8 21.6 %all-to-all-start = ((f32[64,2,4,8,128]{4,3,2,1,0:T(8,128)}), f32[64,2,4,8,128]{4,3,2,1,0:T(8,128)}, u32[]{:S(2)}, u32[]{:S(2)}) async-start(f32[64,2,4,8,128]{4,3,2,1,0:T(8,128)} %bitcast.77), calls=%async_computation | async-start | bytes 4194304 | tf_op jit(solution)/shard_map/all_to_all | solution.py:110
  30.5 2.4 %collective-permute-start.4 = (f32[8,8192]{1,0:T(8,128)S(1)}, f32[8,8192]{1,0:T(8,128)S(1)}, u32[]{:S(2)}, u32[]{:S(2)}) collective-permute-start(f32[8,8192]{1,0:T(8,128)S(1)} %collective-permute-done.1), channel_id=1, source_target_pairs={{0,128},{128,256},{256,384},{384,0},{1,129},{129,257},{257,385},{3... | collective-permute-start | bytes 786440 | tf_op jit(solution)/shard_map/ppermute | solution.py:116
  32.9 4.3 %collective-permute-start.3 = (f32[8,8192]{1,0:T(8,128)S(1)}, f32[8,8192]{1,0:T(8,128)S(1)}, u32[]{:S(2)}, u32[]{:S(2)}) collective-permute-start(f32[8,8192]{1,0:T(8,128)S(1)} %collective-permute-done.1), channel_id=1, source_target_pairs={{0,256},{128,384},{256,0},{384,128},{1,257},{129,385},{257,1},{385... | collective-permute-start | bytes 786440 | tf_op jit(solution)/shard_map/ppermute | solution.py:116
  37.2 1.9 collective-permute-start.2
  39.2 10.6 %collective-permute-done.2 = f32[8,8192]{1,0:T(8,128)S(1)} collective-permute-done((f32[8,8192]{1,0:T(8,128)S(1)}, f32[8,8192]{1,0:T(8,128)S(1)}, u32[]{:S(2)}, u32[]{:S(2)}) %collective-permute-start.2) | collective-permute-done | bytes 262176 | tf_op jit(solution)/shard_map/ppermute | solution.py:116
  52.0 72.9 %all-to-all-done = f32[64,2,4,8,128]{4,3,2,1,0:T(8,128)} async-done(((f32[64,2,4,8,128]{4,3,2,1,0:T(8,128)}), f32[64,2,4,8,128]{4,3,2,1,0:T(8,128)}, u32[]{:S(2)}, u32[]{:S(2)}) %all-to-all-start) | async-done | bytes 2097184 | tf_op jit(solution)/shard_map/all_to_all | solution.py:110
  124.9 1.7 fusion.45
  126.6 1.6 convolution_bitcast_fusion
  128.2 1.6 convolution_bitcast_fusion.2
  129.8 1.2 multiply_add_fusion.2
  139.3 1.4 mul.193
  140.7 1.7 fusion.34
  143.3 3.3 %collective-permute-start.6 = (f32[2,4,8192]{2,1,0:T(4,128)}, f32[2,4,8192]{2,1,0:T(4,128)}, u32[]{:S(2)}, u32[]{:S(2)}) collective-permute-start(f32[2,4,8192]{2,1,0:T(4,128)} %get-tuple-element.20), channel_id=1, source_target_pairs={{0,256},{128,384},{256,0},{384,128},{1,257},{129,385},{257,1},{385... | collective-permute-start | bytes 786440 | tf_op jit(solution)/shard_map/ppermute | solution.py:116
  146.6 4.0 %collective-permute-start.5 = (f32[2,4,8192]{2,1,0:T(4,128)}, f32[2,4,8192]{2,1,0:T(4,128)}, u32[]{:S(2)}, u32[]{:S(2)}) collective-permute-start(f32[2,4,8192]{2,1,0:T(4,128)} %get-tuple-element.21), channel_id=1, source_target_pairs={{0,128},{128,256},{256,384},{384,0},{1,129},{129,257},{257,385},{3... | collective-permute-start | bytes 786440 | tf_op jit(solution)/shard_map/ppermute | solution.py:116
  150.6 1.9 collective-permute-start.7
  153.4 1.6 copy.17
  154.9 9.3 %all-to-all-start.1 = ((f32[64,4,8,128]{3,2,1,0:T(8,128)}), f32[64,4,8,128]{3,2,1,0:T(8,128)S(1)}, u32[]{:S(2)}, u32[]{:S(2)}) async-start(f32[64,4,8,128]{3,2,1,0:T(8,128)} %copy.17), calls=%async_computation.1 | async-start | bytes 2097152 | tf_op jit(solution)/shard_map/all_to_all | solution.py:110
  164.2 1.2 fusion.37
  166.2 10.7 %collective-permute-start.9 = (f32[4,8192]{1,0:T(4,128)S(1)}, f32[4,8192]{1,0:T(4,128)S(1)}, u32[]{:S(2)}, u32[]{:S(2)}) collective-permute-start(f32[4,8192]{1,0:T(4,128)S(1)} %dynamic-slice_bitcast_fusion.1), channel_id=1, source_target_pairs={{0,1},{1,0},{2,3},{3,2},{4,5},{5,4},{6,7},{7,6},{8,9},{9,8},{10,11... | collective-permute-start | bytes 393224 | tf_op jit(solution)/shard_map/ppermute | solution.py:165
  178.6 39.8 %all-to-all-done.1 = f32[64,4,8,128]{3,2,1,0:T(8,128)S(1)} async-done(((f32[64,4,8,128]{3,2,1,0:T(8,128)}), f32[64,4,8,128]{3,2,1,0:T(8,128)S(1)}, u32[]{:S(2)}, u32[]{:S(2)}) %all-to-all-start.1) | async-done | bytes 1048608 | tf_op jit(solution)/shard_map/all_to_all | solution.py:110
  219.4 2.3 %shard_map.132 = f32[4,2,4,8,8,128]{5,4,3,2,1,0:T(8,128)} custom-call(s32[1]{0:T(128)} %bitcast.half, f32[4,8,2,4,8,128]{5,4,3,2,1,0:T(8,128)} %bitcast.78), custom_call_target="tpu_custom_call" | custom-call | bytes 2097152 | tf_op jit(solution)/shard_map/pallas_call | solution.py:86
  (47 shorter events, 17.2 us)
Async XLA Ops:
  0.6 3.5 %collective-permute-start = (f32[4,8192]{1,0:T(4,128)}, f32[4,8192]{1,0:T(4,128)S(1)}, u32[]{:S(2)}, u32[]{:S(2)}) collective-permute-start(f32[4,8192]{1,0:T(4,128)} %param.14), channel_id=1, source_target_pairs={{0,1},{1,0},{2,3},{3,2},{4,5},{5,4},{6,7},{7,6},{8,9},{9,8},{10,11... | collective-permute-start | bytes 393224 | tf_op jit(solution)/shard_map/ppermute | solution.py:126
  5.2 25.4 %collective-permute-start.1 = (f32[8,8192]{1,0:T(8,128)S(1)}, f32[8,8192]{1,0:T(8,128)S(1)}, u32[]{:S(2)}, u32[]{:S(2)}) collective-permute-start(f32[8,8192]{1,0:T(8,128)S(1)} %maximum_select_fusion), channel_id=1, source_target_pairs={{0,0},{1,79},{2,2},{3,77},{4,4},{5,75},{6,6},{7,73},{8,8},{9,71},{... | collective-permute-start | bytes 786440 | tf_op jit(solution)/shard_map/ppermute | solution.py:132
  8.8 116.0 %all-to-all-start = ((f32[64,2,4,8,128]{4,3,2,1,0:T(8,128)}), f32[64,2,4,8,128]{4,3,2,1,0:T(8,128)}, u32[]{:S(2)}, u32[]{:S(2)}) async-start(f32[64,2,4,8,128]{4,3,2,1,0:T(8,128)} %bitcast.77), calls=%async_computation | async-start | bytes 4194304 | tf_op jit(solution)/shard_map/all_to_all | solution.py:110
  30.5 19.4 %collective-permute-start.4 = (f32[8,8192]{1,0:T(8,128)S(1)}, f32[8,8192]{1,0:T(8,128)S(1)}, u32[]{:S(2)}, u32[]{:S(2)}) collective-permute-start(f32[8,8192]{1,0:T(8,128)S(1)} %collective-permute-done.1), channel_id=1, source_target_pairs={{0,128},{128,256},{256,384},{384,0},{1,129},{129,257},{257,385},{3... | collective-permute-start | bytes 786440 | tf_op jit(solution)/shard_map/ppermute | solution.py:116
  32.9 17.0 %collective-permute-start.3 = (f32[8,8192]{1,0:T(8,128)S(1)}, f32[8,8192]{1,0:T(8,128)S(1)}, u32[]{:S(2)}, u32[]{:S(2)}) collective-permute-start(f32[8,8192]{1,0:T(8,128)S(1)} %collective-permute-done.1), channel_id=1, source_target_pairs={{0,256},{128,384},{256,0},{384,128},{1,257},{129,385},{257,1},{385... | collective-permute-start | bytes 786440 | tf_op jit(solution)/shard_map/ppermute | solution.py:116
  37.2 12.6 %collective-permute-start.2 = (f32[8,8192]{1,0:T(8,128)S(1)}, f32[8,8192]{1,0:T(8,128)S(1)}, u32[]{:S(2)}, u32[]{:S(2)}) collective-permute-start(f32[8,8192]{1,0:T(8,128)S(1)} %collective-permute-done.1), channel_id=1, source_target_pairs={{0,384},{128,0},{256,128},{384,256},{1,385},{129,1},{257,129},{385... | collective-permute-start | bytes 786440 | tf_op jit(solution)/shard_map/ppermute | solution.py:116
  50.1 0.8 copy-start.3
  128.2 1.6 copy-start.5
  128.2 1.6 copy-start.6
  129.8 1.2 copy-start.1
  134.3 1.0 copy-start.2
  137.4 0.8 copy-start.4
  143.3 20.9 %collective-permute-start.6 = (f32[2,4,8192]{2,1,0:T(4,128)}, f32[2,4,8192]{2,1,0:T(4,128)}, u32[]{:S(2)}, u32[]{:S(2)}) collective-permute-start(f32[2,4,8192]{2,1,0:T(4,128)} %get-tuple-element.20), channel_id=1, source_target_pairs={{0,256},{128,384},{256,0},{384,128},{1,257},{129,385},{257,1},{385... | collective-permute-start | bytes 786440 | tf_op jit(solution)/shard_map/ppermute | solution.py:116
  146.6 17.6 %collective-permute-start.5 = (f32[2,4,8192]{2,1,0:T(4,128)}, f32[2,4,8192]{2,1,0:T(4,128)}, u32[]{:S(2)}, u32[]{:S(2)}) collective-permute-start(f32[2,4,8192]{2,1,0:T(4,128)} %get-tuple-element.21), channel_id=1, source_target_pairs={{0,128},{128,256},{256,384},{384,0},{1,129},{129,257},{257,385},{3... | collective-permute-start | bytes 786440 | tf_op jit(solution)/shard_map/ppermute | solution.py:116
  150.6 13.6 %collective-permute-start.7 = (f32[2,4,8192]{2,1,0:T(4,128)}, f32[2,4,8192]{2,1,0:T(4,128)}, u32[]{:S(2)}, u32[]{:S(2)}) collective-permute-start(f32[2,4,8192]{2,1,0:T(4,128)} %get-tuple-element.22), channel_id=1, source_target_pairs={{0,384},{128,0},{256,128},{384,256},{1,385},{129,1},{257,129},{385... | collective-permute-start | bytes 786440 | tf_op jit(solution)/shard_map/ppermute | solution.py:116
  154.9 63.5 %all-to-all-start.1 = ((f32[64,4,8,128]{3,2,1,0:T(8,128)}), f32[64,4,8,128]{3,2,1,0:T(8,128)S(1)}, u32[]{:S(2)}, u32[]{:S(2)}) async-start(f32[64,4,8,128]{3,2,1,0:T(8,128)} %copy.17), calls=%async_computation.1 | async-start | bytes 2097152 | tf_op jit(solution)/shard_map/all_to_all | solution.py:110
  165.5 0.7 collective-permute-start.8
  166.2 11.7 %collective-permute-start.9 = (f32[4,8192]{1,0:T(4,128)S(1)}, f32[4,8192]{1,0:T(4,128)S(1)}, u32[]{:S(2)}, u32[]{:S(2)}) collective-permute-start(f32[4,8192]{1,0:T(4,128)S(1)} %dynamic-slice_bitcast_fusion.1), channel_id=1, source_target_pairs={{0,1},{1,0},{2,3},{3,2},{4,5},{5,4},{6,7},{7,6},{8,9},{9,8},{10,11... | collective-permute-start | bytes 393224 | tf_op jit(solution)/shard_map/ppermute | solution.py:165
  218.4 1.0 copy-start

commit v2 on v1

v2 whole, which is shorter than its diff:
```python
import math

import jax
import jax.numpy as jnp
import numpy as np
from jax import lax
from jax.experimental import pallas as pl
from jax.experimental.pallas import tpu as pltpu
from jax.sharding import Mesh
from jax.sharding import PartitionSpec as P

INNER = 128
HALF = 72


def two_parts(table):
    high = np.asarray(table, np.float32).astype(jnp.bfloat16)
    return high, (table - high.astype(np.float64)).astype(jnp.bfloat16)


def dft_tables(seq_length, norm):
    padded = 2 * seq_length
    outer = padded // INNER
    rows = seq_length // INNER
    freqs = outer // 2 + 1
    row, freq, inner = np.arange(rows), np.arange(freqs), np.arange(INNER)
    pad = ((0, HALF - freqs), (0, 0))
    angle = 2.0 * np.pi / outer * (freq[:, None] * row[None, :] % outer)
    cos_outer, sin_outer = np.pad(np.cos(angle), pad), np.pad(np.sin(angle), pad)
    weights = np.where((freq == 0) | (freq == freqs - 1), 1.0, 2.0)[:, None] / padded
    weights = np.pad(weights, pad)
    high, low = two_parts(np.concatenate([cos_outer, -sin_outer], axis=0))
    first = np.concatenate([high, high, low], axis=1)
    last = np.concatenate([cos_outer * weights, -sin_outer * weights], axis=0).T
    angle = 2.0 * np.pi / INNER * (inner[:, None] * inner[None, :] % INNER)
    cos_inner, sin_inner = np.cos(angle), np.sin(angle)
    forward = np.block([[cos_inner, -sin_inner], [sin_inner, cos_inner]])
    inverse = np.block([[cos_inner, sin_inner], [-sin_inner, cos_inner]])
    angle = 2.0 * np.pi / padded * (freq[:, None] * inner[None, :] % padded)
    turn = np.stack([np.pad(np.cos(angle), pad), np.pad(np.sin(angle), pad)])
    pairs = dict(last=last, last_scaled=last * norm, forward=forward, inverse=inverse)
    tables = {name: jnp.asarray(np.stack(two_parts(t))) for name, t in pairs.items()}
    tables["first"] = jnp.asarray(first)
    tables["turn"] = jnp.asarray(turn, jnp.float32)
    return tables


def split(values):
    high = values.astype(jnp.bfloat16)
    return high, (values - high.astype(jnp.float32)).astype(jnp.bfloat16)


def dot(a, b):
    return jnp.dot(a, b, preferred_element_type=jnp.float32)


def forward_spectrum(wide, first, turn, forward):
    high, low = split(wide)
    outer = dot(first[...], jnp.concatenate([high, low, high], axis=0))
    cos, sin = turn[0], turn[1]
    turned = []
    for at in range(0, wide.shape[1], INNER):
        real, imag = outer[:HALF, at : at + INNER], outer[HALF:, at : at + INNER]
        turned.append(
            jnp.concatenate([real * cos + imag * sin, imag * cos - real * sin], axis=1)
        )
    high, low = split(jnp.concatenate(turned, axis=0))
    return dot(high, forward[0]) + (dot(low, forward[0]) + dot(high, forward[1]))


def correlate(spec, other):
    real, imag = spec[:, :INNER], spec[:, INNER:]
    other_real, other_imag = other[:, :INNER], other[:, INNER:]
    return jnp.concatenate(
        [real * other_real + imag * other_imag, imag * other_real - real * other_imag], axis=1
    )


def inverse_signal(spec, inverse, turn, last):
    high, low = split(spec)
    middle = dot(high, inverse[0]) + (dot(low, inverse[0]) + dot(high, inverse[1]))
    cos, sin = turn[0], turn[1]
    back = []
    for at in range(0, spec.shape[0], HALF):
        real, imag = middle[at : at + HALF, :INNER], middle[at : at + HALF, INNER:]
        back.append(
            jnp.concatenate([real * cos - imag * sin, imag * cos + real * sin], axis=0)
        )
    high, low = split(jnp.concatenate(back, axis=1))
    return dot(last[0], high) + (dot(last[0], low) + dot(last[1], high))


def rows_to_wide(block):
    return jnp.concatenate([block[:, r, :] for r in range(block.shape[1])], axis=1)


def filter_kernel(first, turn, forward, filters, spec):
    wide = jnp.concatenate([filters[r] for r in range(filters.shape[0])], axis=1)
    spec[...] = forward_spectrum(wide, first, turn, forward)


def input_grad_kernel(at, first, turn, forward, inverse, last, grad, filter_spec, spec, out):
    spec[...] = forward_spectrum(rows_to_wide(grad), first, turn, forward)
    wide = inverse_signal(correlate(spec[...], filter_spec[...]), inverse, turn, last)
    for r in range(out.shape[1]):
        out[:, r, :] = wide[:, r * INNER : (r + 1) * INNER]


def filter_grad_kernel(at, first, turn, forward, inverse, last, tokens, grad_spec, out):
    spec = forward_spectrum(rows_to_wide(tokens), first, turn, forward)
    wide = inverse_signal(correlate(grad_spec[...], spec), inverse, turn, last)
    for r in range(out.shape[0]):
        out[r] = wide[:, r * INNER : (r + 1) * INNER]


def table_specs(tables, names):
    whole = lambda t: pl.BlockSpec(t.shape, lambda i, *_: (0,) * t.ndim)
    return [whole(tables[n]) for n in names], [tables[n] for n in names]


def cost(flops, size):
    return pl.CostEstimate(flops=flops, bytes_accessed=size, transcendentals=0)


LIMIT = pltpu.CompilerParams(vmem_limit_bytes=48 * 2**20)


def filter_spectrum(filters, tables):
    count, r, a, m = filters.shape
    specs, operands = table_specs(tables, ("first", "turn", "forward"))
    return pl.pallas_call(
        filter_kernel,
        grid=(count,),
        out_shape=jax.ShapeDtypeStruct((count, r * HALF, 2 * m), jnp.float32),
        in_specs=specs + [pl.BlockSpec((None, r, a, m), lambda i: (i, 0, 0, 0))],
        out_specs=pl.BlockSpec((None, r * HALF, 2 * m), lambda i: (i, 0, 0)),
        cost_estimate=cost(10**9, 8 * filters.size),
        compiler_params=LIMIT,
    )(*operands, filters)


def input_grad_part(at_x, both, filter_spec, tables):
    a, _, count, r, m = both.shape
    names = ("first", "turn", "forward", "inverse", "last")
    specs, operands = table_specs(tables, names)
    spec_shape = (None, r * HALF, 2 * m)
    grid_spec = pltpu.PrefetchScalarGridSpec(
        num_scalar_prefetch=1,
        grid=(count,),
        in_specs=specs
        + [
            pl.BlockSpec((a, None, None, r, m), lambda i, at: (0, 0, i, 0, 0)),
            pl.BlockSpec(spec_shape, lambda i, at: ((at[0] - i) & (count - 1), 0, 0)),
        ],
        out_specs=[
            pl.BlockSpec(spec_shape, lambda i, at: (i, 0, 0)),
            pl.BlockSpec((a, None, r, m), lambda i, at: (0, i, 0, 0)),
        ],
    )
    return pl.pallas_call(
        input_grad_kernel,
        grid_spec=grid_spec,
        out_shape=[
            jax.ShapeDtypeStruct((count, r * HALF, 2 * m), jnp.float32),
            jax.ShapeDtypeStruct((a, count, r, m), jnp.float32),
        ],
        cost_estimate=cost(2 * 10**9, 8 * both.size),
        compiler_params=LIMIT,
    )(at_x, *operands, both, filter_spec)


def filter_grad_part(at_x, both, grad_spec, tables):
    a, _, count, r, m = both.shape
    names = ("first", "turn", "forward", "inverse", "last_scaled")
    specs, operands = table_specs(tables, names)
    grid_spec = pltpu.PrefetchScalarGridSpec(
        num_scalar_prefetch=1,
        grid=(count,),
        in_specs=specs
        + [
            pl.BlockSpec((a, None, None, r, m), lambda i, at: (0, 1, i, 0, 0)),
            pl.BlockSpec((None, r * HALF, 2 * m), lambda i, at: (i, 0, 0)),
        ],
        out_specs=pl.BlockSpec(
            (None, r, a, m), lambda i, at: ((i - at[0]) & (count - 1), 0, 0, 0)
        ),
    )
    return pl.pallas_call(
        filter_grad_kernel,
        grid_spec=grid_spec,
        out_shape=jax.ShapeDtypeStruct((count, r, a, m), jnp.float32),
        cost_estimate=cost(0, 0),
        compiler_params=LIMIT,
    )(at_x, *operands, both, grad_spec)


def pack_kernel(half, grad, tokens, blocks):
    _, _, y, z, rows, _ = tokens.shape
    own, far, j = half[0], 1 - half[0], rows // 2
    for i in range(y):
        for k in range(z):
            for n, array in enumerate((grad, tokens)):
                near, other = array[:, own, i, k], array[:, far, i, z - 1 - k]
                blocks[i, k, 0, n] = jnp.concatenate([near[:, :j], other[:, :j]], axis=1)
                blocks[i, k, 1, n] = jnp.concatenate([near[:, j:], other[:, j:]], axis=1)


def unpack_kernel(half, blocks, tokens):
    _, _, y, z, rows, _ = tokens.shape
    own, far, j = half[0], 1 - half[0], rows // 2
    for i in range(y):
        for k in range(z):
            low, high = blocks[i, k, 0], blocks[i, k, 1]
            tokens[:, own, i, k] = jnp.concatenate([low[:, :j], high[:, :j]], axis=1)
            tokens[:, far, i, z - 1 - k] = jnp.concatenate([low[:, j:], high[:, j:]], axis=1)


def moving(kernel, half, arrays, shape):
    whole = pl.BlockSpec(memory_space=pltpu.VMEM)
    return pl.pallas_call(
        kernel,
        out_shape=jax.ShapeDtypeStruct(shape, jnp.float32),
        in_specs=[pl.BlockSpec(memory_space=pltpu.SMEM)] + [whole] * len(arrays),
        out_specs=whole,
        cost_estimate=cost(0, 8 * math.prod(shape)),
    )(half, *arrays)


def shards(inputs, grad_out, filters):
    x, h, y, z, c = (lax.axis_size(a) for a in ("x", "zh", "y", "zl", "c"))
    _, channels, block = inputs.shape
    j = channels // (x * h * y * z * c)
    seq_length = filters.shape[1]
    rows = y * z * c
    tables = dft_tables(seq_length, 1.0 / math.sqrt(x * h * seq_length))
    half = lax.axis_index("zh").reshape(1).astype(jnp.int32)
    at_x = lax.axis_index("x").reshape(1).astype(jnp.int32)
    whole_shape = (x, h, y, z, c * j, INNER)

    def exchange(blocks):
        return lax.all_to_all(blocks, ("y", "zl", "c"), 0, 0, tiled=True)

    def facing(v):
        return lax.ppermute(v, ("zh", "zl"), [(i, h * z - 1 - i) for i in range(h * z)])

    def along_x(v, s):
        return lax.ppermute(v, "x", [(i, (i + s) % x) for i in range(x)])

    both = moving(
        pack_kernel,
        half,
        [grad_out.reshape(whole_shape), inputs.reshape(whole_shape)],
        (y, z, c, 2, x, h * j, INNER),
    )
    both, filters = lax.optimization_barrier((both, filters))
    both = exchange(both.reshape(rows, 2, x, h * j, INNER))

    filters = filters.reshape(j, rows, INNER)
    pair = jnp.concatenate([filters, facing(filters)])
    taps = jnp.stack([pair] + [along_x(pair, s) for s in range(1, x)])
    filter_spec = filter_spectrum(taps, tables)

    grad_spec, leaving = input_grad_part(at_x, both, filter_spec, tables)
    returned = exchange(leaving)

    parts = filter_grad_part(at_x, both, grad_spec, tables)
    part = parts[0] + sum(along_x(parts[s], s) for s in range(1, x))
    filter_grad = part[:j] + facing(part[j:])

    blocks = returned.reshape(y, z, c, x, h * j, INNER)
    input_grad = moving(unpack_kernel, half, [blocks], whole_shape)
    return (input_grad.reshape(1, channels, block), filter_grad.reshape(j, seq_length))


def solution(mesh):
    devices = mesh.devices.reshape(4, 2, 4, -1, 2)
    fine = Mesh(devices, ("x", "zh", "y", "zl", "c"))
    tokens = P(("x", "zh"), None, ("y", "zl", "c"))
    owners = P(("x", "zh", "y", "zl", "c"), None)
    return jax.shard_map(
        shards,
        mesh=fine,
        in_specs=(tokens, tokens, owners),
        out_specs=(tokens, owners),
        check_vma=False,
    )
```

time: 225 us -> 203 us (0.902)
  waiting for transfers between devices: 126 us -> 103 us
  Pallas kernels: 5.25 us -> 23.1 us
  matrix products: 11.5 us -> 0 us
  starting transfers between devices: 62.7 us -> 71.1 us
  other arithmetic: 6.98 us -> 0.18 us
  local copies, waits for them, and re-layouts: 8.25 us -> 2.3 us
    all_to_all x2, waiting for transfers between devices: 113 us -> 74.4 us  [exchange(): return lax.all_to_all(blocks, ('y', 'zl', 'c'), 0, 0, tiled=True)]
    pallas_call x0 -> x3, Pallas kernels: none -> 17.8 us  [the longest x1 8.28 us: input_grad_part(): pl.pallas_call(input_grad_kernel, grid_spec=grid_spec, out_shape=[jax.Sha...]
    ppermute x10 -> x8, waiting for transfers between devices: 13.1 us -> 28.3 us  [the longest x6 16.1 us: along_x(): return lax.ppermute(v, 'x', [(i, (i + s) % x) for i in range(x)])]
    dot_general x10 -> x0, matrix products: 11.5 us -> none  [the longest x3 4.19 us: forward_spectrum(): first = jnp.einsum(form, signal, first_table, precision=HIGH)]
    all_to_all x2, starting transfers between devices: 30.9 us -> 36.6 us  [exchange(): return lax.all_to_all(blocks, ('y', 'zl', 'c'), 0, 0, tiled=True)]
    ppermute x10 -> x8, starting transfers between devices: 31.8 us -> 34.5 us  [the longest x6 20.1 us: along_x(): return lax.ppermute(v, 'x', [(i, (i + s) % x) for i in range(x)])]
    add x3 -> x0, other arithmetic: 2.48 us -> none  [the longest x1 1.15 us: forward_spectrum(): real * cos_turn + imag * sin_turn]
  transfers between devices with their start and end apart: 12 -> 10, of which waited for: 5 -> 8; matrix products, arithmetic and copies ran while one was open for 3% -> 1% of each run, Pallas kernels for 1% -> 5%
where the time goes in v2:
time: 203 us; the launch traced here: 200 us
  waiting for transfers between devices  103 us (51%)
  starting transfers between devices  71.1 us (35%)
  Pallas kernels  23.1 us (11%)
  local copies, waits for them, and re-layouts  2.3 us (1%)
    all_to_all x2, waiting for transfers between devices, exchange(): return lax.all_to_all(blocks, ('y', 'zl', 'c'), 0, 0, tiled=True)  74.4 us
    all_to_all x2, starting transfers between devices, exchange(): return lax.all_to_all(blocks, ('y', 'zl', 'c'), 0, 0, tiled=True)  36.6 us
    ppermute x6, starting transfers between devices, along_x(): return lax.ppermute(v, 'x', [(i, (i + s) % x) for i in range(x)])  20.1 us
    ppermute x6, waiting for transfers between devices, along_x(): return lax.ppermute(v, 'x', [(i, (i + s) % x) for i in range(x)])  16.1 us
    ppermute x2, starting transfers between devices, facing(): lax.ppermute(v, ('zh', 'zl'), [(i, h * z - 1 - i) for i in range(h * z)])  14.3 us
    ppermute x2, waiting for transfers between devices, facing(): lax.ppermute(v, ('zh', 'zl'), [(i, h * z - 1 - i) for i in range(h * z)])  12.2 us
    pallas_call x1, Pallas kernels, input_grad_part(): pl.pallas_call(input_grad_kernel, grid_spec=grid_spec, out_shape=[jax.Sha...  8.28 us
    pallas_call x1, Pallas kernels, filter_grad_part(): pl.pallas_call(filter_grad_kernel, grid_spec=grid_spec, out_shape=jax.Sha...  7.22 us
  transfers between devices with their start and end apart: 10, of which 8 were waited for; matrix products, arithmetic and copies ran while one was open for 1% of the time, Pallas kernels for 5%

profile of v2, /device:TPU:6, one launch (start us, length us, event | category | flops | bytes accessed | tf_op | source)
XLA Modules:
  0.0 200.3 jit_solution(2454175204295875025)
XLA Ops:
  0.6 3.0 %shard_map.104 = f32[4,8,2,2,4,8,128]{6,5,4,3,2,1,0:T(8,128)} custom-call(s32[1]{0:T(128)} %bitcast.half, f32[4,2,4,8,8,128]{5,4,3,2,1,0:T(8,128)} %bitcast.33, f32[4,2,4,8,8,128]{5,4,3,2,1,0:T(8,128)} %bitcast.34), custom_call_target="tpu_custom_call" | custom-call | bytes 4194304 | tf_op jit(solution)/shard_map/pallas_call | solution.py:220
  3.7 16.3 %all-to-all-start = ((f32[64,2,4,8,128]{4,3,2,1,0:T(8,128)}), f32[64,2,4,8,128]{4,3,2,1,0:T(8,128)S(1)}, u32[]{:S(2)}, u32[]{:S(2)}) async-start(f32[64,2,4,8,128]{4,3,2,1,0:T(8,128)} %bitcast.32), calls=%async_computation | async-start | bytes 4194304 | tf_op jit(solution)/shard_map/all_to_all | solution.py:241
  20.0 8.5 %collective-permute-start = (f32[4,64,128]{2,1,0:T(8,128)S(1)}, f32[4,64,128]{2,1,0:T(8,128)S(1)}, u32[]{:S(2)}, u32[]{:S(2)}) collective-permute-start(f32[4,64,128]{2,1,0:T(8,128)S(1)} %bitcast.43), channel_id=1, source_target_pairs={{0,78},{2,76},{4,74},{6,72},{8,70},{10,68},{12,66},{14,64},{64,14}... | collective-permute-start | bytes 393224 | tf_op jit(solution)/shard_map/ppermute | solution.py:244
  28.5 3.8 %collective-permute-done = f32[4,64,128]{2,1,0:T(8,128)S(1)} collective-permute-done((f32[4,64,128]{2,1,0:T(8,128)S(1)}, f32[4,64,128]{2,1,0:T(8,128)S(1)}, u32[]{:S(2)}, u32[]{:S(2)}) %collective-permute-start) | collective-permute-done | bytes 131104 | tf_op jit(solution)/shard_map/ppermute | solution.py:244
  32.3 2.7 %collective-permute-start.3 = (f32[8,64,128]{2,1,0:T(8,128)S(1)}, f32[8,64,128]{2,1,0:T(8,128)S(1)}, u32[]{:S(2)}, u32[]{:S(2)}) collective-permute-start(f32[8,64,128]{2,1,0:T(8,128)S(1)} %constant_dynamic-update-slice_fusion), channel_id=1, source_target_pairs={{0,384},{128,0},{256,128},{384,256},{1,385},{129,1},{257,129},{385... | collective-permute-start | bytes 786440 | tf_op jit(solution)/shard_map/ppermute | solution.py:247
  35.1 3.0 %collective-permute-start.2 = (f32[8,64,128]{2,1,0:T(8,128)S(1)}, f32[8,64,128]{2,1,0:T(8,128)S(1)}, u32[]{:S(2)}, u32[]{:S(2)}) collective-permute-start(f32[8,64,128]{2,1,0:T(8,128)S(1)} %constant_dynamic-update-slice_fusion), channel_id=1, source_target_pairs={{0,256},{128,384},{256,0},{384,128},{1,257},{129,385},{257,1},{385... | collective-permute-start | bytes 786440 | tf_op jit(solution)/shard_map/ppermute | solution.py:247
  38.1 4.0 %collective-permute-start.1 = (f32[8,64,128]{2,1,0:T(8,128)S(1)}, f32[8,64,128]{2,1,0:T(8,128)S(1)}, u32[]{:S(2)}, u32[]{:S(2)}) collective-permute-start(f32[8,64,128]{2,1,0:T(8,128)S(1)} %constant_dynamic-update-slice_fusion), channel_id=1, source_target_pairs={{0,128},{128,256},{256,384},{384,0},{1,129},{129,257},{257,385},{3... | collective-permute-start | bytes 786440 | tf_op jit(solution)/shard_map/ppermute | solution.py:247
  42.1 6.8 %collective-permute-done.3 = f32[8,64,128]{2,1,0:T(8,128)S(1)} collective-permute-done((f32[8,64,128]{2,1,0:T(8,128)S(1)}, f32[8,64,128]{2,1,0:T(8,128)S(1)}, u32[]{:S(2)}, u32[]{:S(2)}) %collective-permute-start.3) | collective-permute-done | bytes 262176 | tf_op jit(solution)/shard_map/ppermute | solution.py:247
  48.9 2.5 %collective-permute-done.1 = f32[8,64,128]{2,1,0:T(8,128)S(1)} collective-permute-done((f32[8,64,128]{2,1,0:T(8,128)S(1)}, f32[8,64,128]{2,1,0:T(8,128)S(1)}, u32[]{:S(2)}, u32[]{:S(2)}) %collective-permute-start.1) | collective-permute-done | bytes 262176 | tf_op jit(solution)/shard_map/ppermute | solution.py:247
  51.6 2.3 %shard_map.105.filter_spec = f32[4,576,256]{2,1,0:T(8,128)S(1)} custom-call(bf16[144,192]{1,0:T(8,128)(2,1)S(1)} %copy-done.3, f32[2,72,128]{2,1,0:T(8,128)S(1)} %copy-done.2, bf16[2,256,256]{2,1,0:T(8,128)(2,1)S(1)} %copy-done.1, f32[4,8,64,128]{3,2,1,0:T(8,128)S(1)} %pad_maximum_fusion.filters), custom_call_target="tpu_custom_call" | custom-call | flops 1000000000 | bytes 2097152 | tf_op jit(solution)/shard_map/pallas_call | solution.py:131
  53.9 1.4 copy-done
  55.3 60.4 %all-to-all-done.grad.tokens = f32[64,2,4,8,128]{4,3,2,1,0:T(8,128)S(1)} async-done(((f32[64,2,4,8,128]{4,3,2,1,0:T(8,128)}), f32[64,2,4,8,128]{4,3,2,1,0:T(8,128)S(1)}, u32[]{:S(2)}, u32[]{:S(2)}) %all-to-all-start) | async-done | bytes 2097184 | tf_op jit(solution)/shard_map/all_to_all | solution.py:241
  115.7 8.3 %shard_map.106 = (f32[4,576,256]{2,1,0:T(8,128)}, f32[64,4,8,128]{3,2,1,0:T(8,128)}) custom-call(s32[1]{0:T(128)} %bitcast.1.at, bf16[144,192]{1,0:T(8,128)(2,1)S(1)} %copy-done.3, f32[2,72,128]{2,1,0:T(8,128)S(1)} %copy-done.2, bf16[2,256,256]{2,1,0:T(8,128)(2,1)S(1)} %copy-done.1, bf16[2,256,256]{2,1,0:T(8,128)(2,1)S(1)} %copy-done.4, ...), custom_call_target="tpu_custom_call" | custom-call | flops 2000000000 | bytes 4194304 | tf_op jit(solution)/shard_map/pallas_call | solution.py:160
  124.0 20.3 %all-to-all-start.1 = ((f32[64,4,8,128]{3,2,1,0:T(8,128)}), f32[64,4,8,128]{3,2,1,0:T(8,128)}, u32[]{:S(2)}, u32[]{:S(2)}) async-start(f32[64,4,8,128]{3,2,1,0:T(8,128)} %get-tuple-element.8), calls=%async_computation.1 | async-start | bytes 2097152 | tf_op jit(solution)/shard_map/all_to_all | solution.py:241
  144.3 7.2 %shard_map.108 = f32[4,8,64,128]{3,2,1,0:T(8,128)S(1)} custom-call(s32[1]{0:T(128)} %bitcast.1.at, bf16[144,192]{1,0:T(8,128)(2,1)S(1)} %copy-done.3, f32[2,72,128]{2,1,0:T(8,128)S(1)} %copy-done.2, bf16[2,256,256]{2,1,0:T(8,128)(2,1)S(1)} %copy-done.1, bf16[2,256,256]{2,1,0:T(8,128)(2,1)S(1)} %copy-done.4, bf16[2,64,144]{2,1,0:T(8,128)(2,1)S(1)} %copy-done.5, ...), custom_call_target="tpu_custom_call" | custom-call | tf_op jit(solution)/shard_map/pallas_call | solution.py:188
  151.6 3.3 %collective-permute-start.5 = (f32[8,64,128]{2,1,0:T(8,128)S(1)}, f32[8,64,128]{2,1,0:T(8,128)S(1)}, u32[]{:S(2)}, u32[]{:S(2)}) collective-permute-start(f32[8,64,128]{2,1,0:T(8,128)S(1)} %get-tuple-element.10), channel_id=1, source_target_pairs={{0,256},{128,384},{256,0},{384,128},{1,257},{129,385},{257,1},{385... | collective-permute-start | bytes 786440 | tf_op jit(solution)/shard_map/ppermute | solution.py:247
  154.9 4.0 %collective-permute-start.6 = (f32[8,64,128]{2,1,0:T(8,128)S(1)}, f32[8,64,128]{2,1,0:T(8,128)S(1)}, u32[]{:S(2)}, u32[]{:S(2)}) collective-permute-start(f32[8,64,128]{2,1,0:T(8,128)S(1)} %get-tuple-element.11), channel_id=1, source_target_pairs={{0,384},{128,0},{256,128},{384,256},{1,385},{129,1},{257,129},{385... | collective-permute-start | bytes 786440 | tf_op jit(solution)/shard_map/ppermute | solution.py:247
  159.0 3.0 %collective-permute-start.4 = (f32[8,64,128]{2,1,0:T(8,128)S(1)}, f32[8,64,128]{2,1,0:T(8,128)S(1)}, u32[]{:S(2)}, u32[]{:S(2)}) collective-permute-start(f32[8,64,128]{2,1,0:T(8,128)S(1)} %get-tuple-element.12), channel_id=1, source_target_pairs={{0,128},{128,256},{256,384},{384,0},{1,129},{129,257},{257,385},{3... | collective-permute-start | bytes 786440 | tf_op jit(solution)/shard_map/ppermute | solution.py:247
  162.0 2.2 %collective-permute-done.5 = f32[8,64,128]{2,1,0:T(8,128)S(1)} collective-permute-done((f32[8,64,128]{2,1,0:T(8,128)S(1)}, f32[8,64,128]{2,1,0:T(8,128)S(1)}, u32[]{:S(2)}, u32[]{:S(2)}) %collective-permute-start.5) | collective-permute-done | bytes 262176 | tf_op jit(solution)/shard_map/ppermute | solution.py:247
  164.2 4.6 %collective-permute-done.6 = f32[8,64,128]{2,1,0:T(8,128)S(1)} collective-permute-done((f32[8,64,128]{2,1,0:T(8,128)S(1)}, f32[8,64,128]{2,1,0:T(8,128)S(1)}, u32[]{:S(2)}, u32[]{:S(2)}) %collective-permute-start.6) | collective-permute-done | bytes 262176 | tf_op jit(solution)/shard_map/ppermute | solution.py:247
  168.9 5.9 %collective-permute-start.7 = (f32[4,64,128]{2,1,0:T(8,128)S(1)}, f32[4,64,128]{2,1,0:T(8,128)S(1)}, u32[]{:S(2)}, u32[]{:S(2)}) collective-permute-start(f32[4,64,128]{2,1,0:T(8,128)S(1)} %slice.29), channel_id=1, source_target_pairs={{0,78},{2,76},{4,74},{6,72},{8,70},{10,68},{12,66},{14,64},{64,14}... | collective-permute-start | bytes 393224 | tf_op jit(solution)/shard_map/ppermute | solution.py:244
  174.8 8.4 %collective-permute-done.7 = f32[4,64,128]{2,1,0:T(8,128)S(1)} collective-permute-done((f32[4,64,128]{2,1,0:T(8,128)S(1)}, f32[4,64,128]{2,1,0:T(8,128)S(1)}, u32[]{:S(2)}, u32[]{:S(2)}) %collective-permute-start.7) | collective-permute-done | bytes 131104 | tf_op jit(solution)/shard_map/ppermute | solution.py:244
  184.0 14.0 %all-to-all-done.1 = f32[64,4,8,128]{3,2,1,0:T(8,128)} async-done(((f32[64,4,8,128]{3,2,1,0:T(8,128)}), f32[64,4,8,128]{3,2,1,0:T(8,128)}, u32[]{:S(2)}, u32[]{:S(2)}) %all-to-all-start.1) | async-done | bytes 1048608 | tf_op jit(solution)/shard_map/all_to_all | solution.py:241
  198.0 2.3 %shard_map.107 = f32[4,2,4,8,8,128]{5,4,3,2,1,0:T(8,128)} custom-call(s32[1]{0:T(128)} %bitcast.half, f32[4,8,2,4,8,128]{5,4,3,2,1,0:T(8,128)} %bitcast.9.blocks), custom_call_target="tpu_custom_call" | custom-call | bytes 2097152 | tf_op jit(solution)/shard_map/pallas_call | solution.py:220
  (26 shorter events, 1.1 us)
Async XLA Ops:
  3.7 16.3 %copy-start.7 = (f32[4,8192]{1,0:T(4,128)S(1)}, f32[4,8192]{1,0:T(4,128)}, u32[]{:S(2)}) copy-start(f32[4,8192]{1,0:T(4,128)} %param.11) | copy-start | bytes 393220
  3.7 112.1 %all-to-all-start = ((f32[64,2,4,8,128]{4,3,2,1,0:T(8,128)}), f32[64,2,4,8,128]{4,3,2,1,0:T(8,128)S(1)}, u32[]{:S(2)}, u32[]{:S(2)}) async-start(f32[64,2,4,8,128]{4,3,2,1,0:T(8,128)} %bitcast.32), calls=%async_computation | async-start | bytes 4194304 | tf_op jit(solution)/shard_map/all_to_all | solution.py:241
  20.0 31.6 %copy-start.1 = (bf16[2,256,256]{2,1,0:T(8,128)(2,1)S(1)}, bf16[2,256,256]{2,1,0:T(8,128)(2,1)}, u32[]{:S(2)}) copy-start(bf16[2,256,256]{2,1,0:T(8,128)(2,1)} %constant.26.clone.forward) | copy-start | bytes 786436
  20.0 31.6 %copy-start.2 = (f32[2,72,128]{2,1,0:T(8,128)S(1)}, f32[2,72,128]{2,1,0:T(8,128)}, u32[]{:S(2)}) copy-start(f32[2,72,128]{2,1,0:T(8,128)} %constant.29.clone.turn) | copy-start | bytes 221188
  20.0 31.6 %copy-start.3 = (bf16[144,192]{1,0:T(8,128)(2,1)S(1)}, bf16[144,192]{1,0:T(8,128)(2,1)}, u32[]{:S(2)}) copy-start(bf16[144,192]{1,0:T(8,128)(2,1)} %constant.28.clone.first) | copy-start | bytes 165892
  20.0 12.3 %collective-permute-start = (f32[4,64,128]{2,1,0:T(8,128)S(1)}, f32[4,64,128]{2,1,0:T(8,128)S(1)}, u32[]{:S(2)}, u32[]{:S(2)}) collective-permute-start(f32[4,64,128]{2,1,0:T(8,128)S(1)} %bitcast.43), channel_id=1, source_target_pairs={{0,78},{2,76},{4,74},{6,72},{8,70},{10,68},{12,66},{14,64},{64,14}... | collective-permute-start | bytes 393224 | tf_op jit(solution)/shard_map/ppermute | solution.py:244
  32.3 16.6 %collective-permute-start.3 = (f32[8,64,128]{2,1,0:T(8,128)S(1)}, f32[8,64,128]{2,1,0:T(8,128)S(1)}, u32[]{:S(2)}, u32[]{:S(2)}) collective-permute-start(f32[8,64,128]{2,1,0:T(8,128)S(1)} %constant_dynamic-update-slice_fusion), channel_id=1, source_target_pairs={{0,384},{128,0},{256,128},{384,256},{1,385},{129,1},{257,129},{385... | collective-permute-start | bytes 786440 | tf_op jit(solution)/shard_map/ppermute | solution.py:247
  35.1 13.8 %collective-permute-start.2 = (f32[8,64,128]{2,1,0:T(8,128)S(1)}, f32[8,64,128]{2,1,0:T(8,128)S(1)}, u32[]{:S(2)}, u32[]{:S(2)}) collective-permute-start(f32[8,64,128]{2,1,0:T(8,128)S(1)} %constant_dynamic-update-slice_fusion), channel_id=1, source_target_pairs={{0,256},{128,384},{256,0},{384,128},{1,257},{129,385},{257,1},{385... | collective-permute-start | bytes 786440 | tf_op jit(solution)/shard_map/ppermute | solution.py:247
  38.1 13.3 %collective-permute-start.1 = (f32[8,64,128]{2,1,0:T(8,128)S(1)}, f32[8,64,128]{2,1,0:T(8,128)S(1)}, u32[]{:S(2)}, u32[]{:S(2)}) collective-permute-start(f32[8,64,128]{2,1,0:T(8,128)S(1)} %constant_dynamic-update-slice_fusion), channel_id=1, source_target_pairs={{0,128},{128,256},{256,384},{384,0},{1,129},{129,257},{257,385},{3... | collective-permute-start | bytes 786440 | tf_op jit(solution)/shard_map/ppermute | solution.py:247
  51.5 64.2 %copy-start.4 = (bf16[2,256,256]{2,1,0:T(8,128)(2,1)S(1)}, bf16[2,256,256]{2,1,0:T(8,128)(2,1)}, u32[]{:S(2)}) copy-start(bf16[2,256,256]{2,1,0:T(8,128)(2,1)} %constant.27.clone.inverse) | copy-start | bytes 786436
  51.6 64.2 %copy-start.6 = (bf16[2,64,144]{2,1,0:T(8,128)(2,1)S(1)}, bf16[2,64,144]{2,1,0:T(8,128)(2,1)}, u32[]{:S(2)}) copy-start(bf16[2,64,144]{2,1,0:T(8,128)(2,1)} %constant.24.clone.last) | copy-start | bytes 110596
  53.9 1.4 copy-start
  115.7 28.6 %copy-start.5 = (bf16[2,64,144]{2,1,0:T(8,128)(2,1)S(1)}, bf16[2,64,144]{2,1,0:T(8,128)(2,1)}, u32[]{:S(2)}) copy-start(bf16[2,64,144]{2,1,0:T(8,128)(2,1)} %constant.25.clone.last) | copy-start | bytes 110596
  124.0 74.0 %all-to-all-start.1 = ((f32[64,4,8,128]{3,2,1,0:T(8,128)}), f32[64,4,8,128]{3,2,1,0:T(8,128)}, u32[]{:S(2)}, u32[]{:S(2)}) async-start(f32[64,4,8,128]{3,2,1,0:T(8,128)} %get-tuple-element.8), calls=%async_computation.1 | async-start | bytes 2097152 | tf_op jit(solution)/shard_map/all_to_all | solution.py:241
  151.6 12.6 %collective-permute-start.5 = (f32[8,64,128]{2,1,0:T(8,128)S(1)}, f32[8,64,128]{2,1,0:T(8,128)S(1)}, u32[]{:S(2)}, u32[]{:S(2)}) collective-permute-start(f32[8,64,128]{2,1,0:T(8,128)S(1)} %get-tuple-element.10), channel_id=1, source_target_pairs={{0,256},{128,384},{256,0},{384,128},{1,257},{129,385},{257,1},{385... | collective-permute-start | bytes 786440 | tf_op jit(solution)/shard_map/ppermute | solution.py:247
  154.9 13.9 %collective-permute-start.6 = (f32[8,64,128]{2,1,0:T(8,128)S(1)}, f32[8,64,128]{2,1,0:T(8,128)S(1)}, u32[]{:S(2)}, u32[]{:S(2)}) collective-permute-start(f32[8,64,128]{2,1,0:T(8,128)S(1)} %get-tuple-element.11), channel_id=1, source_target_pairs={{0,384},{128,0},{256,128},{384,256},{1,385},{129,1},{257,129},{385... | collective-permute-start | bytes 786440 | tf_op jit(solution)/shard_map/ppermute | solution.py:247
  159.0 9.8 %collective-permute-start.4 = (f32[8,64,128]{2,1,0:T(8,128)S(1)}, f32[8,64,128]{2,1,0:T(8,128)S(1)}, u32[]{:S(2)}, u32[]{:S(2)}) collective-permute-start(f32[8,64,128]{2,1,0:T(8,128)S(1)} %get-tuple-element.12), channel_id=1, source_target_pairs={{0,128},{128,256},{256,384},{384,0},{1,129},{129,257},{257,385},{3... | collective-permute-start | bytes 786440 | tf_op jit(solution)/shard_map/ppermute | solution.py:247
  168.9 14.3 %collective-permute-start.7 = (f32[4,64,128]{2,1,0:T(8,128)S(1)}, f32[4,64,128]{2,1,0:T(8,128)S(1)}, u32[]{:S(2)}, u32[]{:S(2)}) collective-permute-start(f32[4,64,128]{2,1,0:T(8,128)S(1)} %slice.29), channel_id=1, source_target_pairs={{0,78},{2,76},{4,74},{6,72},{8,70},{10,68},{12,66},{14,64},{64,14}... | collective-permute-start | bytes 393224 | tf_op jit(solution)/shard_map/ppermute | solution.py:244

commit v3 on v2

--- a/solution.py
+++ b/solution.py
@@ -139,8 +139,8 @@
     )(*operands, filters)
 
 
-def input_grad_part(at_x, both, filter_spec, tables):
-    a, _, count, r, m = both.shape
+def input_grad_part(at_x, grad, filter_spec, tables):
+    a, count, r, m = grad.shape
     names = ("first", "turn", "forward", "inverse", "last")
     specs, operands = table_specs(tables, names)
     spec_shape = (None, r * HALF, 2 * m)
@@ -149,7 +149,7 @@
         grid=(count,),
         in_specs=specs
         + [
-            pl.BlockSpec((a, None, None, r, m), lambda i, at: (0, 0, i, 0, 0)),
+            pl.BlockSpec((a, None, r, m), lambda i, at: (0, i, 0, 0)),
             pl.BlockSpec(spec_shape, lambda i, at: ((at[0] - i) & (count - 1), 0, 0)),
         ],
         out_specs=[
@@ -164,13 +164,13 @@
             jax.ShapeDtypeStruct((count, r * HALF, 2 * m), jnp.float32),
             jax.ShapeDtypeStruct((a, count, r, m), jnp.float32),
         ],
-        cost_estimate=cost(2 * 10**9, 8 * both.size),
+        cost_estimate=cost(2 * 10**9, 8 * grad.size),
         compiler_params=LIMIT,
-    )(at_x, *operands, both, filter_spec)
-
-
-def filter_grad_part(at_x, both, grad_spec, tables):
-    a, _, count, r, m = both.shape
+    )(at_x, *operands, grad, filter_spec)
+
+
+def filter_grad_part(at_x, tokens, grad_spec, tables):
+    a, count, r, m = tokens.shape
     names = ("first", "turn", "forward", "inverse", "last_scaled")
     specs, operands = table_specs(tables, names)
     grid_spec = pltpu.PrefetchScalarGridSpec(
@@ -178,7 +178,7 @@
         grid=(count,),
         in_specs=specs
         + [
-            pl.BlockSpec((a, None, None, r, m), lambda i, at: (0, 1, i, 0, 0)),
+            pl.BlockSpec((a, None, r, m), lambda i, at: (0, i, 0, 0)),
             pl.BlockSpec((None, r * HALF, 2 * m), lambda i, at: (i, 0, 0)),
         ],
         out_specs=pl.BlockSpec(
@@ -191,18 +191,17 @@
         out_shape=jax.ShapeDtypeStruct((count, r, a, m), jnp.float32),
         cost_estimate=cost(0, 0),
         compiler_params=LIMIT,
-    )(at_x, *operands, both, grad_spec)
-
-
-def pack_kernel(half, grad, tokens, blocks):
+    )(at_x, *operands, tokens, grad_spec)
+
+
+def pack_kernel(half, tokens, blocks):
     _, _, y, z, rows, _ = tokens.shape
     own, far, j = half[0], 1 - half[0], rows // 2
     for i in range(y):
         for k in range(z):
-            for n, array in enumerate((grad, tokens)):
-                near, other = array[:, own, i, k], array[:, far, i, z - 1 - k]
-                blocks[i, k, 0, n] = jnp.concatenate([near[:, :j], other[:, :j]], axis=1)
-                blocks[i, k, 1, n] = jnp.concatenate([near[:, j:], other[:, j:]], axis=1)
+            near, other = tokens[:, own, i, k], tokens[:, far, i, z - 1 - k]
+            blocks[i, k, 0] = jnp.concatenate([near[:, :j], other[:, :j]], axis=1)
+            blocks[i, k, 1] = jnp.concatenate([near[:, j:], other[:, j:]], axis=1)
 
 
 def unpack_kernel(half, blocks, tokens):
@@ -215,15 +214,15 @@
             tokens[:, far, i, z - 1 - k] = jnp.concatenate([low[:, j:], high[:, j:]], axis=1)
 
 
-def moving(kernel, half, arrays, shape):
+def moving(kernel, half, array, shape):
     whole = pl.BlockSpec(memory_space=pltpu.VMEM)
     return pl.pallas_call(
         kernel,
         out_shape=jax.ShapeDtypeStruct(shape, jnp.float32),
-        in_specs=[pl.BlockSpec(memory_space=pltpu.SMEM)] + [whole] * len(arrays),
+        in_specs=[pl.BlockSpec(memory_space=pltpu.SMEM), whole],
         out_specs=whole,
         cost_estimate=cost(0, 8 * math.prod(shape)),
-    )(half, *arrays)
+    )(half, array)
 
 
 def shards(inputs, grad_out, filters):
@@ -246,29 +245,27 @@
     def along_x(v, s):
         return lax.ppermute(v, "x", [(i, (i + s) % x) for i in range(x)])
 
-    both = moving(
-        pack_kernel,
-        half,
-        [grad_out.reshape(whole_shape), inputs.reshape(whole_shape)],
-        (y, z, c, 2, x, h * j, INNER),
-    )
-    both, filters = lax.optimization_barrier((both, filters))
-    both = exchange(both.reshape(rows, 2, x, h * j, INNER))
+    def to_owners(array):
+        blocks = moving(pack_kernel, half, array.reshape(whole_shape), (y, z, c, x, h * j, INNER))
+        return exchange(blocks.reshape(rows, x, h * j, INNER))
+
+    grad = to_owners(grad_out)
+    tokens = to_owners(inputs)
 
     filters = filters.reshape(j, rows, INNER)
     pair = jnp.concatenate([filters, facing(filters)])
     taps = jnp.stack([pair] + [along_x(pair, s) for s in range(1, x)])
     filter_spec = filter_spectrum(taps, tables)
 
-    grad_spec, leaving = input_grad_part(at_x, both, filter_spec, tables)
+    grad_spec, leaving = input_grad_part(at_x, grad, filter_spec, tables)
     returned = exchange(leaving)
 
-    parts = filter_grad_part(at_x, both, grad_spec, tables)
+    parts = filter_grad_part(at_x, tokens, grad_spec, tables)
     part = parts[0] + sum(along_x(parts[s], s) for s in range(1, x))
     filter_grad = part[:j] + facing(part[j:])
 
     blocks = returned.reshape(y, z, c, x, h * j, INNER)
-    input_grad = moving(unpack_kernel, half, [blocks], whole_shape)
+    input_grad = moving(unpack_kernel, half, blocks, whole_shape)
     return (input_grad.reshape(1, channels, block), filter_grad.reshape(j, seq_length))
 
 

time: 203 us -> 228 us (1.12)
  starting transfers between devices: 71.1 us -> 95.3 us
  local copies, waits for them, and re-layouts: 2.3 us -> 6.97 us
  waiting for transfers between devices: 103 us -> 100 us
    all_to_all x2 -> x3, starting transfers between devices: 36.6 us -> 62.2 us  [exchange(): return lax.all_to_all(blocks, ('y', 'zl', 'c'), 0, 0, tiled=True)]
    all_to_all x2 -> x3, waiting for transfers between devices: 74.4 us -> 66.6 us  [exchange(): return lax.all_to_all(blocks, ('y', 'zl', 'c'), 0, 0, tiled=True)]
    unnamed x19 -> x31, local copies, waits for them, and re-layouts: 2.23 us -> 6.9 us
    ppermute x6, waiting for transfers between devices: 16.1 us -> 18.9 us  [along_x(): return lax.ppermute(v, 'x', [(i, (i + s) % x) for i in range(x)])]
    ppermute x2, waiting for transfers between devices: 12.2 us -> 14.7 us  [facing(): lax.ppermute(v, ('zh', 'zl'), [(i, h * z - 1 - i) for i in range(h * z)])]
    pallas_call x2 -> x3, Pallas kernels: 5.29 us -> 6.84 us  [moving(): pl.pallas_call(kernel, out_shape=jax.ShapeDtypeStruct(shape, jnp.float32)...]
  transfers between devices with their start and end apart: 10 -> 11, of which waited for: 8 -> 11; matrix products, arithmetic and copies ran while one was open for 1% -> 0% of each run, Pallas kernels for 5% -> 8%
where the time goes in v3:
time: 228 us; the launch traced here: 227 us
  waiting for transfers between devices  100 us (44%)
  starting transfers between devices  95.3 us (42%)
  Pallas kernels  23 us (10%)
  local copies, waits for them, and re-layouts  6.97 us (3%)
    all_to_all x3, waiting for transfers between devices, exchange(): return lax.all_to_all(blocks, ('y', 'zl', 'c'), 0, 0, tiled=True)  66.6 us
    all_to_all x3, starting transfers between devices, exchange(): return lax.all_to_all(blocks, ('y', 'zl', 'c'), 0, 0, tiled=True)  62.2 us
    ppermute x6, waiting for transfers between devices, along_x(): return lax.ppermute(v, 'x', [(i, (i + s) % x) for i in range(x)])  18.9 us
    ppermute x6, starting transfers between devices, along_x(): return lax.ppermute(v, 'x', [(i, (i + s) % x) for i in range(x)])  18.2 us
    ppermute x2, starting transfers between devices, facing(): lax.ppermute(v, ('zh', 'zl'), [(i, h * z - 1 - i) for i in range(h * z)])  14.9 us
    ppermute x2, waiting for transfers between devices, facing(): lax.ppermute(v, ('zh', 'zl'), [(i, h * z - 1 - i) for i in range(h * z)])  14.7 us
    pallas_call x1, Pallas kernels, input_grad_part(): pl.pallas_call(input_grad_kernel, grid_spec=grid_spec, out_shape=[jax.Sha...  7.67 us
    unnamed x31, local copies, waits for them, and re-layouts  6.9 us
  transfers between devices with their start and end apart: 11, of which 11 were waited for; matrix products, arithmetic and copies ran while one was open for 0% of the time, Pallas kernels for 8%

profile of v3, /device:TPU:6, one launch (start us, length us, event | category | flops | bytes accessed | tf_op | source)
XLA Modules:
  0.0 226.6 jit_solution(6524831461552857964)
XLA Ops:
  2.9 16.2 %all-to-all-start = ((f32[64,4,8,128]{3,2,1,0:T(8,128)}), f32[64,4,8,128]{3,2,1,0:T(8,128)S(1)}, u32[]{:S(2)}, u32[]{:S(2)}) async-start(f32[64,4,8,128]{3,2,1,0:T(8,128)} %bitcast.34), calls=%async_computation | async-start | bytes 2097152 | tf_op jit(solution)/shard_map/all_to_all | solution.py:240
  19.1 2.3 %shard_map.108 = f32[4,8,2,4,8,128]{5,4,3,2,1,0:T(8,128)} custom-call(s32[1]{0:T(128)} %bitcast.half, f32[4,2,4,8,8,128]{5,4,3,2,1,0:T(8,128)} %bitcast.36), custom_call_target="tpu_custom_call" | custom-call | bytes 2097152 | tf_op jit(solution)/shard_map/pallas_call | solution.py:219
  21.4 49.1 %all-to-all-done.grad = f32[64,4,8,128]{3,2,1,0:T(8,128)S(1)} async-done(((f32[64,4,8,128]{3,2,1,0:T(8,128)}), f32[64,4,8,128]{3,2,1,0:T(8,128)S(1)}, u32[]{:S(2)}, u32[]{:S(2)}) %all-to-all-start) | async-done | bytes 1048608 | tf_op jit(solution)/shard_map/all_to_all | solution.py:240
  71.4 8.2 %all-to-all-start.2 = ((f32[64,4,8,128]{3,2,1,0:T(8,128)}), f32[64,4,8,128]{3,2,1,0:T(8,128)S(1)}, u32[]{:S(2)}, u32[]{:S(2)}) async-start(f32[64,4,8,128]{3,2,1,0:T(8,128)} %bitcast.33), calls=%async_computation.2 | async-start | bytes 2097152 | tf_op jit(solution)/shard_map/all_to_all | solution.py:240
  79.7 8.3 %collective-permute-start = (f32[4,64,128]{2,1,0:T(8,128)S(1)}, f32[4,64,128]{2,1,0:T(8,128)S(1)}, u32[]{:S(2)}, u32[]{:S(2)}) collective-permute-start(f32[4,64,128]{2,1,0:T(8,128)S(1)} %bitcast.45), channel_id=1, source_target_pairs={{0,78},{2,76},{4,74},{6,72},{8,70},{10,68},{12,66},{14,64},{64,14}... | collective-permute-start | bytes 393224 | tf_op jit(solution)/shard_map/ppermute | solution.py:243
  88.0 5.0 %collective-permute-done = f32[4,64,128]{2,1,0:T(8,128)S(1)} collective-permute-done((f32[4,64,128]{2,1,0:T(8,128)S(1)}, f32[4,64,128]{2,1,0:T(8,128)S(1)}, u32[]{:S(2)}, u32[]{:S(2)}) %collective-permute-start) | collective-permute-done | bytes 131104 | tf_op jit(solution)/shard_map/ppermute | solution.py:243
  93.1 2.4 %collective-permute-start.1 = (f32[8,64,128]{2,1,0:T(8,128)S(1)}, f32[8,64,128]{2,1,0:T(8,128)S(1)}, u32[]{:S(2)}, u32[]{:S(2)}) collective-permute-start(f32[8,64,128]{2,1,0:T(8,128)S(1)} %constant_dynamic-update-slice_fusion), channel_id=1, source_target_pairs={{0,128},{128,256},{256,384},{384,0},{1,129},{129,257},{257,385},{3... | collective-permute-start | bytes 786440 | tf_op jit(solution)/shard_map/ppermute | solution.py:246
  95.5 4.3 %collective-permute-start.2 = (f32[8,64,128]{2,1,0:T(8,128)S(1)}, f32[8,64,128]{2,1,0:T(8,128)S(1)}, u32[]{:S(2)}, u32[]{:S(2)}) collective-permute-start(f32[8,64,128]{2,1,0:T(8,128)S(1)} %constant_dynamic-update-slice_fusion), channel_id=1, source_target_pairs={{0,256},{128,384},{256,0},{384,128},{1,257},{129,385},{257,1},{385... | collective-permute-start | bytes 786440 | tf_op jit(solution)/shard_map/ppermute | solution.py:246
  101.8 2.5 %collective-permute-done.1 = f32[8,64,128]{2,1,0:T(8,128)S(1)} collective-permute-done((f32[8,64,128]{2,1,0:T(8,128)S(1)}, f32[8,64,128]{2,1,0:T(8,128)S(1)}, u32[]{:S(2)}, u32[]{:S(2)}) %collective-permute-start.1) | collective-permute-done | bytes 262176 | tf_op jit(solution)/shard_map/ppermute | solution.py:246
  104.2 2.9 %collective-permute-done.2 = f32[8,64,128]{2,1,0:T(8,128)S(1)} collective-permute-done((f32[8,64,128]{2,1,0:T(8,128)S(1)}, f32[8,64,128]{2,1,0:T(8,128)S(1)}, u32[]{:S(2)}, u32[]{:S(2)}) %collective-permute-start.2) | collective-permute-done | bytes 262176 | tf_op jit(solution)/shard_map/ppermute | solution.py:246
  107.2 3.7 %collective-permute-done.3 = f32[8,64,128]{2,1,0:T(8,128)S(1)} collective-permute-done((f32[8,64,128]{2,1,0:T(8,128)S(1)}, f32[8,64,128]{2,1,0:T(8,128)S(1)}, u32[]{:S(2)}, u32[]{:S(2)}) %collective-permute-start.3) | collective-permute-done | bytes 262176 | tf_op jit(solution)/shard_map/ppermute | solution.py:246
  111.1 2.3 %shard_map.105.filter_spec = f32[4,576,256]{2,1,0:T(8,128)S(1)} custom-call(bf16[144,192]{1,0:T(8,128)(2,1)S(1)} %copy-done.7, f32[2,72,128]{2,1,0:T(8,128)S(1)} %copy-done.8, bf16[2,256,256]{2,1,0:T(8,128)(2,1)S(1)} %copy-done.4, f32[4,8,64,128]{3,2,1,0:T(8,128)S(1)} %pad_maximum_fusion.filters), custom_call_target="tpu_custom_call" | custom-call | flops 1000000000 | bytes 2097152 | tf_op jit(solution)/shard_map/pallas_call | solution.py:131
  114.8 7.7 %shard_map.106 = (f32[4,576,256]{2,1,0:T(8,128)S(1)}, f32[64,4,8,128]{3,2,1,0:T(8,128)S(1)}) custom-call(s32[1]{0:T(128)} %bitcast.1.at, bf16[144,192]{1,0:T(8,128)(2,1)S(1)} %copy-done.7, f32[2,72,128]{2,1,0:T(8,128)S(1)} %copy-done.8, bf16[2,256,256]{2,1,0:T(8,128)(2,1)S(1)} %copy-done.5, bf16[2,256,256]{2,1,0:T(8,128)(2,1)S(1)} %copy-done.9, ...), custom_call_target="tpu_custom_call" | custom-call | flops 2000000000 | bytes 2097152 | tf_op jit(solution)/shard_map/pallas_call | solution.py:160
  123.5 10.3 %all-to-all-done.2.tokens = f32[64,4,8,128]{3,2,1,0:T(8,128)S(1)} async-done(((f32[64,4,8,128]{3,2,1,0:T(8,128)}), f32[64,4,8,128]{3,2,1,0:T(8,128)S(1)}, u32[]{:S(2)}, u32[]{:S(2)}) %all-to-all-start.2) | async-done | bytes 1048608 | tf_op jit(solution)/shard_map/all_to_all | solution.py:240
  133.8 37.9 %all-to-all-start.1 = ((f32[64,4,8,128]{3,2,1,0:T(8,128)}), f32[64,4,8,128]{3,2,1,0:T(8,128)}, u32[]{:S(2)}, u32[]{:S(2)}) async-start(f32[64,4,8,128]{3,2,1,0:T(8,128)} %copy-done.1), calls=%async_computation.1 | async-start | bytes 2097152 | tf_op jit(solution)/shard_map/all_to_all | solution.py:240
  174.5 6.2 %shard_map.109 = f32[4,8,64,128]{3,2,1,0:T(8,128)S(1)} custom-call(s32[1]{0:T(128)} %bitcast.1.at, bf16[144,192]{1,0:T(8,128)(2,1)S(1)} %copy-done.7, f32[2,72,128]{2,1,0:T(8,128)S(1)} %copy-done.8, bf16[2,256,256]{2,1,0:T(8,128)(2,1)S(1)} %copy-done.6, bf16[2,256,256]{2,1,0:T(8,128)(2,1)S(1)} %copy-done.10, bf16[2,64,144]{2,1,0:T(8,128)(2,1)S(1)} %copy-done.11, ...), custom_call_target="tpu_custom_call" | custom-call | tf_op jit(solution)/shard_map/pallas_call | solution.py:188
  180.7 2.5 %collective-permute-start.4 = (f32[8,64,128]{2,1,0:T(8,128)S(1)}, f32[8,64,128]{2,1,0:T(8,128)S(1)}, u32[]{:S(2)}, u32[]{:S(2)}) collective-permute-start(f32[8,64,128]{2,1,0:T(8,128)S(1)} %get-tuple-element.8), channel_id=1, source_target_pairs={{0,128},{128,256},{256,384},{384,0},{1,129},{129,257},{257,385},{3... | collective-permute-start | bytes 786440 | tf_op jit(solution)/shard_map/ppermute | solution.py:246
  183.2 4.4 %collective-permute-start.5 = (f32[8,64,128]{2,1,0:T(8,128)S(1)}, f32[8,64,128]{2,1,0:T(8,128)S(1)}, u32[]{:S(2)}, u32[]{:S(2)}) collective-permute-start(f32[8,64,128]{2,1,0:T(8,128)S(1)} %get-tuple-element.6), channel_id=1, source_target_pairs={{0,256},{128,384},{256,0},{384,128},{1,257},{129,385},{257,1},{385... | collective-permute-start | bytes 786440 | tf_op jit(solution)/shard_map/ppermute | solution.py:246
  187.6 2.7 %collective-permute-start.6 = (f32[8,64,128]{2,1,0:T(8,128)S(1)}, f32[8,64,128]{2,1,0:T(8,128)S(1)}, u32[]{:S(2)}, u32[]{:S(2)}) collective-permute-start(f32[8,64,128]{2,1,0:T(8,128)S(1)} %get-tuple-element.7), channel_id=1, source_target_pairs={{0,384},{128,0},{256,128},{384,256},{1,385},{129,1},{257,129},{385... | collective-permute-start | bytes 786440 | tf_op jit(solution)/shard_map/ppermute | solution.py:246
  191.8 4.0 %collective-permute-done.5 = f32[8,64,128]{2,1,0:T(8,128)S(1)} collective-permute-done((f32[8,64,128]{2,1,0:T(8,128)S(1)}, f32[8,64,128]{2,1,0:T(8,128)S(1)}, u32[]{:S(2)}, u32[]{:S(2)}) %collective-permute-start.5) | collective-permute-done | bytes 262176 | tf_op jit(solution)/shard_map/ppermute | solution.py:246
  195.8 4.3 %collective-permute-done.6 = f32[8,64,128]{2,1,0:T(8,128)S(1)} collective-permute-done((f32[8,64,128]{2,1,0:T(8,128)S(1)}, f32[8,64,128]{2,1,0:T(8,128)S(1)}, u32[]{:S(2)}, u32[]{:S(2)}) %collective-permute-start.6) | collective-permute-done | bytes 262176 | tf_op jit(solution)/shard_map/ppermute | solution.py:246
  200.2 6.5 %collective-permute-start.7 = (f32[4,64,128]{2,1,0:T(8,128)S(1)}, f32[4,64,128]{2,1,0:T(8,128)S(1)}, u32[]{:S(2)}, u32[]{:S(2)}) collective-permute-start(f32[4,64,128]{2,1,0:T(8,128)S(1)} %slice.29), channel_id=1, source_target_pairs={{0,78},{2,76},{4,74},{6,72},{8,70},{10,68},{12,66},{14,64},{64,14}... | collective-permute-start | bytes 393224 | tf_op jit(solution)/shard_map/ppermute | solution.py:243
  206.8 9.6 %collective-permute-done.7 = f32[4,64,128]{2,1,0:T(8,128)S(1)} collective-permute-done((f32[4,64,128]{2,1,0:T(8,128)S(1)}, f32[4,64,128]{2,1,0:T(8,128)S(1)}, u32[]{:S(2)}, u32[]{:S(2)}) %collective-permute-start.7) | collective-permute-done | bytes 131104 | tf_op jit(solution)/shard_map/ppermute | solution.py:243
  217.1 7.2 %all-to-all-done.1 = f32[64,4,8,128]{3,2,1,0:T(8,128)} async-done(((f32[64,4,8,128]{3,2,1,0:T(8,128)}), f32[64,4,8,128]{3,2,1,0:T(8,128)}, u32[]{:S(2)}, u32[]{:S(2)}) %all-to-all-start.1) | async-done | bytes 1048608 | tf_op jit(solution)/shard_map/all_to_all | solution.py:240
  (41 shorter events, 15.1 us)
Async XLA Ops:
  2.9 67.6 %all-to-all-start = ((f32[64,4,8,128]{3,2,1,0:T(8,128)}), f32[64,4,8,128]{3,2,1,0:T(8,128)S(1)}, u32[]{:S(2)}, u32[]{:S(2)}) async-start(f32[64,4,8,128]{3,2,1,0:T(8,128)} %bitcast.34), calls=%async_computation | async-start | bytes 2097152 | tf_op jit(solution)/shard_map/all_to_all | solution.py:240
  19.1 60.6 %copy-start.13 = (f32[4,8192]{1,0:T(4,128)S(1)}, f32[4,8192]{1,0:T(4,128)}, u32[]{:S(2)}) copy-start(f32[4,8192]{1,0:T(4,128)} %param.11) | copy-start | bytes 393220
  70.5 1.0 copy-start.2
  71.4 39.5 %copy-start.4 = (bf16[2,256,256]{2,1,0:T(8,128)(2,1)S(1)}, bf16[2,256,256]{2,1,0:T(8,128)(2,1)}, u32[]{:S(2)}) copy-start(bf16[2,256,256]{2,1,0:T(8,128)(2,1)} %constant.26.clone.forward) | copy-start | bytes 786436
  71.4 39.6 %copy-start.7 = (bf16[144,192]{1,0:T(8,128)(2,1)S(1)}, bf16[144,192]{1,0:T(8,128)(2,1)}, u32[]{:S(2)}) copy-start(bf16[144,192]{1,0:T(8,128)(2,1)} %constant.28.clone.first) | copy-start | bytes 165892
  71.4 39.6 %copy-start.8 = (f32[2,72,128]{2,1,0:T(8,128)S(1)}, f32[2,72,128]{2,1,0:T(8,128)}, u32[]{:S(2)}) copy-start(f32[2,72,128]{2,1,0:T(8,128)} %constant.29.clone.turn) | copy-start | bytes 221188
  71.4 62.4 %all-to-all-start.2 = ((f32[64,4,8,128]{3,2,1,0:T(8,128)}), f32[64,4,8,128]{3,2,1,0:T(8,128)S(1)}, u32[]{:S(2)}, u32[]{:S(2)}) async-start(f32[64,4,8,128]{3,2,1,0:T(8,128)} %bitcast.33), calls=%async_computation.2 | async-start | bytes 2097152 | tf_op jit(solution)/shard_map/all_to_all | solution.py:240
  79.7 13.4 %collective-permute-start = (f32[4,64,128]{2,1,0:T(8,128)S(1)}, f32[4,64,128]{2,1,0:T(8,128)S(1)}, u32[]{:S(2)}, u32[]{:S(2)}) collective-permute-start(f32[4,64,128]{2,1,0:T(8,128)S(1)} %bitcast.45), channel_id=1, source_target_pairs={{0,78},{2,76},{4,74},{6,72},{8,70},{10,68},{12,66},{14,64},{64,14}... | collective-permute-start | bytes 393224 | tf_op jit(solution)/shard_map/ppermute | solution.py:243
  93.1 11.1 %collective-permute-start.1 = (f32[8,64,128]{2,1,0:T(8,128)S(1)}, f32[8,64,128]{2,1,0:T(8,128)S(1)}, u32[]{:S(2)}, u32[]{:S(2)}) collective-permute-start(f32[8,64,128]{2,1,0:T(8,128)S(1)} %constant_dynamic-update-slice_fusion), channel_id=1, source_target_pairs={{0,128},{128,256},{256,384},{384,0},{1,129},{129,257},{257,385},{3... | collective-permute-start | bytes 786440 | tf_op jit(solution)/shard_map/ppermute | solution.py:246
  95.5 11.7 %collective-permute-start.2 = (f32[8,64,128]{2,1,0:T(8,128)S(1)}, f32[8,64,128]{2,1,0:T(8,128)S(1)}, u32[]{:S(2)}, u32[]{:S(2)}) collective-permute-start(f32[8,64,128]{2,1,0:T(8,128)S(1)} %constant_dynamic-update-slice_fusion), channel_id=1, source_target_pairs={{0,256},{128,384},{256,0},{384,128},{1,257},{129,385},{257,1},{385... | collective-permute-start | bytes 786440 | tf_op jit(solution)/shard_map/ppermute | solution.py:246
  99.8 11.1 %collective-permute-start.3 = (f32[8,64,128]{2,1,0:T(8,128)S(1)}, f32[8,64,128]{2,1,0:T(8,128)S(1)}, u32[]{:S(2)}, u32[]{:S(2)}) collective-permute-start(f32[8,64,128]{2,1,0:T(8,128)S(1)} %constant_dynamic-update-slice_fusion), channel_id=1, source_target_pairs={{0,384},{128,0},{256,128},{384,256},{1,385},{129,1},{257,129},{385... | collective-permute-start | bytes 786440 | tf_op jit(solution)/shard_map/ppermute | solution.py:246
  111.0 3.8 %copy-start.3 = (f32[64,4,8,128]{3,2,1,0:T(8,128)S(1)}, f32[64,4,8,128]{3,2,1,0:T(8,128)}, u32[]{:S(2)}) copy-start(f32[64,4,8,128]{3,2,1,0:T(8,128)} %copy-done.2) | copy-start | bytes 3145732
  111.0 3.8 %copy-start.5 = (bf16[2,256,256]{2,1,0:T(8,128)(2,1)S(1)}, bf16[2,256,256]{2,1,0:T(8,128)(2,1)}, u32[]{:S(2)}) copy-start(bf16[2,256,256]{2,1,0:T(8,128)(2,1)} %constant.26.clone.forward) | copy-start | bytes 786436
  111.0 3.8 %copy-start.9 = (bf16[2,256,256]{2,1,0:T(8,128)(2,1)S(1)}, bf16[2,256,256]{2,1,0:T(8,128)(2,1)}, u32[]{:S(2)}) copy-start(bf16[2,256,256]{2,1,0:T(8,128)(2,1)} %constant.27.clone.inverse) | copy-start | bytes 786436
  111.0 3.8 %copy-start.12 = (bf16[2,64,144]{2,1,0:T(8,128)(2,1)S(1)}, bf16[2,64,144]{2,1,0:T(8,128)(2,1)}, u32[]{:S(2)}) copy-start(bf16[2,64,144]{2,1,0:T(8,128)(2,1)} %constant.24.clone.last) | copy-start | bytes 110596
  113.4 1.4 copy-start
  122.5 1.0 copy-start.1
  133.8 90.5 %all-to-all-start.1 = ((f32[64,4,8,128]{3,2,1,0:T(8,128)}), f32[64,4,8,128]{3,2,1,0:T(8,128)}, u32[]{:S(2)}, u32[]{:S(2)}) async-start(f32[64,4,8,128]{3,2,1,0:T(8,128)} %copy-done.1), calls=%async_computation.1 | async-start | bytes 2097152 | tf_op jit(solution)/shard_map/all_to_all | solution.py:240
  171.7 1.0 copy-start.6
  172.7 0.9 copy-start.10
  180.7 11.1 %collective-permute-start.4 = (f32[8,64,128]{2,1,0:T(8,128)S(1)}, f32[8,64,128]{2,1,0:T(8,128)S(1)}, u32[]{:S(2)}, u32[]{:S(2)}) collective-permute-start(f32[8,64,128]{2,1,0:T(8,128)S(1)} %get-tuple-element.8), channel_id=1, source_target_pairs={{0,128},{128,256},{256,384},{384,0},{1,129},{129,257},{257,385},{3... | collective-permute-start | bytes 786440 | tf_op jit(solution)/shard_map/ppermute | solution.py:246
  183.2 12.6 %collective-permute-start.5 = (f32[8,64,128]{2,1,0:T(8,128)S(1)}, f32[8,64,128]{2,1,0:T(8,128)S(1)}, u32[]{:S(2)}, u32[]{:S(2)}) collective-permute-start(f32[8,64,128]{2,1,0:T(8,128)S(1)} %get-tuple-element.6), channel_id=1, source_target_pairs={{0,256},{128,384},{256,0},{384,128},{1,257},{129,385},{257,1},{385... | collective-permute-start | bytes 786440 | tf_op jit(solution)/shard_map/ppermute | solution.py:246
  187.6 12.5 %collective-permute-start.6 = (f32[8,64,128]{2,1,0:T(8,128)S(1)}, f32[8,64,128]{2,1,0:T(8,128)S(1)}, u32[]{:S(2)}, u32[]{:S(2)}) collective-permute-start(f32[8,64,128]{2,1,0:T(8,128)S(1)} %get-tuple-element.7), channel_id=1, source_target_pairs={{0,384},{128,0},{256,128},{384,256},{1,385},{129,1},{257,129},{385... | collective-permute-start | bytes 786440 | tf_op jit(solution)/shard_map/ppermute | solution.py:246
  200.2 16.2 %collective-permute-start.7 = (f32[4,64,128]{2,1,0:T(8,128)S(1)}, f32[4,64,128]{2,1,0:T(8,128)S(1)}, u32[]{:S(2)}, u32[]{:S(2)}) collective-permute-start(f32[4,64,128]{2,1,0:T(8,128)S(1)} %slice.29), channel_id=1, source_target_pairs={{0,78},{2,76},{4,74},{6,72},{8,70},{10,68},{12,66},{14,64},{64,14}... | collective-permute-start | bytes 393224 | tf_op jit(solution)/shard_map/ppermute | solution.py:243
  (1 other events, 0.8 us)

commit v4 on v2

--- a/solution.py
+++ b/solution.py
@@ -13,9 +13,10 @@
 HALF = 72
 
 
-def two_parts(table):
+def three_parts(table, axis):
     high = np.asarray(table, np.float32).astype(jnp.bfloat16)
-    return high, (table - high.astype(np.float64)).astype(jnp.bfloat16)
+    low = (table - high.astype(np.float64)).astype(jnp.bfloat16)
+    return jnp.asarray(np.concatenate([high, high, low], axis=axis))
 
 
 def dft_tables(seq_length, norm):
@@ -29,8 +30,7 @@
     cos_outer, sin_outer = np.pad(np.cos(angle), pad), np.pad(np.sin(angle), pad)
     weights = np.where((freq == 0) | (freq == freqs - 1), 1.0, 2.0)[:, None] / padded
     weights = np.pad(weights, pad)
-    high, low = two_parts(np.concatenate([cos_outer, -sin_outer], axis=0))
-    first = np.concatenate([high, high, low], axis=1)
+    first = np.concatenate([cos_outer, -sin_outer], axis=0)
     last = np.concatenate([cos_outer * weights, -sin_outer * weights], axis=0).T
     angle = 2.0 * np.pi / INNER * (inner[:, None] * inner[None, :] % INNER)
     cos_inner, sin_inner = np.cos(angle), np.sin(angle)
@@ -38,9 +38,10 @@
     inverse = np.block([[cos_inner, sin_inner], [-sin_inner, cos_inner]])
     angle = 2.0 * np.pi / padded * (freq[:, None] * inner[None, :] % padded)
     turn = np.stack([np.pad(np.cos(angle), pad), np.pad(np.sin(angle), pad)])
-    pairs = dict(last=last, last_scaled=last * norm, forward=forward, inverse=inverse)
-    tables = {name: jnp.asarray(np.stack(two_parts(t))) for name, t in pairs.items()}
-    tables["first"] = jnp.asarray(first)
+    left = dict(first=first, last=last, last_scaled=last * norm)
+    right = dict(forward=forward, inverse=inverse)
+    tables = {name: three_parts(t, 1) for name, t in left.items()}
+    tables.update({name: three_parts(t, 0) for name, t in right.items()})
     tables["turn"] = jnp.asarray(turn, jnp.float32)
     return tables
 
@@ -65,7 +66,7 @@
             jnp.concatenate([real * cos + imag * sin, imag * cos - real * sin], axis=1)
         )
     high, low = split(jnp.concatenate(turned, axis=0))
-    return dot(high, forward[0]) + (dot(low, forward[0]) + dot(high, forward[1]))
+    return dot(jnp.concatenate([high, low, high], axis=1), forward[...])
 
 
 def correlate(spec, other):
@@ -78,7 +79,7 @@
 
 def inverse_signal(spec, inverse, turn, last):
     high, low = split(spec)
-    middle = dot(high, inverse[0]) + (dot(low, inverse[0]) + dot(high, inverse[1]))
+    middle = dot(jnp.concatenate([high, low, high], axis=1), inverse[...])
     cos, sin = turn[0], turn[1]
     back = []
     for at in range(0, spec.shape[0], HALF):
@@ -87,11 +88,18 @@
             jnp.concatenate([real * cos - imag * sin, imag * cos + real * sin], axis=0)
         )
     high, low = split(jnp.concatenate(back, axis=1))
-    return dot(last[0], high) + (dot(last[0], low) + dot(last[1], high))
+    return dot(last[...], jnp.concatenate([high, low, high], axis=0))
+
+
+def row(r, block):
+    a, rows, _ = block.shape
+    return pl.ds(r, a, stride=rows)
 
 
 def rows_to_wide(block):
-    return jnp.concatenate([block[:, r, :] for r in range(block.shape[1])], axis=1)
+    a, rows, m = block.shape
+    flat = block.reshape(a * rows, m)
+    return jnp.concatenate([flat[row(r, block), :] for r in range(rows)], axis=1)
 
 
 def filter_kernel(first, turn, forward, filters, spec):
@@ -102,8 +110,10 @@
 def input_grad_kernel(at, first, turn, forward, inverse, last, grad, filter_spec, spec, out):
     spec[...] = forward_spectrum(rows_to_wide(grad), first, turn, forward)
     wide = inverse_signal(correlate(spec[...], filter_spec[...]), inverse, turn, last)
-    for r in range(out.shape[1]):
-        out[:, r, :] = wide[:, r * INNER : (r + 1) * INNER]
+    a, rows, m = out.shape
+    flat = out.reshape(a * rows, m)
+    for r in range(rows):
+        flat[row(r, out), :] = wide[:, r * INNER : (r + 1) * INNER]
 
 
 def filter_grad_kernel(at, first, turn, forward, inverse, last, tokens, grad_spec, out):
@@ -134,7 +144,7 @@
         out_shape=jax.ShapeDtypeStruct((count, r * HALF, 2 * m), jnp.float32),
         in_specs=specs + [pl.BlockSpec((None, r, a, m), lambda i: (i, 0, 0, 0))],
         out_specs=pl.BlockSpec((None, r * HALF, 2 * m), lambda i: (i, 0, 0)),
-        cost_estimate=cost(10**9, 8 * filters.size),
+        cost_estimate=cost(83 * 10**9, 8 * filters.size),
         compiler_params=LIMIT,
     )(*operands, filters)
 
@@ -252,11 +262,9 @@
         [grad_out.reshape(whole_shape), inputs.reshape(whole_shape)],
         (y, z, c, 2, x, h * j, INNER),
     )
-    both, filters = lax.optimization_barrier((both, filters))
     both = exchange(both.reshape(rows, 2, x, h * j, INNER))
 
-    filters = filters.reshape(j, rows, INNER)
-    pair = jnp.concatenate([filters, facing(filters)])
+    pair = jnp.concatenate([filters, facing(filters)]).reshape(h * j, rows, INNER)
     taps = jnp.stack([pair] + [along_x(pair, s) for s in range(1, x)])
     filter_spec = filter_spectrum(taps, tables)
 

time: 203 us -> 195 us (0.961); the launches traced: 200 us -> 195 us
  starting transfers between devices: 71.1 us -> 56.4 us
  waiting for transfers between devices: 103 us -> 112 us
    all_to_all x2, starting transfers between devices: 36.6 us -> 21.4 us  [exchange(): return lax.all_to_all(blocks, ('y', 'zl', 'c'), 0, 0, tiled=True)]
    all_to_all x2, waiting for transfers between devices: 74.4 us -> 88.3 us  [exchange(): return lax.all_to_all(blocks, ('y', 'zl', 'c'), 0, 0, tiled=True)]
    ppermute x2, waiting for transfers between devices: 12.2 us -> 7.93 us  [facing(): lax.ppermute(v, ('zh', 'zl'), [(i, h * z - 1 - i) for i in range(h * z)])]
  transfers between devices with their start and end apart: 10 -> 10, of which waited for: 8 -> 8; matrix products, arithmetic and copies ran while one was open for 1% -> 1% of each run, Pallas kernels for 5% -> 6%
where the time goes in v4:
time: 195 us
  waiting for transfers between devices  112 us (57%)
  starting transfers between devices  56.4 us (29%)
  Pallas kernels  21.9 us (11%)
  local copies, waits for them, and re-layouts  2.33 us (1%)
    all_to_all x2, waiting for transfers between devices, exchange(): return lax.all_to_all(blocks, ('y', 'zl', 'c'), 0, 0, tiled=True)  88.3 us
    all_to_all x2, starting transfers between devices, exchange(): return lax.all_to_all(blocks, ('y', 'zl', 'c'), 0, 0, tiled=True)  21.4 us
    ppermute x6, starting transfers between devices, along_x(): return lax.ppermute(v, 'x', [(i, (i + s) % x) for i in range(x)])  19.6 us
    ppermute x6, waiting for transfers between devices, along_x(): return lax.ppermute(v, 'x', [(i, (i + s) % x) for i in range(x)])  15.8 us
    ppermute x2, starting transfers between devices, facing(): lax.ppermute(v, ('zh', 'zl'), [(i, h * z - 1 - i) for i in range(h * z)])  15.4 us
    ppermute x2, waiting for transfers between devices, facing(): lax.ppermute(v, ('zh', 'zl'), [(i, h * z - 1 - i) for i in range(h * z)])  7.93 us
    pallas_call x1, Pallas kernels, input_grad_part(): pl.pallas_call(input_grad_kernel, grid_spec=grid_spec, out_shape=[jax.Sha...  7.55 us
    pallas_call x1, Pallas kernels, filter_grad_part(): pl.pallas_call(filter_grad_kernel, grid_spec=grid_spec, out_shape=jax.Sha...  6.8 us
  transfers between devices with their start and end apart: 10, of which 8 were waited for; matrix products, arithmetic and copies ran while one was open for 1% of the time, Pallas kernels for 6%

profile of v4, /device:TPU:6, one launch (start us, length us, event | category | flops | bytes accessed | tf_op | source)
XLA Modules:
  0.0 194.8 jit_solution(1653727016196517579)
XLA Ops:
  0.6 11.4 %collective-permute-start = (f32[4,8192]{1,0:T(4,128)}, f32[4,8192]{1,0:T(4,128)S(1)}, u32[]{:S(2)}, u32[]{:S(2)}) collective-permute-start(f32[4,8192]{1,0:T(4,128)} %param.11), channel_id=1, source_target_pairs={{0,78},{2,76},{4,74},{6,72},{8,70},{10,68},{12,66},{14,64},{64,14}... | collective-permute-start | bytes 393224 | tf_op jit(solution)/shard_map/ppermute | solution.py:254
  12.0 3.0 %shard_map.104 = f32[4,8,2,2,4,8,128]{6,5,4,3,2,1,0:T(8,128)} custom-call(s32[1]{0:T(128)} %bitcast.half, f32[4,2,4,8,8,128]{5,4,3,2,1,0:T(8,128)} %bitcast.35, f32[4,2,4,8,8,128]{5,4,3,2,1,0:T(8,128)} %bitcast.36), custom_call_target="tpu_custom_call" | custom-call | bytes 4194304 | tf_op jit(solution)/shard_map/pallas_call | solution.py:230
  15.1 11.3 %all-to-all-start = ((f32[64,2,4,8,128]{4,3,2,1,0:T(8,128)}), f32[64,2,4,8,128]{4,3,2,1,0:T(8,128)S(1)}, u32[]{:S(2)}, u32[]{:S(2)}) async-start(f32[64,2,4,8,128]{4,3,2,1,0:T(8,128)} %bitcast.34), calls=%async_computation | async-start | bytes 4194304 | tf_op jit(solution)/shard_map/all_to_all | solution.py:251
  26.6 3.3 %collective-permute-start.2 = (f32[8,64,128]{2,1,0:T(8,128)S(1)}, f32[8,64,128]{2,1,0:T(8,128)S(1)}, u32[]{:S(2)}, u32[]{:S(2)}) collective-permute-start(f32[8,64,128]{2,1,0:T(8,128)S(1)} %bitcast.38), channel_id=1, source_target_pairs={{0,256},{128,384},{256,0},{384,128},{1,257},{129,385},{257,1},{385... | collective-permute-start | bytes 786440 | tf_op jit(solution)/shard_map/ppermute | solution.py:257
  29.9 4.0 %collective-permute-start.1 = (f32[8,64,128]{2,1,0:T(8,128)S(1)}, f32[8,64,128]{2,1,0:T(8,128)S(1)}, u32[]{:S(2)}, u32[]{:S(2)}) collective-permute-start(f32[8,64,128]{2,1,0:T(8,128)S(1)} %bitcast.39), channel_id=1, source_target_pairs={{0,128},{128,256},{256,384},{384,0},{1,129},{129,257},{257,385},{3... | collective-permute-start | bytes 786440 | tf_op jit(solution)/shard_map/ppermute | solution.py:257
  33.9 1.9 collective-permute-start.3
  35.8 2.6 %collective-permute-done.2 = f32[8,64,128]{2,1,0:T(8,128)S(1)} collective-permute-done((f32[8,64,128]{2,1,0:T(8,128)S(1)}, f32[8,64,128]{2,1,0:T(8,128)S(1)}, u32[]{:S(2)}, u32[]{:S(2)}) %collective-permute-start.2) | collective-permute-done | bytes 262176 | tf_op jit(solution)/shard_map/ppermute | solution.py:257
  38.5 3.2 %collective-permute-done.1 = f32[8,64,128]{2,1,0:T(8,128)S(1)} collective-permute-done((f32[8,64,128]{2,1,0:T(8,128)S(1)}, f32[8,64,128]{2,1,0:T(8,128)S(1)}, u32[]{:S(2)}, u32[]{:S(2)}) %collective-permute-start.1) | collective-permute-done | bytes 262176 | tf_op jit(solution)/shard_map/ppermute | solution.py:257
  41.6 3.2 %collective-permute-done.3 = f32[8,64,128]{2,1,0:T(8,128)} collective-permute-done((f32[8,64,128]{2,1,0:T(8,128)S(1)}, f32[8,64,128]{2,1,0:T(8,128)}, u32[]{:S(2)}, u32[]{:S(2)}) %collective-permute-start.3) | collective-permute-done | bytes 262176 | tf_op jit(solution)/shard_map/ppermute | solution.py:257
  45.9 2.3 %shard_map.105.filter_spec = f32[4,576,256]{2,1,0:T(8,128)S(1)} custom-call(bf16[144,192]{1,0:T(8,128)(2,1)S(1)} %copy-done.3, f32[2,72,128]{2,1,0:T(8,128)S(1)} %copy-done.2, bf16[768,256]{1,0:T(8,128)(2,1)S(1)} %copy-done, f32[4,8,64,128]{3,2,1,0:T(8,128)S(1)} %pad_maximum_fusion.filters), custom_call_target="tpu_custom_call" | custom-call | flops 83000000512 | bytes 2097152 | tf_op jit(solution)/shard_map/pallas_call | solution.py:141
  48.3 1.4 copy-done.6
  49.7 71.3 %all-to-all-done.grad.tokens = f32[64,2,4,8,128]{4,3,2,1,0:T(8,128)S(1)} async-done(((f32[64,2,4,8,128]{4,3,2,1,0:T(8,128)}), f32[64,2,4,8,128]{4,3,2,1,0:T(8,128)S(1)}, u32[]{:S(2)}, u32[]{:S(2)}) %all-to-all-start) | async-done | bytes 2097184 | tf_op jit(solution)/shard_map/all_to_all | solution.py:251
  121.0 7.5 %shard_map.106 = (f32[4,576,256]{2,1,0:T(8,128)}, f32[64,4,8,128]{3,2,1,0:T(8,128)}) custom-call(s32[1]{0:T(128)} %bitcast.1.at, bf16[144,192]{1,0:T(8,128)(2,1)S(1)} %copy-done.3, f32[2,72,128]{2,1,0:T(8,128)S(1)} %copy-done.2, bf16[768,256]{1,0:T(8,128)(2,1)S(1)} %copy-done, bf16[768,256]{1,0:T(8,128)(2,1)S(1)} %copy-done.1, ...), custom_call_target="tpu_custom_call" | custom-call | flops 2000000000 | bytes 4194304 | tf_op jit(solution)/shard_map/pallas_call | solution.py:170
  128.5 10.1 %all-to-all-start.1 = ((f32[64,4,8,128]{3,2,1,0:T(8,128)}), f32[64,4,8,128]{3,2,1,0:T(8,128)}, u32[]{:S(2)}, u32[]{:S(2)}) async-start(f32[64,4,8,128]{3,2,1,0:T(8,128)} %get-tuple-element.4), calls=%async_computation.1 | async-start | bytes 2097152 | tf_op jit(solution)/shard_map/all_to_all | solution.py:251
  138.6 6.8 %shard_map.108 = f32[4,8,64,128]{3,2,1,0:T(8,128)S(1)} custom-call(s32[1]{0:T(128)} %bitcast.1.at, bf16[144,192]{1,0:T(8,128)(2,1)S(1)} %copy-done.3, f32[2,72,128]{2,1,0:T(8,128)S(1)} %copy-done.2, bf16[768,256]{1,0:T(8,128)(2,1)S(1)} %copy-done, bf16[768,256]{1,0:T(8,128)(2,1)S(1)} %copy-done.1, bf16[64,432]{1,0:T(8,128)(2,1)S(1)} %copy-done.4, ...), custom_call_target="tpu_custom_call" | custom-call | tf_op jit(solution)/shard_map/pallas_call | solution.py:198
  145.5 3.3 %collective-permute-start.5 = (f32[8,64,128]{2,1,0:T(8,128)S(1)}, f32[8,64,128]{2,1,0:T(8,128)S(1)}, u32[]{:S(2)}, u32[]{:S(2)}) collective-permute-start(f32[8,64,128]{2,1,0:T(8,128)S(1)} %get-tuple-element.6), channel_id=1, source_target_pairs={{0,256},{128,384},{256,0},{384,128},{1,257},{129,385},{257,1},{385... | collective-permute-start | bytes 786440 | tf_op jit(solution)/shard_map/ppermute | solution.py:257
  148.8 1.9 collective-permute-start.6
  150.7 5.1 %collective-permute-start.4 = (f32[8,64,128]{2,1,0:T(8,128)S(1)}, f32[8,64,128]{2,1,0:T(8,128)S(1)}, u32[]{:S(2)}, u32[]{:S(2)}) collective-permute-start(f32[8,64,128]{2,1,0:T(8,128)S(1)} %get-tuple-element.8), channel_id=1, source_target_pairs={{0,128},{128,256},{256,384},{384,0},{1,129},{129,257},{257,385},{3... | collective-permute-start | bytes 786440 | tf_op jit(solution)/shard_map/ppermute | solution.py:257
  155.9 2.2 %collective-permute-done.5 = f32[8,64,128]{2,1,0:T(8,128)S(1)} collective-permute-done((f32[8,64,128]{2,1,0:T(8,128)S(1)}, f32[8,64,128]{2,1,0:T(8,128)S(1)}, u32[]{:S(2)}, u32[]{:S(2)}) %collective-permute-start.5) | collective-permute-done | bytes 262176 | tf_op jit(solution)/shard_map/ppermute | solution.py:257
  158.1 4.6 %collective-permute-done.6 = f32[8,64,128]{2,1,0:T(8,128)S(1)} collective-permute-done((f32[8,64,128]{2,1,0:T(8,128)S(1)}, f32[8,64,128]{2,1,0:T(8,128)S(1)}, u32[]{:S(2)}, u32[]{:S(2)}) %collective-permute-start.6) | collective-permute-done | bytes 262176 | tf_op jit(solution)/shard_map/ppermute | solution.py:257
  162.8 4.0 %collective-permute-start.7 = (f32[4,64,128]{2,1,0:T(8,128)S(1)}, f32[4,64,128]{2,1,0:T(8,128)S(1)}, u32[]{:S(2)}, u32[]{:S(2)}) collective-permute-start(f32[4,64,128]{2,1,0:T(8,128)S(1)} %slice.29), channel_id=1, source_target_pairs={{0,78},{2,76},{4,74},{6,72},{8,70},{10,68},{12,66},{14,64},{64,14}... | collective-permute-start | bytes 393224 | tf_op jit(solution)/shard_map/ppermute | solution.py:254
  166.8 7.9 %collective-permute-done.7 = f32[4,64,128]{2,1,0:T(8,128)S(1)} collective-permute-done((f32[4,64,128]{2,1,0:T(8,128)S(1)}, f32[4,64,128]{2,1,0:T(8,128)S(1)}, u32[]{:S(2)}, u32[]{:S(2)}) %collective-permute-start.7) | collective-permute-done | bytes 131104 | tf_op jit(solution)/shard_map/ppermute | solution.py:254
  175.4 17.1 %all-to-all-done.1 = f32[64,4,8,128]{3,2,1,0:T(8,128)} async-done(((f32[64,4,8,128]{3,2,1,0:T(8,128)}), f32[64,4,8,128]{3,2,1,0:T(8,128)}, u32[]{:S(2)}, u32[]{:S(2)}) %all-to-all-start.1) | async-done | bytes 1048608 | tf_op jit(solution)/shard_map/all_to_all | solution.py:251
  192.5 2.3 %shard_map.107 = f32[4,2,4,8,8,128]{5,4,3,2,1,0:T(8,128)} custom-call(s32[1]{0:T(128)} %bitcast.half, f32[4,8,2,4,8,128]{5,4,3,2,1,0:T(8,128)} %bitcast.8.blocks), custom_call_target="tpu_custom_call" | custom-call | bytes 2097152 | tf_op jit(solution)/shard_map/pallas_call | solution.py:230
  (25 shorter events, 2.1 us)
Async XLA Ops:
  0.6 25.8 %collective-permute-start = (f32[4,8192]{1,0:T(4,128)}, f32[4,8192]{1,0:T(4,128)S(1)}, u32[]{:S(2)}, u32[]{:S(2)}) collective-permute-start(f32[4,8192]{1,0:T(4,128)} %param.11), channel_id=1, source_target_pairs={{0,78},{2,76},{4,74},{6,72},{8,70},{10,68},{12,66},{14,64},{64,14}... | collective-permute-start | bytes 393224 | tf_op jit(solution)/shard_map/ppermute | solution.py:254
  15.1 11.4 %copy-start.7 = (f32[4,8192]{1,0:T(4,128)S(1)}, f32[4,8192]{1,0:T(4,128)}, u32[]{:S(2)}) copy-start(f32[4,8192]{1,0:T(4,128)} %param.11) | copy-start | bytes 393220
  15.1 105.9 %all-to-all-start = ((f32[64,2,4,8,128]{4,3,2,1,0:T(8,128)}), f32[64,2,4,8,128]{4,3,2,1,0:T(8,128)S(1)}, u32[]{:S(2)}, u32[]{:S(2)}) async-start(f32[64,2,4,8,128]{4,3,2,1,0:T(8,128)} %bitcast.34), calls=%async_computation | async-start | bytes 4194304 | tf_op jit(solution)/shard_map/all_to_all | solution.py:251
  26.4 19.5 %copy-start = (bf16[768,256]{1,0:T(8,128)(2,1)S(1)}, bf16[768,256]{1,0:T(8,128)(2,1)}, u32[]{:S(2)}) copy-start(bf16[768,256]{1,0:T(8,128)(2,1)} %constant.27.clone.forward) | copy-start | bytes 1179652
  26.4 19.5 %copy-start.2 = (f32[2,72,128]{2,1,0:T(8,128)S(1)}, f32[2,72,128]{2,1,0:T(8,128)}, u32[]{:S(2)}) copy-start(f32[2,72,128]{2,1,0:T(8,128)} %constant.29.clone.turn) | copy-start | bytes 221188
  26.4 19.5 %copy-start.3 = (bf16[144,192]{1,0:T(8,128)(2,1)S(1)}, bf16[144,192]{1,0:T(8,128)(2,1)}, u32[]{:S(2)}) copy-start(bf16[144,192]{1,0:T(8,128)(2,1)} %constant.24.clone.first) | copy-start | bytes 165892
  26.6 11.9 %collective-permute-start.2 = (f32[8,64,128]{2,1,0:T(8,128)S(1)}, f32[8,64,128]{2,1,0:T(8,128)S(1)}, u32[]{:S(2)}, u32[]{:S(2)}) collective-permute-start(f32[8,64,128]{2,1,0:T(8,128)S(1)} %bitcast.38), channel_id=1, source_target_pairs={{0,256},{128,384},{256,0},{384,128},{1,257},{129,385},{257,1},{385... | collective-permute-start | bytes 786440 | tf_op jit(solution)/shard_map/ppermute | solution.py:257
  29.9 11.8 %collective-permute-start.1 = (f32[8,64,128]{2,1,0:T(8,128)S(1)}, f32[8,64,128]{2,1,0:T(8,128)S(1)}, u32[]{:S(2)}, u32[]{:S(2)}) collective-permute-start(f32[8,64,128]{2,1,0:T(8,128)S(1)} %bitcast.39), channel_id=1, source_target_pairs={{0,128},{128,256},{256,384},{384,0},{1,129},{129,257},{257,385},{3... | collective-permute-start | bytes 786440 | tf_op jit(solution)/shard_map/ppermute | solution.py:257
  33.9 10.9 %collective-permute-start.3 = (f32[8,64,128]{2,1,0:T(8,128)S(1)}, f32[8,64,128]{2,1,0:T(8,128)}, u32[]{:S(2)}, u32[]{:S(2)}) collective-permute-start(f32[8,64,128]{2,1,0:T(8,128)S(1)} %bitcast.40), channel_id=1, source_target_pairs={{0,384},{128,0},{256,128},{384,256},{1,385},{129,1},{257,129},{385... | collective-permute-start | bytes 786440 | tf_op jit(solution)/shard_map/ppermute | solution.py:257
  45.9 75.1 %copy-start.1 = (bf16[768,256]{1,0:T(8,128)(2,1)S(1)}, bf16[768,256]{1,0:T(8,128)(2,1)}, u32[]{:S(2)}) copy-start(bf16[768,256]{1,0:T(8,128)(2,1)} %constant.28.clone.inverse) | copy-start | bytes 1179652
  45.9 75.0 %copy-start.5 = (bf16[64,432]{1,0:T(8,128)(2,1)S(1)}, bf16[64,432]{1,0:T(8,128)(2,1)}, u32[]{:S(2)}) copy-start(bf16[64,432]{1,0:T(8,128)(2,1)} %constant.25.clone.last) | copy-start | bytes 165892
  48.2 1.4 copy-start.6
  121.0 17.6 %copy-start.4 = (bf16[64,432]{1,0:T(8,128)(2,1)S(1)}, bf16[64,432]{1,0:T(8,128)(2,1)}, u32[]{:S(2)}) copy-start(bf16[64,432]{1,0:T(8,128)(2,1)} %constant.26.clone.last) | copy-start | bytes 165892
  128.5 64.0 %all-to-all-start.1 = ((f32[64,4,8,128]{3,2,1,0:T(8,128)}), f32[64,4,8,128]{3,2,1,0:T(8,128)}, u32[]{:S(2)}, u32[]{:S(2)}) async-start(f32[64,4,8,128]{3,2,1,0:T(8,128)} %get-tuple-element.4), calls=%async_computation.1 | async-start | bytes 2097152 | tf_op jit(solution)/shard_map/all_to_all | solution.py:251
  145.5 12.6 %collective-permute-start.5 = (f32[8,64,128]{2,1,0:T(8,128)S(1)}, f32[8,64,128]{2,1,0:T(8,128)S(1)}, u32[]{:S(2)}, u32[]{:S(2)}) collective-permute-start(f32[8,64,128]{2,1,0:T(8,128)S(1)} %get-tuple-element.6), channel_id=1, source_target_pairs={{0,256},{128,384},{256,0},{384,128},{1,257},{129,385},{257,1},{385... | collective-permute-start | bytes 786440 | tf_op jit(solution)/shard_map/ppermute | solution.py:257
  148.8 13.9 %collective-permute-start.6 = (f32[8,64,128]{2,1,0:T(8,128)S(1)}, f32[8,64,128]{2,1,0:T(8,128)S(1)}, u32[]{:S(2)}, u32[]{:S(2)}) collective-permute-start(f32[8,64,128]{2,1,0:T(8,128)S(1)} %get-tuple-element.7), channel_id=1, source_target_pairs={{0,384},{128,0},{256,128},{384,256},{1,385},{129,1},{257,129},{385... | collective-permute-start | bytes 786440 | tf_op jit(solution)/shard_map/ppermute | solution.py:257
  150.7 11.9 %collective-permute-start.4 = (f32[8,64,128]{2,1,0:T(8,128)S(1)}, f32[8,64,128]{2,1,0:T(8,128)S(1)}, u32[]{:S(2)}, u32[]{:S(2)}) collective-permute-start(f32[8,64,128]{2,1,0:T(8,128)S(1)} %get-tuple-element.8), channel_id=1, source_target_pairs={{0,128},{128,256},{256,384},{384,0},{1,129},{129,257},{257,385},{3... | collective-permute-start | bytes 786440 | tf_op jit(solution)/shard_map/ppermute | solution.py:257
  162.8 11.9 %collective-permute-start.7 = (f32[4,64,128]{2,1,0:T(8,128)S(1)}, f32[4,64,128]{2,1,0:T(8,128)S(1)}, u32[]{:S(2)}, u32[]{:S(2)}) collective-permute-start(f32[4,64,128]{2,1,0:T(8,128)S(1)} %slice.29), channel_id=1, source_target_pairs={{0,78},{2,76},{4,74},{6,72},{8,70},{10,68},{12,66},{14,64},{64,14}... | collective-permute-start | bytes 393224 | tf_op jit(solution)/shard_map/ppermute | solution.py:254

commit v5 on v4

--- a/solution.py
+++ b/solution.py
@@ -262,6 +262,7 @@
         [grad_out.reshape(whole_shape), inputs.reshape(whole_shape)],
         (y, z, c, 2, x, h * j, INNER),
     )
+    both, filters = lax.optimization_barrier((both, filters))
     both = exchange(both.reshape(rows, 2, x, h * j, INNER))
 
     pair = jnp.concatenate([filters, facing(filters)]).reshape(h * j, rows, INNER)

time: 195 us -> 195 us (level)
  transfers between devices with their start and end apart: 10 -> 10, of which waited for: 8 -> 9; matrix products, arithmetic and copies ran while one was open for 1% -> 1% of each run, Pallas kernels for 6% -> 5%
where the time goes in v5:
time: 195 us
  waiting for transfers between devices  112 us (57%)
  starting transfers between devices  56.2 us (29%)
  Pallas kernels  22 us (11%)
  local copies, waits for them, and re-layouts  2.33 us (1%)
    all_to_all x2, waiting for transfers between devices, exchange(): return lax.all_to_all(blocks, ('y', 'zl', 'c'), 0, 0, tiled=True)  88.1 us
    all_to_all x2, starting transfers between devices, exchange(): return lax.all_to_all(blocks, ('y', 'zl', 'c'), 0, 0, tiled=True)  21.3 us
    ppermute x6, starting transfers between devices, along_x(): return lax.ppermute(v, 'x', [(i, (i + s) % x) for i in range(x)])  19.6 us
    ppermute x2, starting transfers between devices, facing(): lax.ppermute(v, ('zh', 'zl'), [(i, h * z - 1 - i) for i in range(h * z)])  15.4 us
    ppermute x6, waiting for transfers between devices, along_x(): return lax.ppermute(v, 'x', [(i, (i + s) % x) for i in range(x)])  15.4 us
    ppermute x2, waiting for transfers between devices, facing(): lax.ppermute(v, ('zh', 'zl'), [(i, h * z - 1 - i) for i in range(h * z)])  8.6 us
    pallas_call x1, Pallas kernels, input_grad_part(): pl.pallas_call(input_grad_kernel, grid_spec=grid_spec, out_shape=[jax.Sha...  7.56 us
    pallas_call x1, Pallas kernels, filter_grad_part(): pl.pallas_call(filter_grad_kernel, grid_spec=grid_spec, out_shape=jax.Sha...  6.79 us
  transfers between devices with their start and end apart: 10, of which 9 were waited for; matrix products, arithmetic and copies ran while one was open for 1% of the time, Pallas kernels for 5%

profile of v5, /device:TPU:6, one launch (start us, length us, event | category | flops | bytes accessed | tf_op | source)
XLA Modules:
  0.0 194.7 jit_solution(6512271158212900525)
XLA Ops:
  0.6 3.1 %shard_map.104 = f32[4,8,2,2,4,8,128]{6,5,4,3,2,1,0:T(8,128)} custom-call(s32[1]{0:T(128)} %bitcast.half, f32[4,2,4,8,8,128]{5,4,3,2,1,0:T(8,128)} %bitcast.35, f32[4,2,4,8,8,128]{5,4,3,2,1,0:T(8,128)} %bitcast.36), custom_call_target="tpu_custom_call" | custom-call | bytes 4194304 | tf_op jit(solution)/shard_map/pallas_call | solution.py:230
  3.7 11.4 %collective-permute-start = (f32[4,8192]{1,0:T(4,128)S(1)}, f32[4,8192]{1,0:T(4,128)S(1)}, u32[]{:S(2)}, u32[]{:S(2)}) collective-permute-start(f32[4,8192]{1,0:T(4,128)S(1)} %copy-done.7), channel_id=1, source_target_pairs={{0,78},{2,76},{4,74},{6,72},{8,70},{10,68},{12,66},{14,64},{64,14}... | collective-permute-start | bytes 393224 | tf_op jit(solution)/shard_map/ppermute | solution.py:254
  15.1 11.2 %all-to-all-start = ((f32[64,2,4,8,128]{4,3,2,1,0:T(8,128)}), f32[64,2,4,8,128]{4,3,2,1,0:T(8,128)S(1)}, u32[]{:S(2)}, u32[]{:S(2)}) async-start(f32[64,2,4,8,128]{4,3,2,1,0:T(8,128)} %bitcast.34), calls=%async_computation | async-start | bytes 4194304 | tf_op jit(solution)/shard_map/all_to_all | solution.py:251
  27.1 3.3 %collective-permute-start.2 = (f32[8,64,128]{2,1,0:T(8,128)S(1)}, f32[8,64,128]{2,1,0:T(8,128)S(1)}, u32[]{:S(2)}, u32[]{:S(2)}) collective-permute-start(f32[8,64,128]{2,1,0:T(8,128)S(1)} %bitcast.38), channel_id=1, source_target_pairs={{0,256},{128,384},{256,0},{384,128},{1,257},{129,385},{257,1},{385... | collective-permute-start | bytes 786440 | tf_op jit(solution)/shard_map/ppermute | solution.py:257
  30.5 4.0 %collective-permute-start.1 = (f32[8,64,128]{2,1,0:T(8,128)S(1)}, f32[8,64,128]{2,1,0:T(8,128)S(1)}, u32[]{:S(2)}, u32[]{:S(2)}) collective-permute-start(f32[8,64,128]{2,1,0:T(8,128)S(1)} %bitcast.39), channel_id=1, source_target_pairs={{0,128},{128,256},{256,384},{384,0},{1,129},{129,257},{257,385},{3... | collective-permute-start | bytes 786440 | tf_op jit(solution)/shard_map/ppermute | solution.py:257
  34.5 1.9 collective-permute-start.3
  36.4 2.2 %collective-permute-done.2 = f32[8,64,128]{2,1,0:T(8,128)S(1)} collective-permute-done((f32[8,64,128]{2,1,0:T(8,128)S(1)}, f32[8,64,128]{2,1,0:T(8,128)S(1)}, u32[]{:S(2)}, u32[]{:S(2)}) %collective-permute-start.2) | collective-permute-done | bytes 262176 | tf_op jit(solution)/shard_map/ppermute | solution.py:257
  38.6 3.2 %collective-permute-done.1 = f32[8,64,128]{2,1,0:T(8,128)S(1)} collective-permute-done((f32[8,64,128]{2,1,0:T(8,128)S(1)}, f32[8,64,128]{2,1,0:T(8,128)S(1)}, u32[]{:S(2)}, u32[]{:S(2)}) %collective-permute-start.1) | collective-permute-done | bytes 262176 | tf_op jit(solution)/shard_map/ppermute | solution.py:257
  41.8 3.2 %collective-permute-done.3 = f32[8,64,128]{2,1,0:T(8,128)} collective-permute-done((f32[8,64,128]{2,1,0:T(8,128)S(1)}, f32[8,64,128]{2,1,0:T(8,128)}, u32[]{:S(2)}, u32[]{:S(2)}) %collective-permute-start.3) | collective-permute-done | bytes 262176 | tf_op jit(solution)/shard_map/ppermute | solution.py:257
  46.0 2.3 %shard_map.105.filter_spec = f32[4,576,256]{2,1,0:T(8,128)S(1)} custom-call(bf16[144,192]{1,0:T(8,128)(2,1)S(1)} %copy-done.3, f32[2,72,128]{2,1,0:T(8,128)S(1)} %copy-done.2, bf16[768,256]{1,0:T(8,128)(2,1)S(1)} %copy-done, f32[4,8,64,128]{3,2,1,0:T(8,128)S(1)} %pad_maximum_fusion.filters), custom_call_target="tpu_custom_call" | custom-call | flops 83000000512 | bytes 2097152 | tf_op jit(solution)/shard_map/pallas_call | solution.py:141
  48.4 1.4 copy-done.6
  49.8 71.1 %all-to-all-done.grad.tokens = f32[64,2,4,8,128]{4,3,2,1,0:T(8,128)S(1)} async-done(((f32[64,2,4,8,128]{4,3,2,1,0:T(8,128)}), f32[64,2,4,8,128]{4,3,2,1,0:T(8,128)S(1)}, u32[]{:S(2)}, u32[]{:S(2)}) %all-to-all-start) | async-done | bytes 2097184 | tf_op jit(solution)/shard_map/all_to_all | solution.py:251
  120.9 7.6 %shard_map.106 = (f32[4,576,256]{2,1,0:T(8,128)}, f32[64,4,8,128]{3,2,1,0:T(8,128)}) custom-call(s32[1]{0:T(128)} %bitcast.1.at, bf16[144,192]{1,0:T(8,128)(2,1)S(1)} %copy-done.3, f32[2,72,128]{2,1,0:T(8,128)S(1)} %copy-done.2, bf16[768,256]{1,0:T(8,128)(2,1)S(1)} %copy-done, bf16[768,256]{1,0:T(8,128)(2,1)S(1)} %copy-done.1, ...), custom_call_target="tpu_custom_call" | custom-call | flops 2000000000 | bytes 4194304 | tf_op jit(solution)/shard_map/pallas_call | solution.py:170
  128.4 10.1 %all-to-all-start.1 = ((f32[64,4,8,128]{3,2,1,0:T(8,128)}), f32[64,4,8,128]{3,2,1,0:T(8,128)}, u32[]{:S(2)}, u32[]{:S(2)}) async-start(f32[64,4,8,128]{3,2,1,0:T(8,128)} %get-tuple-element.8), calls=%async_computation.1 | async-start | bytes 2097152 | tf_op jit(solution)/shard_map/all_to_all | solution.py:251
  138.5 6.8 %shard_map.108 = f32[4,8,64,128]{3,2,1,0:T(8,128)S(1)} custom-call(s32[1]{0:T(128)} %bitcast.1.at, bf16[144,192]{1,0:T(8,128)(2,1)S(1)} %copy-done.3, f32[2,72,128]{2,1,0:T(8,128)S(1)} %copy-done.2, bf16[768,256]{1,0:T(8,128)(2,1)S(1)} %copy-done, bf16[768,256]{1,0:T(8,128)(2,1)S(1)} %copy-done.1, bf16[64,432]{1,0:T(8,128)(2,1)S(1)} %copy-done.4, ...), custom_call_target="tpu_custom_call" | custom-call | tf_op jit(solution)/shard_map/pallas_call | solution.py:198
  145.4 3.3 %collective-permute-start.5 = (f32[8,64,128]{2,1,0:T(8,128)S(1)}, f32[8,64,128]{2,1,0:T(8,128)S(1)}, u32[]{:S(2)}, u32[]{:S(2)}) collective-permute-start(f32[8,64,128]{2,1,0:T(8,128)S(1)} %get-tuple-element.10), channel_id=1, source_target_pairs={{0,256},{128,384},{256,0},{384,128},{1,257},{129,385},{257,1},{385... | collective-permute-start | bytes 786440 | tf_op jit(solution)/shard_map/ppermute | solution.py:257
  148.7 1.9 collective-permute-start.6
  150.6 5.1 %collective-permute-start.4 = (f32[8,64,128]{2,1,0:T(8,128)S(1)}, f32[8,64,128]{2,1,0:T(8,128)S(1)}, u32[]{:S(2)}, u32[]{:S(2)}) collective-permute-start(f32[8,64,128]{2,1,0:T(8,128)S(1)} %get-tuple-element.12), channel_id=1, source_target_pairs={{0,128},{128,256},{256,384},{384,0},{1,129},{129,257},{257,385},{3... | collective-permute-start | bytes 786440 | tf_op jit(solution)/shard_map/ppermute | solution.py:257
  155.8 2.2 %collective-permute-done.5 = f32[8,64,128]{2,1,0:T(8,128)S(1)} collective-permute-done((f32[8,64,128]{2,1,0:T(8,128)S(1)}, f32[8,64,128]{2,1,0:T(8,128)S(1)}, u32[]{:S(2)}, u32[]{:S(2)}) %collective-permute-start.5) | collective-permute-done | bytes 262176 | tf_op jit(solution)/shard_map/ppermute | solution.py:257
  158.0 4.6 %collective-permute-done.6 = f32[8,64,128]{2,1,0:T(8,128)S(1)} collective-permute-done((f32[8,64,128]{2,1,0:T(8,128)S(1)}, f32[8,64,128]{2,1,0:T(8,128)S(1)}, u32[]{:S(2)}, u32[]{:S(2)}) %collective-permute-start.6) | collective-permute-done | bytes 262176 | tf_op jit(solution)/shard_map/ppermute | solution.py:257
  162.7 4.0 %collective-permute-start.7 = (f32[4,64,128]{2,1,0:T(8,128)S(1)}, f32[4,64,128]{2,1,0:T(8,128)S(1)}, u32[]{:S(2)}, u32[]{:S(2)}) collective-permute-start(f32[4,64,128]{2,1,0:T(8,128)S(1)} %slice.29), channel_id=1, source_target_pairs={{0,78},{2,76},{4,74},{6,72},{8,70},{10,68},{12,66},{14,64},{64,14}... | collective-permute-start | bytes 393224 | tf_op jit(solution)/shard_map/ppermute | solution.py:254
  166.7 7.9 %collective-permute-done.7 = f32[4,64,128]{2,1,0:T(8,128)S(1)} collective-permute-done((f32[4,64,128]{2,1,0:T(8,128)S(1)}, f32[4,64,128]{2,1,0:T(8,128)S(1)}, u32[]{:S(2)}, u32[]{:S(2)}) %collective-permute-start.7) | collective-permute-done | bytes 131104 | tf_op jit(solution)/shard_map/ppermute | solution.py:254
  175.4 17.0 %all-to-all-done.1 = f32[64,4,8,128]{3,2,1,0:T(8,128)} async-done(((f32[64,4,8,128]{3,2,1,0:T(8,128)}), f32[64,4,8,128]{3,2,1,0:T(8,128)}, u32[]{:S(2)}, u32[]{:S(2)}) %all-to-all-start.1) | async-done | bytes 1048608 | tf_op jit(solution)/shard_map/all_to_all | solution.py:251
  192.4 2.3 %shard_map.107 = f32[4,2,4,8,8,128]{5,4,3,2,1,0:T(8,128)} custom-call(s32[1]{0:T(128)} %bitcast.half, f32[4,8,2,4,8,128]{5,4,3,2,1,0:T(8,128)} %bitcast.8.blocks), custom_call_target="tpu_custom_call" | custom-call | bytes 2097152 | tf_op jit(solution)/shard_map/pallas_call | solution.py:230
  (25 shorter events, 2.8 us)
Async XLA Ops:
  0.6 3.1 %copy-start.7 = (f32[4,8192]{1,0:T(4,128)S(1)}, f32[4,8192]{1,0:T(4,128)}, u32[]{:S(2)}) copy-start(f32[4,8192]{1,0:T(4,128)} %param.11) | copy-start | bytes 393220
  3.7 23.3 %collective-permute-start = (f32[4,8192]{1,0:T(4,128)S(1)}, f32[4,8192]{1,0:T(4,128)S(1)}, u32[]{:S(2)}, u32[]{:S(2)}) collective-permute-start(f32[4,8192]{1,0:T(4,128)S(1)} %copy-done.7), channel_id=1, source_target_pairs={{0,78},{2,76},{4,74},{6,72},{8,70},{10,68},{12,66},{14,64},{64,14}... | collective-permute-start | bytes 393224 | tf_op jit(solution)/shard_map/ppermute | solution.py:254
  15.1 105.8 %all-to-all-start = ((f32[64,2,4,8,128]{4,3,2,1,0:T(8,128)}), f32[64,2,4,8,128]{4,3,2,1,0:T(8,128)S(1)}, u32[]{:S(2)}, u32[]{:S(2)}) async-start(f32[64,2,4,8,128]{4,3,2,1,0:T(8,128)} %bitcast.34), calls=%async_computation | async-start | bytes 4194304 | tf_op jit(solution)/shard_map/all_to_all | solution.py:251
  26.3 19.7 %copy-start = (bf16[768,256]{1,0:T(8,128)(2,1)S(1)}, bf16[768,256]{1,0:T(8,128)(2,1)}, u32[]{:S(2)}) copy-start(bf16[768,256]{1,0:T(8,128)(2,1)} %constant.27.clone.forward) | copy-start | bytes 1179652
  26.3 19.7 %copy-start.2 = (f32[2,72,128]{2,1,0:T(8,128)S(1)}, f32[2,72,128]{2,1,0:T(8,128)}, u32[]{:S(2)}) copy-start(f32[2,72,128]{2,1,0:T(8,128)} %constant.29.clone.turn) | copy-start | bytes 221188
  26.3 19.7 %copy-start.3 = (bf16[144,192]{1,0:T(8,128)(2,1)S(1)}, bf16[144,192]{1,0:T(8,128)(2,1)}, u32[]{:S(2)}) copy-start(bf16[144,192]{1,0:T(8,128)(2,1)} %constant.24.clone.first) | copy-start | bytes 165892
  27.1 11.5 %collective-permute-start.2 = (f32[8,64,128]{2,1,0:T(8,128)S(1)}, f32[8,64,128]{2,1,0:T(8,128)S(1)}, u32[]{:S(2)}, u32[]{:S(2)}) collective-permute-start(f32[8,64,128]{2,1,0:T(8,128)S(1)} %bitcast.38), channel_id=1, source_target_pairs={{0,256},{128,384},{256,0},{384,128},{1,257},{129,385},{257,1},{385... | collective-permute-start | bytes 786440 | tf_op jit(solution)/shard_map/ppermute | solution.py:257
  30.5 11.3 %collective-permute-start.1 = (f32[8,64,128]{2,1,0:T(8,128)S(1)}, f32[8,64,128]{2,1,0:T(8,128)S(1)}, u32[]{:S(2)}, u32[]{:S(2)}) collective-permute-start(f32[8,64,128]{2,1,0:T(8,128)S(1)} %bitcast.39), channel_id=1, source_target_pairs={{0,128},{128,256},{256,384},{384,0},{1,129},{129,257},{257,385},{3... | collective-permute-start | bytes 786440 | tf_op jit(solution)/shard_map/ppermute | solution.py:257
  34.5 10.5 %collective-permute-start.3 = (f32[8,64,128]{2,1,0:T(8,128)S(1)}, f32[8,64,128]{2,1,0:T(8,128)}, u32[]{:S(2)}, u32[]{:S(2)}) collective-permute-start(f32[8,64,128]{2,1,0:T(8,128)S(1)} %bitcast.40), channel_id=1, source_target_pairs={{0,384},{128,0},{256,128},{384,256},{1,385},{129,1},{257,129},{385... | collective-permute-start | bytes 786440 | tf_op jit(solution)/shard_map/ppermute | solution.py:257
  46.0 74.9 %copy-start.1 = (bf16[768,256]{1,0:T(8,128)(2,1)S(1)}, bf16[768,256]{1,0:T(8,128)(2,1)}, u32[]{:S(2)}) copy-start(bf16[768,256]{1,0:T(8,128)(2,1)} %constant.28.clone.inverse) | copy-start | bytes 1179652
  46.0 74.8 %copy-start.5 = (bf16[64,432]{1,0:T(8,128)(2,1)S(1)}, bf16[64,432]{1,0:T(8,128)(2,1)}, u32[]{:S(2)}) copy-start(bf16[64,432]{1,0:T(8,128)(2,1)} %constant.25.clone.last) | copy-start | bytes 165892
  48.4 1.4 copy-start.6
  120.9 17.7 %copy-start.4 = (bf16[64,432]{1,0:T(8,128)(2,1)S(1)}, bf16[64,432]{1,0:T(8,128)(2,1)}, u32[]{:S(2)}) copy-start(bf16[64,432]{1,0:T(8,128)(2,1)} %constant.26.clone.last) | copy-start | bytes 165892
  128.4 64.0 %all-to-all-start.1 = ((f32[64,4,8,128]{3,2,1,0:T(8,128)}), f32[64,4,8,128]{3,2,1,0:T(8,128)}, u32[]{:S(2)}, u32[]{:S(2)}) async-start(f32[64,4,8,128]{3,2,1,0:T(8,128)} %get-tuple-element.8), calls=%async_computation.1 | async-start | bytes 2097152 | tf_op jit(solution)/shard_map/all_to_all | solution.py:251
  145.4 12.6 %collective-permute-start.5 = (f32[8,64,128]{2,1,0:T(8,128)S(1)}, f32[8,64,128]{2,1,0:T(8,128)S(1)}, u32[]{:S(2)}, u32[]{:S(2)}) collective-permute-start(f32[8,64,128]{2,1,0:T(8,128)S(1)} %get-tuple-element.10), channel_id=1, source_target_pairs={{0,256},{128,384},{256,0},{384,128},{1,257},{129,385},{257,1},{385... | collective-permute-start | bytes 786440 | tf_op jit(solution)/shard_map/ppermute | solution.py:257
  148.7 13.9 %collective-permute-start.6 = (f32[8,64,128]{2,1,0:T(8,128)S(1)}, f32[8,64,128]{2,1,0:T(8,128)S(1)}, u32[]{:S(2)}, u32[]{:S(2)}) collective-permute-start(f32[8,64,128]{2,1,0:T(8,128)S(1)} %get-tuple-element.11), channel_id=1, source_target_pairs={{0,384},{128,0},{256,128},{384,256},{1,385},{129,1},{257,129},{385... | collective-permute-start | bytes 786440 | tf_op jit(solution)/shard_map/ppermute | solution.py:257
  150.6 12.0 %collective-permute-start.4 = (f32[8,64,128]{2,1,0:T(8,128)S(1)}, f32[8,64,128]{2,1,0:T(8,128)S(1)}, u32[]{:S(2)}, u32[]{:S(2)}) collective-permute-start(f32[8,64,128]{2,1,0:T(8,128)S(1)} %get-tuple-element.12), channel_id=1, source_target_pairs={{0,128},{128,256},{256,384},{384,0},{1,129},{129,257},{257,385},{3... | collective-permute-start | bytes 786440 | tf_op jit(solution)/shard_map/ppermute | solution.py:257
  162.7 11.9 %collective-permute-start.7 = (f32[4,64,128]{2,1,0:T(8,128)S(1)}, f32[4,64,128]{2,1,0:T(8,128)S(1)}, u32[]{:S(2)}, u32[]{:S(2)}) collective-permute-start(f32[4,64,128]{2,1,0:T(8,128)S(1)} %slice.29), channel_id=1, source_target_pairs={{0,78},{2,76},{4,74},{6,72},{8,70},{10,68},{12,66},{14,64},{64,14}... | collective-permute-start | bytes 393224 | tf_op jit(solution)/shard_map/ppermute | solution.py:254

commit v6 on v4

v6 whole, which is shorter than its diff:
```python
import math

import jax
import jax.numpy as jnp
import numpy as np
from jax import lax
from jax.experimental import pallas as pl
from jax.experimental.pallas import tpu as pltpu
from jax.sharding import Mesh
from jax.sharding import PartitionSpec as P

INNER = 128
HALF = 72


def three_parts(table, axis):
    high = np.asarray(table, np.float32).astype(jnp.bfloat16)
    low = (table - high.astype(np.float64)).astype(jnp.bfloat16)
    return jnp.asarray(np.concatenate([high, high, low], axis=axis))


def dft_tables(seq_length, norm):
    padded = 2 * seq_length
    outer = padded // INNER
    rows = seq_length // INNER
    freqs = outer // 2 + 1
    row, freq, inner = np.arange(rows), np.arange(freqs), np.arange(INNER)
    pad = ((0, HALF - freqs), (0, 0))
    angle = 2.0 * np.pi / outer * (freq[:, None] * row[None, :] % outer)
    cos_outer, sin_outer = np.pad(np.cos(angle), pad), np.pad(np.sin(angle), pad)
    weights = np.where((freq == 0) | (freq == freqs - 1), 1.0, 2.0)[:, None] / padded
    weights = np.pad(weights, pad)
    first = np.concatenate([cos_outer, -sin_outer], axis=0)
    last = np.concatenate([cos_outer * weights, -sin_outer * weights], axis=0).T
    angle = 2.0 * np.pi / INNER * (inner[:, None] * inner[None, :] % INNER)
    cos_inner, sin_inner = np.cos(angle), np.sin(angle)
    forward = np.block([[cos_inner, -sin_inner], [sin_inner, cos_inner]])
    inverse = np.block([[cos_inner, sin_inner], [-sin_inner, cos_inner]])
    angle = 2.0 * np.pi / padded * (freq[:, None] * inner[None, :] % padded)
    turn = np.stack([np.pad(np.cos(angle), pad), np.pad(np.sin(angle), pad)])
    left = dict(first=first, last=last, last_scaled=last * norm)
    right = dict(forward=forward, inverse=inverse)
    tables = {name: three_parts(t, 1) for name, t in left.items()}
    tables.update({name: three_parts(t, 0) for name, t in right.items()})
    tables["turn"] = jnp.asarray(turn, jnp.float32)
    return tables


def split(values):
    high = values.astype(jnp.bfloat16)
    return high, (values - high.astype(jnp.float32)).astype(jnp.bfloat16)


def dot(a, b):
    return jnp.dot(a, b, preferred_element_type=jnp.float32)


def forward_spectrum(wide, first, turn, forward):
    high, low = split(wide)
    outer = dot(first[...], jnp.concatenate([high, low, high], axis=0))
    cos, sin = turn[0], turn[1]
    turned = []
    for at in range(0, wide.shape[1], INNER):
        real, imag = outer[:HALF, at : at + INNER], outer[HALF:, at : at + INNER]
        turned.append(
            jnp.concatenate([real * cos + imag * sin, imag * cos - real * sin], axis=1)
        )
    high, low = split(jnp.concatenate(turned, axis=0))
    return dot(jnp.concatenate([high, low, high], axis=1), forward[...])


def correlate(spec, other):
    real, imag = spec[:, :INNER], spec[:, INNER:]
    other_real, other_imag = other[:, :INNER], other[:, INNER:]
    return jnp.concatenate(
        [real * other_real + imag * other_imag, imag * other_real - real * other_imag], axis=1
    )


def inverse_signal(spec, inverse, turn, last):
    high, low = split(spec)
    middle = dot(jnp.concatenate([high, low, high], axis=1), inverse[...])
    cos, sin = turn[0], turn[1]
    back = []
    for at in range(0, spec.shape[0], HALF):
        real, imag = middle[at : at + HALF, :INNER], middle[at : at + HALF, INNER:]
        back.append(
            jnp.concatenate([real * cos - imag * sin, imag * cos + real * sin], axis=0)
        )
    high, low = split(jnp.concatenate(back, axis=1))
    return dot(last[...], jnp.concatenate([high, low, high], axis=0))


def row(r, block):
    a, rows, _ = block.shape
    return pl.ds(r, a, stride=rows)


def rows_to_wide(block):
    a, rows, m = block.shape
    flat = block.reshape(a * rows, m)
    return jnp.concatenate([flat[row(r, block), :] for r in range(rows)], axis=1)


def filter_kernel(at, first, turn, forward, filters, spec):
    wide = jnp.concatenate([filters[r] for r in range(filters.shape[0])], axis=1)
    spec[...] = forward_spectrum(wide, first, turn, forward)


def input_grad_kernel(first, turn, forward, inverse, last, grad, filter_spec, spec, out):
    spec[...] = forward_spectrum(rows_to_wide(grad), first, turn, forward)
    wide = inverse_signal(correlate(spec[...], filter_spec[...]), inverse, turn, last)
    a, rows, m = out.shape
    flat = out.reshape(a * rows, m)
    for r in range(rows):
        flat[row(r, out), :] = wide[:, r * INNER : (r + 1) * INNER]


def filter_grad_kernel(first, turn, forward, inverse, last, tokens, grad_spec, out, total):
    spec = forward_spectrum(rows_to_wide(tokens), first, turn, forward)
    share = correlate(grad_spec[...], spec)
    seq = pl.program_id(1)

    @pl.when(seq == 0)
    def _():
        total[...] = share

    @pl.when(seq > 0)
    def _():
        total[...] += share

    @pl.when(seq == pl.num_programs(1) - 1)
    def _():
        wide = inverse_signal(total[...], inverse, turn, last)
        for r in range(out.shape[0]):
            out[r] = wide[:, r * INNER : (r + 1) * INNER]


def table_specs(tables, names):
    whole = lambda t: pl.BlockSpec(t.shape, lambda *_: (0,) * t.ndim)
    return [whole(tables[n]) for n in names], [tables[n] for n in names]


def cost(flops, size):
    return pl.CostEstimate(flops=flops, bytes_accessed=size, transcendentals=0)


LIMIT = pltpu.CompilerParams(vmem_limit_bytes=48 * 2**20)


def filter_spectrum(at_x, filters, tables):
    count, r, a, m = filters.shape
    specs, operands = table_specs(tables, ("first", "turn", "forward"))
    grid_spec = pltpu.PrefetchScalarGridSpec(
        num_scalar_prefetch=1,
        grid=(count,),
        in_specs=specs + [pl.BlockSpec((None, r, a, m), lambda i, at: (i, 0, 0, 0))],
        out_specs=pl.BlockSpec(
            (None, r * HALF, 2 * m), lambda i, at: ((at[0] - i) & (count - 1), 0, 0)
        ),
    )
    return pl.pallas_call(
        filter_kernel,
        grid_spec=grid_spec,
        out_shape=jax.ShapeDtypeStruct((count, r * HALF, 2 * m), jnp.float32),
        cost_estimate=cost(10**9, 8 * filters.size),
        compiler_params=LIMIT,
    )(at_x, *operands, filters)


def input_grad_part(both, filter_spec, tables):
    seqs, a, _, pairs, r, m = both.shape
    names = ("first", "turn", "forward", "inverse", "last")
    specs, operands = table_specs(tables, names)
    spec_shape = (None, r * HALF, 2 * m)
    return pl.pallas_call(
        input_grad_kernel,
        grid=(pairs, seqs),
        in_specs=specs
        + [
            pl.BlockSpec((None, a, None, None, r, m), lambda p, q: (q, 0, 0, p, 0, 0)),
            pl.BlockSpec(spec_shape, lambda p, q: (p, 0, 0)),
        ],
        out_specs=[
            pl.BlockSpec((None, *spec_shape), lambda p, q: (q, p, 0, 0)),
            pl.BlockSpec((None, a, None, r, m), lambda p, q: (q, 0, p, 0, 0)),
        ],
        out_shape=[
            jax.ShapeDtypeStruct((seqs, pairs, r * HALF, 2 * m), jnp.float32),
            jax.ShapeDtypeStruct((seqs, a, pairs, r, m), jnp.float32),
        ],
        cost_estimate=cost(2 * 10**9, 8 * both.size),
        compiler_params=LIMIT,
    )(*operands, both, filter_spec)


def filter_grad_part(both, grad_spec, tables):
    seqs, a, _, pairs, r, m = both.shape
    names = ("first", "turn", "forward", "inverse", "last_scaled")
    specs, operands = table_specs(tables, names)
    return pl.pallas_call(
        filter_grad_kernel,
        grid=(pairs, seqs),
        in_specs=specs
        + [
            pl.BlockSpec((None, a, None, None, r, m), lambda p, q: (q, 0, 1, p, 0, 0)),
            pl.BlockSpec((None, None, r * HALF, 2 * m), lambda p, q: (q, p, 0, 0)),
        ],
        out_specs=pl.BlockSpec((None, r, a, m), lambda p, q: (p, 0, 0, 0)),
        out_shape=jax.ShapeDtypeStruct((pairs, r, a, m), jnp.float32),
        scratch_shapes=[pltpu.VMEM((r * HALF, 2 * m), jnp.float32)],
        cost_estimate=cost(0, 0),
        compiler_params=LIMIT,
    )(*operands, both, grad_spec)


def pack_kernel(grad, tokens, blocks):
    x, h, y, z, rows, lanes = tokens.shape
    j = rows // 2
    for g in range(h):
        for i in range(y):
            for k in range(z):
                for n, array in enumerate((grad, tokens)):
                    tiles = array[:, g, i, k].reshape(x // 2, 2, rows, lanes)
                    low, high = tiles[:, 0], tiles[:, 1]
                    blocks[g, i, k, 0, n] = jnp.concatenate([low[:, :j], high[:, :j]], axis=1)
                    blocks[g, i, k, 1, n] = jnp.concatenate([low[:, j:], high[:, j:]], axis=1)


def unpack_kernel(blocks, tokens):
    x, h, y, z, rows, lanes = tokens.shape
    j = rows // 2
    for g in range(h):
        for i in range(y):
            for k in range(z):
                low, high = blocks[g, i, k, 0], blocks[g, i, k, 1]
                even = jnp.concatenate([low[:, :j], high[:, :j]], axis=1)
                odd = jnp.concatenate([low[:, j:], high[:, j:]], axis=1)
                tokens[:, g, i, k] = jnp.stack([even, odd], axis=1).reshape(x, rows, lanes)


def moving(kernel, arrays, shape):
    whole = pl.BlockSpec(memory_space=pltpu.VMEM)
    return pl.pallas_call(
        kernel,
        out_shape=jax.ShapeDtypeStruct(shape, jnp.float32),
        in_specs=[whole] * len(arrays),
        out_specs=whole,
        cost_estimate=cost(0, 8 * math.prod(shape)),
    )(*arrays)


def shards(inputs, grad_out, filters):
    x, h, y, z, c = (lax.axis_size(a) for a in ("x", "zh", "y", "zl", "c"))
    _, channels, block = inputs.shape
    j = channels // (x * h * y * z * c)
    seq_length = filters.shape[1]
    rows = y * z * c
    pairs = x // 2
    tables = dft_tables(seq_length, 1.0 / math.sqrt(x * h * seq_length))
    at_x = lax.axis_index("x").reshape(1).astype(jnp.int32)
    whole_shape = (x, h, y, z, c * j, INNER)

    def exchange(blocks):
        return lax.all_to_all(blocks, ("zh", "y", "zl", "c"), 0, 0, tiled=True)

    def along_x(v, s):
        return lax.ppermute(v, "x", [(i, (i + s) % x) for i in range(x)])

    both = moving(
        pack_kernel,
        [grad_out.reshape(whole_shape), inputs.reshape(whole_shape)],
        (h, y, z, c, 2, pairs, 2 * j, INNER),
    )
    both = exchange(both.reshape(h * rows, 2, pairs, 2 * j, INNER))
    both = both.reshape(h, rows, 2, pairs, 2 * j, INNER)

    own = filters.reshape(j, rows, INNER)
    taps = jnp.stack([own] + [along_x(own, s) for s in range(1, x)])
    filter_spec = filter_spectrum(at_x, taps, tables).reshape(pairs, 2 * j * HALF, 2 * INNER)

    grad_spec, leaving = input_grad_part(both, filter_spec, tables)
    returned = exchange(leaving.reshape(h * rows, pairs, 2 * j, INNER))

    parts = filter_grad_part(both, grad_spec, tables).reshape(x, j, rows, INNER)
    share = [
        lax.dynamic_index_in_dim(parts, (at_x[0] + s) % x, 0, keepdims=False) for s in range(x)
    ]
    filter_grad = share[0] + sum(along_x(share[s], s) for s in range(1, x))

    blocks = returned.reshape(h, y, z, c, pairs, 2 * j, INNER)
    input_grad = moving(unpack_kernel, [blocks], whole_shape)
    return (input_grad.reshape(1, channels, block), filter_grad.reshape(j, seq_length))


def solution(mesh):
    devices = mesh.devices.reshape(4, 2, 4, -1, 2)
    fine = Mesh(devices, ("x", "zh", "y", "zl", "c"))
    tokens = P(("x", "zh"), None, ("y", "zl", "c"))
    owners = P(("x", "zh", "y", "zl", "c"), None)
    return jax.shard_map(
        shards,
        mesh=fine,
        in_specs=(tokens, tokens, owners),
        out_specs=(tokens, owners),
        check_vma=False,
    )
```

time: 195 us -> 199 us (1.021)
  waiting for transfers between devices: 112 us -> 126 us
  starting transfers between devices: 56.4 us -> 47.2 us
  Pallas kernels: 21.9 us -> 18 us
  local copies, waits for them, and re-layouts: 2.33 us -> 5.61 us
    all_to_all x2, waiting for transfers between devices: 88.3 us -> 116 us  [exchange(): return lax.all_to_all(blocks, ('zh', 'y', 'zl', 'c'), 0, 0, tiled=True)]
    ppermute x2 -> x0, starting transfers between devices: 15.4 us -> none  [facing(): lax.ppermute(v, ('zh', 'zl'), [(i, h * z - 1 - i) for i in range(h * z)])]
    ppermute x2 -> x0, waiting for transfers between devices: 7.93 us -> none  [facing(): lax.ppermute(v, ('zh', 'zl'), [(i, h * z - 1 - i) for i in range(h * z)])]
    all_to_all x2, starting transfers between devices: 21.4 us -> 28.3 us  [exchange(): return lax.all_to_all(blocks, ('zh', 'y', 'zl', 'c'), 0, 0, tiled=True)]
    ppermute x6, waiting for transfers between devices: 15.8 us -> 10.1 us  [along_x(): return lax.ppermute(v, 'x', [(i, (i + s) % x) for i in range(x)])]
    pallas_call x3, Pallas kernels: 16.7 us -> 12.7 us  [the longest x1 6.49 us: input_grad_part(): pl.pallas_call(input_grad_kernel, grid=(pairs, seqs), in_specs=specs + [p...]
    unnamed x18 -> x22, local copies, waits for them, and re-layouts: 2.26 us -> 5.57 us
  transfers between devices with their start and end apart: 10 -> 8, of which waited for: 8 -> 6; matrix products, arithmetic and copies ran while one was open for 1% -> 0% of each run, Pallas kernels for 6% -> 3%
where the time goes in v6:
time: 199 us; the launch traced here: 198 us
  waiting for transfers between devices  126 us (63%)
  starting transfers between devices  47.2 us (24%)
  Pallas kernels  18 us (9%)
  local copies, waits for them, and re-layouts  5.61 us (3%)
    all_to_all x2, waiting for transfers between devices, exchange(): return lax.all_to_all(blocks, ('zh', 'y', 'zl', 'c'), 0, 0, tiled=True)  116 us
    all_to_all x2, starting transfers between devices, exchange(): return lax.all_to_all(blocks, ('zh', 'y', 'zl', 'c'), 0, 0, tiled=True)  28.3 us
    ppermute x6, starting transfers between devices, along_x(): return lax.ppermute(v, 'x', [(i, (i + s) % x) for i in range(x)])  18.9 us
    ppermute x6, waiting for transfers between devices, along_x(): return lax.ppermute(v, 'x', [(i, (i + s) % x) for i in range(x)])  10.1 us
    pallas_call x1, Pallas kernels, input_grad_part(): pl.pallas_call(input_grad_kernel, grid=(pairs, seqs), in_specs=specs + [p...  6.49 us
    unnamed x22, local copies, waits for them, and re-layouts  5.57 us
    pallas_call x2, Pallas kernels, moving(): pl.pallas_call(kernel, out_shape=jax.ShapeDtypeStruct(shape, jnp.float32)...  5.28 us
    pallas_call x1, Pallas kernels, filter_grad_part(): pl.pallas_call(filter_grad_kernel, grid=(pairs, seqs), in_specs=specs + [...  4.41 us
  transfers between devices with their start and end apart: 8, of which 6 were waited for; matrix products, arithmetic and copies ran while one was open for 0% of the time, Pallas kernels for 3%

profile of v6, /device:TPU:6, one launch (start us, length us, event | category | flops | bytes accessed | tf_op | source)
XLA Modules:
  0.0 197.9 jit_solution(135293858904313831)
XLA Ops:
  0.6 3.0 %shard_map.104 = f32[2,4,8,2,2,2,8,128]{7,6,5,4,3,2,1,0:T(8,128)} custom-call(f32[4,2,4,8,8,128]{5,4,3,2,1,0:T(8,128)} %bitcast.43, f32[4,2,4,8,8,128]{5,4,3,2,1,0:T(8,128)} %bitcast.44), custom_call_target="tpu_custom_call" | custom-call | bytes 4194304 | tf_op jit(solution)/shard_map/pallas_call | solution.py:244
  3.7 20.1 %all-to-all-start = ((f32[128,2,2,8,128]{4,3,2,1,0:T(8,128)}), f32[128,2,2,8,128]{4,3,2,1,0:T(8,128)S(1)}, u32[]{:S(2)}, u32[]{:S(2)}) async-start(f32[128,2,2,8,128]{4,3,2,1,0:T(8,128)} %bitcast.41), calls=%async_computation | async-start | bytes 4194304 | tf_op jit(solution)/shard_map/all_to_all | solution.py:265
  23.8 2.7 %collective-permute-start.2 = (f32[4,64,128]{2,1,0:T(8,128)S(1)}, f32[4,64,128]{2,1,0:T(8,128)S(1)}, u32[]{:S(2)}, u32[]{:S(2)}) collective-permute-start(f32[4,64,128]{2,1,0:T(8,128)S(1)} %bitcast.45), channel_id=1, source_target_pairs={{0,384},{128,0},{256,128},{384,256},{1,385},{129,1},{257,129},{385... | collective-permute-start | bytes 393224 | tf_op jit(solution)/shard_map/ppermute | solution.py:268
  26.5 3.0 %collective-permute-start.1 = (f32[4,64,128]{2,1,0:T(8,128)S(1)}, f32[4,64,128]{2,1,0:T(8,128)S(1)}, u32[]{:S(2)}, u32[]{:S(2)}) collective-permute-start(f32[4,64,128]{2,1,0:T(8,128)S(1)} %bitcast.46), channel_id=1, source_target_pairs={{0,256},{128,384},{256,0},{384,128},{1,257},{129,385},{257,1},{385... | collective-permute-start | bytes 393224 | tf_op jit(solution)/shard_map/ppermute | solution.py:268
  29.6 4.0 %collective-permute-start = (f32[4,64,128]{2,1,0:T(8,128)S(1)}, f32[4,64,128]{2,1,0:T(8,128)S(1)}, u32[]{:S(2)}, u32[]{:S(2)}) collective-permute-start(f32[4,64,128]{2,1,0:T(8,128)S(1)} %bitcast.47), channel_id=1, source_target_pairs={{0,128},{128,256},{256,384},{384,0},{1,129},{129,257},{257,385},{3... | collective-permute-start | bytes 393224 | tf_op jit(solution)/shard_map/ppermute | solution.py:268
  33.6 1.3 collective-permute-done.1
  34.9 2.5 %collective-permute-done = f32[4,64,128]{2,1,0:T(8,128)S(1)} collective-permute-done((f32[4,64,128]{2,1,0:T(8,128)S(1)}, f32[4,64,128]{2,1,0:T(8,128)S(1)}, u32[]{:S(2)}, u32[]{:S(2)}) %collective-permute-start) | collective-permute-done | bytes 131104 | tf_op jit(solution)/shard_map/ppermute | solution.py:268
  37.5 1.8 shard_map.105
  39.4 1.0 copy-done.6
  40.4 82.9 %all-to-all-done = f32[128,2,2,8,128]{4,3,2,1,0:T(8,128)S(1)} async-done(((f32[128,2,2,8,128]{4,3,2,1,0:T(8,128)}), f32[128,2,2,8,128]{4,3,2,1,0:T(8,128)S(1)}, u32[]{:S(2)}, u32[]{:S(2)}) %all-to-all-start) | async-done | bytes 2097184 | tf_op jit(solution)/shard_map/all_to_all | solution.py:265
  123.3 1.3 copy-done.7
  124.6 6.5 %shard_map.106 = (f32[2,2,576,256]{3,2,1,0:T(8,128)}, f32[2,64,2,8,128]{4,3,2,1,0:T(8,128)}) custom-call(bf16[144,192]{1,0:T(8,128)(2,1)S(1)} %copy-done.3, f32[2,72,128]{2,1,0:T(8,128)S(1)} %copy-done.4, bf16[768,256]{1,0:T(8,128)(2,1)S(1)} %copy-done.1, bf16[768,256]{1,0:T(8,128)(2,1)S(1)} %copy-done.2, bf16[64,432]{1,0:T(8,128)(2,1)S(1)} %copy-done.8, ...), custom_call_target="tpu_custom_call" | custom-call | flops 2000000000 | bytes 4194304 | tf_op jit(solution)/shard_map/pallas_call | solution.py:176
  131.1 8.2 %all-to-all-start.1 = ((f32[128,2,8,128]{3,2,1,0:T(8,128)}), f32[128,2,8,128]{3,2,1,0:T(8,128)}, u32[]{:S(2)}, u32[]{:S(2)}) async-start(f32[128,2,8,128]{3,2,1,0:T(8,128)} %bitcast.9), calls=%async_computation.1 | async-start | bytes 2097152 | tf_op jit(solution)/shard_map/all_to_all | solution.py:265
  139.3 1.7 copy-done
  141.0 0.8 copy-done.5
  141.8 4.4 %shard_map.108 = f32[2,8,64,128]{3,2,1,0:T(8,128)S(1)} custom-call(bf16[144,192]{1,0:T(8,128)(2,1)S(1)} %copy-done.3, f32[2,72,128]{2,1,0:T(8,128)S(1)} %copy-done.4, bf16[768,256]{1,0:T(8,128)(2,1)S(1)} %copy-done.1, bf16[768,256]{1,0:T(8,128)(2,1)S(1)} %copy-done.2, bf16[64,432]{1,0:T(8,128)(2,1)S(1)} %copy-done.5, f32[2,64,2,2,8,128]{5,4,3,2,1,0:T(8,128)S(1)} %bitcast.37, ...), custom_call_target="tpu_custom_call" | custom-call | tf_op jit(solution)/shard_map/pallas_call | solution.py:201
  146.3 2.7 %collective-permute-start.5 = (f32[4,64,128]{2,1,0:T(8,128)S(1)}, f32[4,64,128]{2,1,0:T(8,128)S(1)}, u32[]{:S(2)}, u32[]{:S(2)}) collective-permute-start(f32[4,64,128]{2,1,0:T(8,128)S(1)} %get-tuple-element.7), channel_id=1, source_target_pairs={{0,384},{128,0},{256,128},{384,256},{1,385},{129,1},{257,129},{385... | collective-permute-start | bytes 393224 | tf_op jit(solution)/shard_map/ppermute | solution.py:268
  149.0 4.3 %collective-permute-start.3 = (f32[4,64,128]{2,1,0:T(8,128)S(1)}, f32[4,64,128]{2,1,0:T(8,128)S(1)}, u32[]{:S(2)}, u32[]{:S(2)}) collective-permute-start(f32[4,64,128]{2,1,0:T(8,128)S(1)} %get-tuple-element.8), channel_id=1, source_target_pairs={{0,128},{128,256},{256,384},{384,0},{1,129},{129,257},{257,385},{3... | collective-permute-start | bytes 393224 | tf_op jit(solution)/shard_map/ppermute | solution.py:268
  153.3 2.1 %collective-permute-start.4 = (f32[4,64,128]{2,1,0:T(8,128)S(1)}, f32[4,64,128]{2,1,0:T(8,128)S(1)}, u32[]{:S(2)}, u32[]{:S(2)}) collective-permute-start(f32[4,64,128]{2,1,0:T(8,128)S(1)} %get-tuple-element.6), channel_id=1, source_target_pairs={{0,256},{128,384},{256,0},{384,128},{1,257},{129,385},{257,1},{385... | collective-permute-start | bytes 393224 | tf_op jit(solution)/shard_map/ppermute | solution.py:268
  155.5 3.2 %collective-permute-done.3 = f32[4,64,128]{2,1,0:T(8,128)S(1)} collective-permute-done((f32[4,64,128]{2,1,0:T(8,128)S(1)}, f32[4,64,128]{2,1,0:T(8,128)S(1)}, u32[]{:S(2)}, u32[]{:S(2)}) %collective-permute-start.3) | collective-permute-done | bytes 131104 | tf_op jit(solution)/shard_map/ppermute | solution.py:268
  158.7 3.1 %collective-permute-done.4 = f32[4,64,128]{2,1,0:T(8,128)S(1)} collective-permute-done((f32[4,64,128]{2,1,0:T(8,128)S(1)}, f32[4,64,128]{2,1,0:T(8,128)S(1)}, u32[]{:S(2)}, u32[]{:S(2)}) %collective-permute-start.4) | collective-permute-done | bytes 131104 | tf_op jit(solution)/shard_map/ppermute | solution.py:268
  161.7 0.7 copy.17
  162.5 33.1 %all-to-all-done.1 = f32[128,2,8,128]{3,2,1,0:T(8,128)} async-done(((f32[128,2,8,128]{3,2,1,0:T(8,128)}), f32[128,2,8,128]{3,2,1,0:T(8,128)}, u32[]{:S(2)}, u32[]{:S(2)}) %all-to-all-start.1) | async-done | bytes 1048608 | tf_op jit(solution)/shard_map/all_to_all | solution.py:265
  195.6 2.3 %shard_map.107 = f32[4,2,4,8,8,128]{5,4,3,2,1,0:T(8,128)} custom-call(f32[2,4,8,2,2,8,128]{6,5,4,3,2,1,0:T(8,128)} %bitcast.10.blocks), custom_call_target="tpu_custom_call" | custom-call | bytes 2097152 | tf_op jit(solution)/shard_map/pallas_call | solution.py:244
  (22 shorter events, 0.2 us)
Async XLA Ops:
  3.6 20.1 %copy-start.9 = (f32[4,8192]{1,0:T(4,128)S(1)}, f32[4,8192]{1,0:T(4,128)}, u32[]{:S(2)}) copy-start(f32[4,8192]{1,0:T(4,128)} %param.11) | copy-start | bytes 393220
  3.6 33.9 %copy-start.1 = (bf16[768,256]{1,0:T(8,128)(2,1)S(1)}, bf16[768,256]{1,0:T(8,128)(2,1)}, u32[]{:S(2)}) copy-start(bf16[768,256]{1,0:T(8,128)(2,1)} %constant.61.clone.forward) | copy-start | bytes 1179652
  3.6 33.9 %copy-start.3 = (bf16[144,192]{1,0:T(8,128)(2,1)S(1)}, bf16[144,192]{1,0:T(8,128)(2,1)}, u32[]{:S(2)}) copy-start(bf16[144,192]{1,0:T(8,128)(2,1)} %constant.58.clone.first) | copy-start | bytes 165892
  3.6 33.9 %copy-start.4 = (f32[2,72,128]{2,1,0:T(8,128)S(1)}, f32[2,72,128]{2,1,0:T(8,128)}, u32[]{:S(2)}) copy-start(f32[2,72,128]{2,1,0:T(8,128)} %constant.63.clone.turn) | copy-start | bytes 221188
  3.7 119.6 %all-to-all-start = ((f32[128,2,2,8,128]{4,3,2,1,0:T(8,128)}), f32[128,2,2,8,128]{4,3,2,1,0:T(8,128)S(1)}, u32[]{:S(2)}, u32[]{:S(2)}) async-start(f32[128,2,2,8,128]{4,3,2,1,0:T(8,128)} %bitcast.41), calls=%async_computation | async-start | bytes 4194304 | tf_op jit(solution)/shard_map/all_to_all | solution.py:265
  23.8 9.8 %collective-permute-start.2 = (f32[4,64,128]{2,1,0:T(8,128)S(1)}, f32[4,64,128]{2,1,0:T(8,128)S(1)}, u32[]{:S(2)}, u32[]{:S(2)}) collective-permute-start(f32[4,64,128]{2,1,0:T(8,128)S(1)} %bitcast.45), channel_id=1, source_target_pairs={{0,384},{128,0},{256,128},{384,256},{1,385},{129,1},{257,129},{385... | collective-permute-start | bytes 393224 | tf_op jit(solution)/shard_map/ppermute | solution.py:268
  26.5 8.4 %collective-permute-start.1 = (f32[4,64,128]{2,1,0:T(8,128)S(1)}, f32[4,64,128]{2,1,0:T(8,128)S(1)}, u32[]{:S(2)}, u32[]{:S(2)}) collective-permute-start(f32[4,64,128]{2,1,0:T(8,128)S(1)} %bitcast.46), channel_id=1, source_target_pairs={{0,256},{128,384},{256,0},{384,128},{1,257},{129,385},{257,1},{385... | collective-permute-start | bytes 393224 | tf_op jit(solution)/shard_map/ppermute | solution.py:268
  29.6 7.9 %collective-permute-start = (f32[4,64,128]{2,1,0:T(8,128)S(1)}, f32[4,64,128]{2,1,0:T(8,128)S(1)}, u32[]{:S(2)}, u32[]{:S(2)}) collective-permute-start(f32[4,64,128]{2,1,0:T(8,128)S(1)} %bitcast.47), channel_id=1, source_target_pairs={{0,128},{128,256},{256,384},{384,0},{1,129},{129,257},{257,385},{3... | collective-permute-start | bytes 393224 | tf_op jit(solution)/shard_map/ppermute | solution.py:268
  37.5 85.8 %copy-start.2 = (bf16[768,256]{1,0:T(8,128)(2,1)S(1)}, bf16[768,256]{1,0:T(8,128)(2,1)}, u32[]{:S(2)}) copy-start(bf16[768,256]{1,0:T(8,128)(2,1)} %constant.62.clone.inverse) | copy-start | bytes 1179652
  37.5 85.8 %copy-start.8 = (bf16[64,432]{1,0:T(8,128)(2,1)S(1)}, bf16[64,432]{1,0:T(8,128)(2,1)}, u32[]{:S(2)}) copy-start(bf16[64,432]{1,0:T(8,128)(2,1)} %constant.59.clone.last) | copy-start | bytes 165892
  39.3 1.0 copy-start.6
  123.3 1.3 copy-start.7
  131.1 64.6 %all-to-all-start.1 = ((f32[128,2,8,128]{3,2,1,0:T(8,128)}), f32[128,2,8,128]{3,2,1,0:T(8,128)}, u32[]{:S(2)}, u32[]{:S(2)}) async-start(f32[128,2,8,128]{3,2,1,0:T(8,128)} %bitcast.9), calls=%async_computation.1 | async-start | bytes 2097152 | tf_op jit(solution)/shard_map/all_to_all | solution.py:265
  139.3 1.7 copy-start
  141.0 0.8 copy-start.5
  146.3 9.2 %collective-permute-start.5 = (f32[4,64,128]{2,1,0:T(8,128)S(1)}, f32[4,64,128]{2,1,0:T(8,128)S(1)}, u32[]{:S(2)}, u32[]{:S(2)}) collective-permute-start(f32[4,64,128]{2,1,0:T(8,128)S(1)} %get-tuple-element.7), channel_id=1, source_target_pairs={{0,384},{128,0},{256,128},{384,256},{1,385},{129,1},{257,129},{385... | collective-permute-start | bytes 393224 | tf_op jit(solution)/shard_map/ppermute | solution.py:268
  149.0 9.6 %collective-permute-start.3 = (f32[4,64,128]{2,1,0:T(8,128)S(1)}, f32[4,64,128]{2,1,0:T(8,128)S(1)}, u32[]{:S(2)}, u32[]{:S(2)}) collective-permute-start(f32[4,64,128]{2,1,0:T(8,128)S(1)} %get-tuple-element.8), channel_id=1, source_target_pairs={{0,128},{128,256},{256,384},{384,0},{1,129},{129,257},{257,385},{3... | collective-permute-start | bytes 393224 | tf_op jit(solution)/shard_map/ppermute | solution.py:268
  153.3 8.4 %collective-permute-start.4 = (f32[4,64,128]{2,1,0:T(8,128)S(1)}, f32[4,64,128]{2,1,0:T(8,128)S(1)}, u32[]{:S(2)}, u32[]{:S(2)}) collective-permute-start(f32[4,64,128]{2,1,0:T(8,128)S(1)} %get-tuple-element.6), channel_id=1, source_target_pairs={{0,256},{128,384},{256,0},{384,128},{1,257},{129,385},{257,1},{385... | collective-permute-start | bytes 393224 | tf_op jit(solution)/shard_map/ppermute | solution.py:268

commit v7 on v5

--- a/solution.py
+++ b/solution.py
@@ -144,7 +144,7 @@
         out_shape=jax.ShapeDtypeStruct((count, r * HALF, 2 * m), jnp.float32),
         in_specs=specs + [pl.BlockSpec((None, r, a, m), lambda i: (i, 0, 0, 0))],
         out_specs=pl.BlockSpec((None, r * HALF, 2 * m), lambda i: (i, 0, 0)),
-        cost_estimate=cost(83 * 10**9, 8 * filters.size),
+        cost_estimate=cost(10**9, 8 * filters.size),
         compiler_params=LIMIT,
     )(*operands, filters)
 
@@ -204,36 +204,88 @@
     )(at_x, *operands, both, grad_spec)
 
 
-def pack_kernel(half, grad, tokens, blocks):
+def in_parts(incoming, work, outgoing):
+    for copies in incoming:
+        for copy in copies:
+            copy.start()
+    for i, copies in enumerate(incoming):
+        for copy in copies:
+            copy.wait()
+        work(i)
+        outgoing[i].start()
+    for copy in outgoing:
+        copy.wait()
+
+
+def pack_kernel(half, grad, tokens, blocks, arrived, leaving, in_sems, out_sems):
     _, _, y, z, rows, _ = tokens.shape
     own, far, j = half[0], 1 - half[0], rows // 2
-    for i in range(y):
+    arrays = (grad, tokens)
+    incoming = [
+        [
+            pltpu.make_async_copy(array.at[:, :, i], arrived.at[i, n], in_sems.at[i, n])
+            for n, array in enumerate(arrays)
+        ]
+        for i in range(y)
+    ]
+    outgoing = [
+        pltpu.make_async_copy(leaving.at[i], blocks.at[i], out_sems.at[i]) for i in range(y)
+    ]
+
+    def work(i):
         for k in range(z):
-            for n, array in enumerate((grad, tokens)):
-                near, other = array[:, own, i, k], array[:, far, i, z - 1 - k]
-                blocks[i, k, 0, n] = jnp.concatenate([near[:, :j], other[:, :j]], axis=1)
-                blocks[i, k, 1, n] = jnp.concatenate([near[:, j:], other[:, j:]], axis=1)
-
-
-def unpack_kernel(half, blocks, tokens):
-    _, _, y, z, rows, _ = tokens.shape
+            for n in range(len(arrays)):
+                near, other = arrived[i, n, :, own, k], arrived[i, n, :, far, k ^ (z // 2)]
+                leaving[i, k, 0, n] = jnp.concatenate([near[:, :j], other[:, :j]], axis=1)
+                leaving[i, k, 1, n] = jnp.concatenate([near[:, j:], other[:, j:]], axis=1)
+
+    in_parts(incoming, work, outgoing)
+
+
+def unpack_kernel(half, blocks, tokens, arrived, leaving, in_sems, out_sems):
+    y, z, _, _, rows, _ = blocks.shape
     own, far, j = half[0], 1 - half[0], rows // 2
-    for i in range(y):
+    incoming = [
+        [pltpu.make_async_copy(blocks.at[i], arrived.at[i], in_sems.at[i])] for i in range(y)
+    ]
+    outgoing = [
+        pltpu.make_async_copy(leaving.at[i], tokens.at[:, :, i], out_sems.at[i])
+        for i in range(y)
+    ]
+
+    def work(i):
         for k in range(z):
-            low, high = blocks[i, k, 0], blocks[i, k, 1]
-            tokens[:, own, i, k] = jnp.concatenate([low[:, :j], high[:, :j]], axis=1)
-            tokens[:, far, i, z - 1 - k] = jnp.concatenate([low[:, j:], high[:, j:]], axis=1)
-
-
-def moving(kernel, half, arrays, shape):
-    whole = pl.BlockSpec(memory_space=pltpu.VMEM)
+            low, high = arrived[i, k, 0], arrived[i, k, 1]
+            leaving[i, :, own, k] = jnp.concatenate([low[:, :j], high[:, :j]], axis=1)
+            leaving[i, :, far, k ^ (z // 2)] = jnp.concatenate([low[:, j:], high[:, j:]], axis=1)
+
+    in_parts(incoming, work, outgoing)
+
+
+def moving(kernel, half, arrays, shape, scratch, sems):
+    anywhere = pl.BlockSpec(memory_space=pl.ANY)
     return pl.pallas_call(
         kernel,
         out_shape=jax.ShapeDtypeStruct(shape, jnp.float32),
-        in_specs=[pl.BlockSpec(memory_space=pltpu.SMEM)] + [whole] * len(arrays),
-        out_specs=whole,
+        in_specs=[pl.BlockSpec(memory_space=pltpu.SMEM)] + [anywhere] * len(arrays),
+        out_specs=anywhere,
+        scratch_shapes=[pltpu.VMEM(v, jnp.float32) for v in scratch]
+        + [pltpu.SemaphoreType.DMA(v) for v in sems],
         cost_estimate=cost(0, 8 * math.prod(shape)),
     )(half, *arrays)
+
+
+def pack(half, grad, tokens):
+    x, h, y, z, rows, lanes = grad.shape
+    shape = (y, z, 2, 2, x, rows, lanes)
+    scratch = [(y, 2, x, h, z, rows, lanes), shape]
+    return moving(pack_kernel, half, [grad, tokens], shape, scratch, [(y, 2), (y,)])
+
+
+def unpack(half, blocks, shape):
+    x, h, y, z, rows, lanes = shape
+    scratch = [blocks.shape, (y, x, h, z, rows, lanes)]
+    return moving(unpack_kernel, half, [blocks], shape, scratch, [(y,), (y,)])
 
 
 def shards(inputs, grad_out, filters):
@@ -251,17 +303,12 @@
         return lax.all_to_all(blocks, ("y", "zl", "c"), 0, 0, tiled=True)
 
     def facing(v):
-        return lax.ppermute(v, ("zh", "zl"), [(i, h * z - 1 - i) for i in range(h * z)])
+        return lax.ppermute(v, ("zh", "zl"), [(i, i ^ z ^ (z // 2)) for i in range(h * z)])
 
     def along_x(v, s):
         return lax.ppermute(v, "x", [(i, (i + s) % x) for i in range(x)])
 
-    both = moving(
-        pack_kernel,
-        half,
-        [grad_out.reshape(whole_shape), inputs.reshape(whole_shape)],
-        (y, z, c, 2, x, h * j, INNER),
-    )
+    both = pack(half, grad_out.reshape(whole_shape), inputs.reshape(whole_shape))
     both, filters = lax.optimization_barrier((both, filters))
     both = exchange(both.reshape(rows, 2, x, h * j, INNER))
 
@@ -277,7 +324,7 @@
     filter_grad = part[:j] + facing(part[j:])
 
     blocks = returned.reshape(y, z, c, x, h * j, INNER)
-    input_grad = moving(unpack_kernel, half, [blocks], whole_shape)
+    input_grad = unpack(half, blocks, whole_shape)
     return (input_grad.reshape(1, channels, block), filter_grad.reshape(j, seq_length))
 
 

time: 195 us -> 198 us (1.015)
  waiting for transfers between devices: 112 us -> 116 us
    ppermute x2, waiting for transfers between devices: 8.6 us -> 96.2 us  [facing(): lax.ppermute(v, ('zh', 'zl'), [(i, i ^ z ^ z // 2) for i in range(h * z)])]
    all_to_all x2, waiting for transfers between devices: 88.1 us -> 3.36 us  [exchange(): return lax.all_to_all(blocks, ('y', 'zl', 'c'), 0, 0, tiled=True)]
  transfers between devices with their start and end apart: 10 -> 10, of which waited for: 9 -> 8; matrix products, arithmetic and copies ran while one was open for 1% -> 1% of each run, Pallas kernels for 5% -> 5%
where the time goes in v7:
time: 198 us; the launch traced here: 197 us
  waiting for transfers between devices  116 us (59%)
  starting transfers between devices  55.6 us (28%)
  Pallas kernels  21.2 us (11%)
  local copies, waits for them, and re-layouts  2.33 us (1%)
    ppermute x2, waiting for transfers between devices, facing(): lax.ppermute(v, ('zh', 'zl'), [(i, i ^ z ^ z // 2) for i in range(h * z)])  96.2 us
    all_to_all x2, starting transfers between devices, exchange(): return lax.all_to_all(blocks, ('y', 'zl', 'c'), 0, 0, tiled=True)  21.8 us
    ppermute x6, starting transfers between devices, along_x(): return lax.ppermute(v, 'x', [(i, (i + s) % x) for i in range(x)])  18.7 us
    ppermute x6, waiting for transfers between devices, along_x(): return lax.ppermute(v, 'x', [(i, (i + s) % x) for i in range(x)])  16.4 us
    ppermute x2, starting transfers between devices, facing(): lax.ppermute(v, ('zh', 'zl'), [(i, i ^ z ^ z // 2) for i in range(h * z)])  15 us
    pallas_call x1, Pallas kernels, input_grad_part(): pl.pallas_call(input_grad_kernel, grid_spec=grid_spec, out_shape=[jax.Sha...  7.57 us
    pallas_call x1, Pallas kernels, filter_grad_part(): pl.pallas_call(filter_grad_kernel, grid_spec=grid_spec, out_shape=jax.Sha...  6.8 us
    pallas_call x2, Pallas kernels, moving(): pl.pallas_call(kernel, out_shape=jax.ShapeDtypeStruct(shape, jnp.float32)...  4.51 us
  transfers between devices with their start and end apart: 10, of which 8 were waited for; matrix products, arithmetic and copies ran while one was open for 1% of the time, Pallas kernels for 5%

profile of v7, /device:TPU:6, one launch (start us, length us, event | category | flops | bytes accessed | tf_op | source)
XLA Modules:
  0.0 197.2 jit_solution(3714554546273585882)
XLA Ops:
  0.6 2.5 %shard_map.104 = f32[4,8,2,2,4,8,128]{6,5,4,3,2,1,0:T(8,128)} custom-call(s32[1]{0:T(128)} %bitcast.half, f32[4,2,4,8,8,128]{5,4,3,2,1,0:T(8,128)} %bitcast.35, f32[4,2,4,8,8,128]{5,4,3,2,1,0:T(8,128)} %bitcast.36), custom_call_target="tpu_custom_call" | custom-call | bytes 4194304 | tf_op jit(solution)/shard_map/pallas_call | solution.py:267
  3.2 16.3 %all-to-all-start = ((f32[64,2,4,8,128]{4,3,2,1,0:T(8,128)}), f32[64,2,4,8,128]{4,3,2,1,0:T(8,128)S(1)}, u32[]{:S(2)}, u32[]{:S(2)}) async-start(f32[64,2,4,8,128]{4,3,2,1,0:T(8,128)} %bitcast.34), calls=%async_computation | async-start | bytes 4194304 | tf_op jit(solution)/shard_map/all_to_all | solution.py:303
  19.5 8.5 %collective-permute-start = (f32[4,8192]{1,0:T(4,128)S(1)}, f32[4,8192]{1,0:T(4,128)S(1)}, u32[]{:S(2)}, u32[]{:S(2)}) collective-permute-start(f32[4,8192]{1,0:T(4,128)S(1)} %copy-done.7), channel_id=1, source_target_pairs={{0,72},{2,74},{4,76},{6,78},{8,64},{10,66},{12,68},{14,70},{64,8},... | collective-permute-start | bytes 393224 | tf_op jit(solution)/shard_map/ppermute | solution.py:306
  28.0 77.0 %collective-permute-done = f32[4,8192]{1,0:T(4,128)S(1)} collective-permute-done((f32[4,8192]{1,0:T(4,128)S(1)}, f32[4,8192]{1,0:T(4,128)S(1)}, u32[]{:S(2)}, u32[]{:S(2)}) %collective-permute-start) | collective-permute-done | bytes 131104 | tf_op jit(solution)/shard_map/ppermute | solution.py:306
  105.1 3.3 %collective-permute-start.2 = (f32[8,64,128]{2,1,0:T(8,128)S(1)}, f32[8,64,128]{2,1,0:T(8,128)S(1)}, u32[]{:S(2)}, u32[]{:S(2)}) collective-permute-start(f32[8,64,128]{2,1,0:T(8,128)S(1)} %bitcast.38), channel_id=1, source_target_pairs={{0,256},{128,384},{256,0},{384,128},{1,257},{129,385},{257,1},{385... | collective-permute-start | bytes 786440 | tf_op jit(solution)/shard_map/ppermute | solution.py:309
  108.4 4.0 %collective-permute-start.1 = (f32[8,64,128]{2,1,0:T(8,128)S(1)}, f32[8,64,128]{2,1,0:T(8,128)S(1)}, u32[]{:S(2)}, u32[]{:S(2)}) collective-permute-start(f32[8,64,128]{2,1,0:T(8,128)S(1)} %bitcast.39), channel_id=1, source_target_pairs={{0,128},{128,256},{256,384},{384,0},{1,129},{129,257},{257,385},{3... | collective-permute-start | bytes 786440 | tf_op jit(solution)/shard_map/ppermute | solution.py:309
  112.4 1.9 collective-permute-start.3
  114.3 2.5 %collective-permute-done.2 = f32[8,64,128]{2,1,0:T(8,128)S(1)} collective-permute-done((f32[8,64,128]{2,1,0:T(8,128)S(1)}, f32[8,64,128]{2,1,0:T(8,128)S(1)}, u32[]{:S(2)}, u32[]{:S(2)}) %collective-permute-start.2) | collective-permute-done | bytes 262176 | tf_op jit(solution)/shard_map/ppermute | solution.py:309
  116.9 3.2 %collective-permute-done.1 = f32[8,64,128]{2,1,0:T(8,128)S(1)} collective-permute-done((f32[8,64,128]{2,1,0:T(8,128)S(1)}, f32[8,64,128]{2,1,0:T(8,128)S(1)}, u32[]{:S(2)}, u32[]{:S(2)}) %collective-permute-start.1) | collective-permute-done | bytes 262176 | tf_op jit(solution)/shard_map/ppermute | solution.py:309
  120.0 3.2 %collective-permute-done.3 = f32[8,64,128]{2,1,0:T(8,128)} collective-permute-done((f32[8,64,128]{2,1,0:T(8,128)S(1)}, f32[8,64,128]{2,1,0:T(8,128)}, u32[]{:S(2)}, u32[]{:S(2)}) %collective-permute-start.3) | collective-permute-done | bytes 262176 | tf_op jit(solution)/shard_map/ppermute | solution.py:309
  124.3 2.3 %shard_map.105.filter_spec = f32[4,576,256]{2,1,0:T(8,128)S(1)} custom-call(bf16[144,192]{1,0:T(8,128)(2,1)S(1)} %copy-done.4, f32[2,72,128]{2,1,0:T(8,128)S(1)} %copy-done.3, bf16[768,256]{1,0:T(8,128)(2,1)S(1)} %copy-done.1, f32[4,8,64,128]{3,2,1,0:T(8,128)S(1)} %pad_maximum_fusion.filters), custom_call_target="tpu_custom_call" | custom-call | flops 1000000000 | bytes 2097152 | tf_op jit(solution)/shard_map/pallas_call | solution.py:141
  126.6 1.4 copy-done
  128.1 7.6 %shard_map.106 = (f32[4,576,256]{2,1,0:T(8,128)}, f32[64,4,8,128]{3,2,1,0:T(8,128)}) custom-call(s32[1]{0:T(128)} %bitcast.1.at, bf16[144,192]{1,0:T(8,128)(2,1)S(1)} %copy-done.4, f32[2,72,128]{2,1,0:T(8,128)S(1)} %copy-done.3, bf16[768,256]{1,0:T(8,128)(2,1)S(1)} %copy-done.1, bf16[768,256]{1,0:T(8,128)(2,1)S(1)} %copy-done.2, ...), custom_call_target="tpu_custom_call" | custom-call | flops 2000000000 | bytes 4194304 | tf_op jit(solution)/shard_map/pallas_call | solution.py:170
  135.7 5.5 %all-to-all-start.1 = ((f32[64,4,8,128]{3,2,1,0:T(8,128)}), f32[64,4,8,128]{3,2,1,0:T(8,128)}, u32[]{:S(2)}, u32[]{:S(2)}) async-start(f32[64,4,8,128]{3,2,1,0:T(8,128)} %get-tuple-element.8), calls=%async_computation.1 | async-start | bytes 2097152 | tf_op jit(solution)/shard_map/all_to_all | solution.py:303
  141.2 6.8 %shard_map.108 = f32[4,8,64,128]{3,2,1,0:T(8,128)S(1)} custom-call(s32[1]{0:T(128)} %bitcast.1.at, bf16[144,192]{1,0:T(8,128)(2,1)S(1)} %copy-done.4, f32[2,72,128]{2,1,0:T(8,128)S(1)} %copy-done.3, bf16[768,256]{1,0:T(8,128)(2,1)S(1)} %copy-done.1, bf16[768,256]{1,0:T(8,128)(2,1)S(1)} %copy-done.2, bf16[64,432]{1,0:T(8,128)(2,1)S(1)} %copy-done.5, ...), custom_call_target="tpu_custom_call" | custom-call | tf_op jit(solution)/shard_map/pallas_call | solution.py:198
  148.1 2.5 %collective-permute-start.5 = (f32[8,64,128]{2,1,0:T(8,128)S(1)}, f32[8,64,128]{2,1,0:T(8,128)S(1)}, u32[]{:S(2)}, u32[]{:S(2)}) collective-permute-start(f32[8,64,128]{2,1,0:T(8,128)S(1)} %get-tuple-element.10), channel_id=1, source_target_pairs={{0,256},{128,384},{256,0},{384,128},{1,257},{129,385},{257,1},{385... | collective-permute-start | bytes 786440 | tf_op jit(solution)/shard_map/ppermute | solution.py:309
  150.5 1.9 collective-permute-start.6
  152.5 5.1 %collective-permute-start.4 = (f32[8,64,128]{2,1,0:T(8,128)S(1)}, f32[8,64,128]{2,1,0:T(8,128)S(1)}, u32[]{:S(2)}, u32[]{:S(2)}) collective-permute-start(f32[8,64,128]{2,1,0:T(8,128)S(1)} %get-tuple-element.12), channel_id=1, source_target_pairs={{0,128},{128,256},{256,384},{384,0},{1,129},{129,257},{257,385},{3... | collective-permute-start | bytes 786440 | tf_op jit(solution)/shard_map/ppermute | solution.py:309
  157.6 3.1 %collective-permute-done.5 = f32[8,64,128]{2,1,0:T(8,128)S(1)} collective-permute-done((f32[8,64,128]{2,1,0:T(8,128)S(1)}, f32[8,64,128]{2,1,0:T(8,128)S(1)}, u32[]{:S(2)}, u32[]{:S(2)}) %collective-permute-start.5) | collective-permute-done | bytes 262176 | tf_op jit(solution)/shard_map/ppermute | solution.py:309
  160.7 4.5 %collective-permute-done.6 = f32[8,64,128]{2,1,0:T(8,128)S(1)} collective-permute-done((f32[8,64,128]{2,1,0:T(8,128)S(1)}, f32[8,64,128]{2,1,0:T(8,128)S(1)}, u32[]{:S(2)}, u32[]{:S(2)}) %collective-permute-start.6) | collective-permute-done | bytes 262176 | tf_op jit(solution)/shard_map/ppermute | solution.py:309
  165.3 6.6 %collective-permute-start.7 = (f32[4,64,128]{2,1,0:T(8,128)S(1)}, f32[4,64,128]{2,1,0:T(8,128)S(1)}, u32[]{:S(2)}, u32[]{:S(2)}) collective-permute-start(f32[4,64,128]{2,1,0:T(8,128)S(1)} %slice.29), channel_id=1, source_target_pairs={{0,72},{2,74},{4,76},{6,78},{8,64},{10,66},{12,68},{14,70},{64,8},... | collective-permute-start | bytes 393224 | tf_op jit(solution)/shard_map/ppermute | solution.py:306
  171.8 19.3 %collective-permute-done.7 = f32[4,64,128]{2,1,0:T(8,128)S(1)} collective-permute-done((f32[4,64,128]{2,1,0:T(8,128)S(1)}, f32[4,64,128]{2,1,0:T(8,128)S(1)}, u32[]{:S(2)}, u32[]{:S(2)}) %collective-permute-start.7) | collective-permute-done | bytes 131104 | tf_op jit(solution)/shard_map/ppermute | solution.py:306
  191.9 3.4 %all-to-all-done.1 = f32[64,4,8,128]{3,2,1,0:T(8,128)} async-done(((f32[64,4,8,128]{3,2,1,0:T(8,128)}), f32[64,4,8,128]{3,2,1,0:T(8,128)}, u32[]{:S(2)}, u32[]{:S(2)}) %all-to-all-start.1) | async-done | bytes 1048608 | tf_op jit(solution)/shard_map/all_to_all | solution.py:303
  195.2 2.0 %shard_map.107 = f32[4,2,4,8,8,128]{5,4,3,2,1,0:T(8,128)} custom-call(s32[1]{0:T(128)} %bitcast.half, f32[4,8,2,4,8,128]{5,4,3,2,1,0:T(8,128)} %bitcast.8.blocks), custom_call_target="tpu_custom_call" | custom-call | bytes 2097152 | tf_op jit(solution)/shard_map/pallas_call | solution.py:267
  (25 shorter events, 2.1 us)
Async XLA Ops:
  3.2 16.3 %copy-start.7 = (f32[4,8192]{1,0:T(4,128)S(1)}, f32[4,8192]{1,0:T(4,128)}, u32[]{:S(2)}) copy-start(f32[4,8192]{1,0:T(4,128)} %param.11) | copy-start | bytes 393220
  3.2 124.9 %all-to-all-start = ((f32[64,2,4,8,128]{4,3,2,1,0:T(8,128)}), f32[64,2,4,8,128]{4,3,2,1,0:T(8,128)S(1)}, u32[]{:S(2)}, u32[]{:S(2)}) async-start(f32[64,2,4,8,128]{4,3,2,1,0:T(8,128)} %bitcast.34), calls=%async_computation | async-start | bytes 4194304 | tf_op jit(solution)/shard_map/all_to_all | solution.py:303
  19.5 104.8 %copy-start.1 = (bf16[768,256]{1,0:T(8,128)(2,1)S(1)}, bf16[768,256]{1,0:T(8,128)(2,1)}, u32[]{:S(2)}) copy-start(bf16[768,256]{1,0:T(8,128)(2,1)} %constant.27.clone.forward) | copy-start | bytes 1179652
  19.5 104.8 %copy-start.3 = (f32[2,72,128]{2,1,0:T(8,128)S(1)}, f32[2,72,128]{2,1,0:T(8,128)}, u32[]{:S(2)}) copy-start(f32[2,72,128]{2,1,0:T(8,128)} %constant.29.clone.turn) | copy-start | bytes 221188
  19.5 104.8 %copy-start.4 = (bf16[144,192]{1,0:T(8,128)(2,1)S(1)}, bf16[144,192]{1,0:T(8,128)(2,1)}, u32[]{:S(2)}) copy-start(bf16[144,192]{1,0:T(8,128)(2,1)} %constant.24.clone.first) | copy-start | bytes 165892
  19.5 85.4 %collective-permute-start = (f32[4,8192]{1,0:T(4,128)S(1)}, f32[4,8192]{1,0:T(4,128)S(1)}, u32[]{:S(2)}, u32[]{:S(2)}) collective-permute-start(f32[4,8192]{1,0:T(4,128)S(1)} %copy-done.7), channel_id=1, source_target_pairs={{0,72},{2,74},{4,76},{6,78},{8,64},{10,66},{12,68},{14,70},{64,8},... | collective-permute-start | bytes 393224 | tf_op jit(solution)/shard_map/ppermute | solution.py:306
  105.1 11.8 %collective-permute-start.2 = (f32[8,64,128]{2,1,0:T(8,128)S(1)}, f32[8,64,128]{2,1,0:T(8,128)S(1)}, u32[]{:S(2)}, u32[]{:S(2)}) collective-permute-start(f32[8,64,128]{2,1,0:T(8,128)S(1)} %bitcast.38), channel_id=1, source_target_pairs={{0,256},{128,384},{256,0},{384,128},{1,257},{129,385},{257,1},{385... | collective-permute-start | bytes 786440 | tf_op jit(solution)/shard_map/ppermute | solution.py:309
  108.4 11.6 %collective-permute-start.1 = (f32[8,64,128]{2,1,0:T(8,128)S(1)}, f32[8,64,128]{2,1,0:T(8,128)S(1)}, u32[]{:S(2)}, u32[]{:S(2)}) collective-permute-start(f32[8,64,128]{2,1,0:T(8,128)S(1)} %bitcast.39), channel_id=1, source_target_pairs={{0,128},{128,256},{256,384},{384,0},{1,129},{129,257},{257,385},{3... | collective-permute-start | bytes 786440 | tf_op jit(solution)/shard_map/ppermute | solution.py:309
  112.4 10.8 %collective-permute-start.3 = (f32[8,64,128]{2,1,0:T(8,128)S(1)}, f32[8,64,128]{2,1,0:T(8,128)}, u32[]{:S(2)}, u32[]{:S(2)}) collective-permute-start(f32[8,64,128]{2,1,0:T(8,128)S(1)} %bitcast.40), channel_id=1, source_target_pairs={{0,384},{128,0},{256,128},{384,256},{1,385},{129,1},{257,129},{385... | collective-permute-start | bytes 786440 | tf_op jit(solution)/shard_map/ppermute | solution.py:309
  124.3 3.8 %copy-start.2 = (bf16[768,256]{1,0:T(8,128)(2,1)S(1)}, bf16[768,256]{1,0:T(8,128)(2,1)}, u32[]{:S(2)}) copy-start(bf16[768,256]{1,0:T(8,128)(2,1)} %constant.28.clone.inverse) | copy-start | bytes 1179652
  124.3 3.8 %copy-start.6 = (bf16[64,432]{1,0:T(8,128)(2,1)S(1)}, bf16[64,432]{1,0:T(8,128)(2,1)}, u32[]{:S(2)}) copy-start(bf16[64,432]{1,0:T(8,128)(2,1)} %constant.25.clone.last) | copy-start | bytes 165892
  126.6 1.4 copy-start
  128.1 13.1 %copy-start.5 = (bf16[64,432]{1,0:T(8,128)(2,1)S(1)}, bf16[64,432]{1,0:T(8,128)(2,1)}, u32[]{:S(2)}) copy-start(bf16[64,432]{1,0:T(8,128)(2,1)} %constant.26.clone.last) | copy-start | bytes 165892
  135.7 59.6 %all-to-all-start.1 = ((f32[64,4,8,128]{3,2,1,0:T(8,128)}), f32[64,4,8,128]{3,2,1,0:T(8,128)}, u32[]{:S(2)}, u32[]{:S(2)}) async-start(f32[64,4,8,128]{3,2,1,0:T(8,128)} %get-tuple-element.8), calls=%async_computation.1 | async-start | bytes 2097152 | tf_op jit(solution)/shard_map/all_to_all | solution.py:303
  148.1 12.6 %collective-permute-start.5 = (f32[8,64,128]{2,1,0:T(8,128)S(1)}, f32[8,64,128]{2,1,0:T(8,128)S(1)}, u32[]{:S(2)}, u32[]{:S(2)}) collective-permute-start(f32[8,64,128]{2,1,0:T(8,128)S(1)} %get-tuple-element.10), channel_id=1, source_target_pairs={{0,256},{128,384},{256,0},{384,128},{1,257},{129,385},{257,1},{385... | collective-permute-start | bytes 786440 | tf_op jit(solution)/shard_map/ppermute | solution.py:309
  150.5 14.6 %collective-permute-start.6 = (f32[8,64,128]{2,1,0:T(8,128)S(1)}, f32[8,64,128]{2,1,0:T(8,128)S(1)}, u32[]{:S(2)}, u32[]{:S(2)}) collective-permute-start(f32[8,64,128]{2,1,0:T(8,128)S(1)} %get-tuple-element.11), channel_id=1, source_target_pairs={{0,384},{128,0},{256,128},{384,256},{1,385},{129,1},{257,129},{385... | collective-permute-start | bytes 786440 | tf_op jit(solution)/shard_map/ppermute | solution.py:309
  152.5 12.7 %collective-permute-start.4 = (f32[8,64,128]{2,1,0:T(8,128)S(1)}, f32[8,64,128]{2,1,0:T(8,128)S(1)}, u32[]{:S(2)}, u32[]{:S(2)}) collective-permute-start(f32[8,64,128]{2,1,0:T(8,128)S(1)} %get-tuple-element.12), channel_id=1, source_target_pairs={{0,128},{128,256},{256,384},{384,0},{1,129},{129,257},{257,385},{3... | collective-permute-start | bytes 786440 | tf_op jit(solution)/shard_map/ppermute | solution.py:309
  165.3 25.8 %collective-permute-start.7 = (f32[4,64,128]{2,1,0:T(8,128)S(1)}, f32[4,64,128]{2,1,0:T(8,128)S(1)}, u32[]{:S(2)}, u32[]{:S(2)}) collective-permute-start(f32[4,64,128]{2,1,0:T(8,128)S(1)} %slice.29), channel_id=1, source_target_pairs={{0,72},{2,74},{4,76},{6,78},{8,64},{10,66},{12,68},{14,70},{64,8},... | collective-permute-start | bytes 393224 | tf_op jit(solution)/shard_map/ppermute | solution.py:306

commit v8 on v7

--- a/solution.py
+++ b/solution.py
@@ -144,7 +144,7 @@
         out_shape=jax.ShapeDtypeStruct((count, r * HALF, 2 * m), jnp.float32),
         in_specs=specs + [pl.BlockSpec((None, r, a, m), lambda i: (i, 0, 0, 0))],
         out_specs=pl.BlockSpec((None, r * HALF, 2 * m), lambda i: (i, 0, 0)),
-        cost_estimate=cost(10**9, 8 * filters.size),
+        cost_estimate=cost(83 * 10**9, 8 * filters.size),
         compiler_params=LIMIT,
     )(*operands, filters)
 
@@ -235,7 +235,7 @@
     def work(i):
         for k in range(z):
             for n in range(len(arrays)):
-                near, other = arrived[i, n, :, own, k], arrived[i, n, :, far, k ^ (z // 2)]
+                near, other = arrived[i, n, :, own, k], arrived[i, n, :, far, z - 1 - k]
                 leaving[i, k, 0, n] = jnp.concatenate([near[:, :j], other[:, :j]], axis=1)
                 leaving[i, k, 1, n] = jnp.concatenate([near[:, j:], other[:, j:]], axis=1)
 
@@ -257,7 +257,7 @@
         for k in range(z):
             low, high = arrived[i, k, 0], arrived[i, k, 1]
             leaving[i, :, own, k] = jnp.concatenate([low[:, :j], high[:, :j]], axis=1)
-            leaving[i, :, far, k ^ (z // 2)] = jnp.concatenate([low[:, j:], high[:, j:]], axis=1)
+            leaving[i, :, far, z - 1 - k] = jnp.concatenate([low[:, j:], high[:, j:]], axis=1)
 
     in_parts(incoming, work, outgoing)
 
@@ -303,7 +303,7 @@
         return lax.all_to_all(blocks, ("y", "zl", "c"), 0, 0, tiled=True)
 
     def facing(v):
-        return lax.ppermute(v, ("zh", "zl"), [(i, i ^ z ^ (z // 2)) for i in range(h * z)])
+        return lax.ppermute(v, ("zh", "zl"), [(i, h * z - 1 - i) for i in range(h * z)])
 
     def along_x(v, s):
         return lax.ppermute(v, "x", [(i, (i + s) % x) for i in range(x)])

time: 198 us -> 195 us (0.985)
  waiting for transfers between devices: 116 us -> 112 us
    ppermute x2, waiting for transfers between devices: 96.2 us -> 8.7 us  [facing(): lax.ppermute(v, ('zh', 'zl'), [(i, h * z - 1 - i) for i in range(h * z)])]
    all_to_all x2, waiting for transfers between devices: 3.36 us -> 88 us  [exchange(): return lax.all_to_all(blocks, ('y', 'zl', 'c'), 0, 0, tiled=True)]
  transfers between devices with their start and end apart: 10 -> 10, of which waited for: 8 -> 9; matrix products, arithmetic and copies ran while one was open for 1% -> 1% of each run, Pallas kernels for 5% -> 5%
where the time goes in v8:
time: 195 us; the launch traced here: 194 us
  waiting for transfers between devices  112 us (57%)
  starting transfers between devices  56.3 us (29%)
  Pallas kernels  21.2 us (11%)
  local copies, waits for them, and re-layouts  2.33 us (1%)
    all_to_all x2, waiting for transfers between devices, exchange(): return lax.all_to_all(blocks, ('y', 'zl', 'c'), 0, 0, tiled=True)  88 us
    all_to_all x2, starting transfers between devices, exchange(): return lax.all_to_all(blocks, ('y', 'zl', 'c'), 0, 0, tiled=True)  21.3 us
    ppermute x6, starting transfers between devices, along_x(): return lax.ppermute(v, 'x', [(i, (i + s) % x) for i in range(x)])  19.6 us
    ppermute x2, starting transfers between devices, facing(): lax.ppermute(v, ('zh', 'zl'), [(i, h * z - 1 - i) for i in range(h * z)])  15.4 us
    ppermute x6, waiting for transfers between devices, along_x(): return lax.ppermute(v, 'x', [(i, (i + s) % x) for i in range(x)])  15.3 us
    ppermute x2, waiting for transfers between devices, facing(): lax.ppermute(v, ('zh', 'zl'), [(i, h * z - 1 - i) for i in range(h * z)])  8.7 us
    pallas_call x1, Pallas kernels, input_grad_part(): pl.pallas_call(input_grad_kernel, grid_spec=grid_spec, out_shape=[jax.Sha...  7.56 us
    pallas_call x1, Pallas kernels, filter_grad_part(): pl.pallas_call(filter_grad_kernel, grid_spec=grid_spec, out_shape=jax.Sha...  6.8 us
  transfers between devices with their start and end apart: 10, of which 9 were waited for; matrix products, arithmetic and copies ran while one was open for 1% of the time, Pallas kernels for 5%

profile of v8, /device:TPU:6, one launch (start us, length us, event | category | flops | bytes accessed | tf_op | source)
XLA Modules:
  0.0 193.9 jit_solution(5877560137511924186)
XLA Ops:
  0.6 2.5 %shard_map.104 = f32[4,8,2,2,4,8,128]{6,5,4,3,2,1,0:T(8,128)} custom-call(s32[1]{0:T(128)} %bitcast.half, f32[4,2,4,8,8,128]{5,4,3,2,1,0:T(8,128)} %bitcast.35, f32[4,2,4,8,8,128]{5,4,3,2,1,0:T(8,128)} %bitcast.36), custom_call_target="tpu_custom_call" | custom-call | bytes 4194304 | tf_op jit(solution)/shard_map/pallas_call | solution.py:267
  3.2 11.4 %collective-permute-start = (f32[4,8192]{1,0:T(4,128)S(1)}, f32[4,8192]{1,0:T(4,128)S(1)}, u32[]{:S(2)}, u32[]{:S(2)}) collective-permute-start(f32[4,8192]{1,0:T(4,128)S(1)} %copy-done.7), channel_id=1, source_target_pairs={{0,78},{2,76},{4,74},{6,72},{8,70},{10,68},{12,66},{14,64},{64,14}... | collective-permute-start | bytes 393224 | tf_op jit(solution)/shard_map/ppermute | solution.py:306
  14.6 11.2 %all-to-all-start = ((f32[64,2,4,8,128]{4,3,2,1,0:T(8,128)}), f32[64,2,4,8,128]{4,3,2,1,0:T(8,128)S(1)}, u32[]{:S(2)}, u32[]{:S(2)}) async-start(f32[64,2,4,8,128]{4,3,2,1,0:T(8,128)} %bitcast.34), calls=%async_computation | async-start | bytes 4194304 | tf_op jit(solution)/shard_map/all_to_all | solution.py:303
  26.6 3.3 %collective-permute-start.2 = (f32[8,64,128]{2,1,0:T(8,128)S(1)}, f32[8,64,128]{2,1,0:T(8,128)S(1)}, u32[]{:S(2)}, u32[]{:S(2)}) collective-permute-start(f32[8,64,128]{2,1,0:T(8,128)S(1)} %bitcast.38), channel_id=1, source_target_pairs={{0,256},{128,384},{256,0},{384,128},{1,257},{129,385},{257,1},{385... | collective-permute-start | bytes 786440 | tf_op jit(solution)/shard_map/ppermute | solution.py:309
  30.0 4.0 %collective-permute-start.1 = (f32[8,64,128]{2,1,0:T(8,128)S(1)}, f32[8,64,128]{2,1,0:T(8,128)S(1)}, u32[]{:S(2)}, u32[]{:S(2)}) collective-permute-start(f32[8,64,128]{2,1,0:T(8,128)S(1)} %bitcast.39), channel_id=1, source_target_pairs={{0,128},{128,256},{256,384},{384,0},{1,129},{129,257},{257,385},{3... | collective-permute-start | bytes 786440 | tf_op jit(solution)/shard_map/ppermute | solution.py:309
  34.0 1.9 collective-permute-start.3
  35.9 2.2 %collective-permute-done.2 = f32[8,64,128]{2,1,0:T(8,128)S(1)} collective-permute-done((f32[8,64,128]{2,1,0:T(8,128)S(1)}, f32[8,64,128]{2,1,0:T(8,128)S(1)}, u32[]{:S(2)}, u32[]{:S(2)}) %collective-permute-start.2) | collective-permute-done | bytes 262176 | tf_op jit(solution)/shard_map/ppermute | solution.py:309
  38.1 3.2 %collective-permute-done.1 = f32[8,64,128]{2,1,0:T(8,128)S(1)} collective-permute-done((f32[8,64,128]{2,1,0:T(8,128)S(1)}, f32[8,64,128]{2,1,0:T(8,128)S(1)}, u32[]{:S(2)}, u32[]{:S(2)}) %collective-permute-start.1) | collective-permute-done | bytes 262176 | tf_op jit(solution)/shard_map/ppermute | solution.py:309
  41.3 3.2 %collective-permute-done.3 = f32[8,64,128]{2,1,0:T(8,128)} collective-permute-done((f32[8,64,128]{2,1,0:T(8,128)S(1)}, f32[8,64,128]{2,1,0:T(8,128)}, u32[]{:S(2)}, u32[]{:S(2)}) %collective-permute-start.3) | collective-permute-done | bytes 262176 | tf_op jit(solution)/shard_map/ppermute | solution.py:309
  45.5 2.3 %shard_map.105.filter_spec = f32[4,576,256]{2,1,0:T(8,128)S(1)} custom-call(bf16[144,192]{1,0:T(8,128)(2,1)S(1)} %copy-done.3, f32[2,72,128]{2,1,0:T(8,128)S(1)} %copy-done.2, bf16[768,256]{1,0:T(8,128)(2,1)S(1)} %copy-done, f32[4,8,64,128]{3,2,1,0:T(8,128)S(1)} %pad_maximum_fusion.filters), custom_call_target="tpu_custom_call" | custom-call | flops 83000000512 | bytes 2097152 | tf_op jit(solution)/shard_map/pallas_call | solution.py:141
  47.9 1.4 copy-done.6
  49.3 71.1 %all-to-all-done.grad.tokens = f32[64,2,4,8,128]{4,3,2,1,0:T(8,128)S(1)} async-done(((f32[64,2,4,8,128]{4,3,2,1,0:T(8,128)}), f32[64,2,4,8,128]{4,3,2,1,0:T(8,128)S(1)}, u32[]{:S(2)}, u32[]{:S(2)}) %all-to-all-start) | async-done | bytes 2097184 | tf_op jit(solution)/shard_map/all_to_all | solution.py:303
  120.4 7.6 %shard_map.106 = (f32[4,576,256]{2,1,0:T(8,128)}, f32[64,4,8,128]{3,2,1,0:T(8,128)}) custom-call(s32[1]{0:T(128)} %bitcast.1.at, bf16[144,192]{1,0:T(8,128)(2,1)S(1)} %copy-done.3, f32[2,72,128]{2,1,0:T(8,128)S(1)} %copy-done.2, bf16[768,256]{1,0:T(8,128)(2,1)S(1)} %copy-done, bf16[768,256]{1,0:T(8,128)(2,1)S(1)} %copy-done.1, ...), custom_call_target="tpu_custom_call" | custom-call | flops 2000000000 | bytes 4194304 | tf_op jit(solution)/shard_map/pallas_call | solution.py:170
  127.9 10.1 %all-to-all-start.1 = ((f32[64,4,8,128]{3,2,1,0:T(8,128)}), f32[64,4,8,128]{3,2,1,0:T(8,128)}, u32[]{:S(2)}, u32[]{:S(2)}) async-start(f32[64,4,8,128]{3,2,1,0:T(8,128)} %get-tuple-element.8), calls=%async_computation.1 | async-start | bytes 2097152 | tf_op jit(solution)/shard_map/all_to_all | solution.py:303
  138.0 6.8 %shard_map.108 = f32[4,8,64,128]{3,2,1,0:T(8,128)S(1)} custom-call(s32[1]{0:T(128)} %bitcast.1.at, bf16[144,192]{1,0:T(8,128)(2,1)S(1)} %copy-done.3, f32[2,72,128]{2,1,0:T(8,128)S(1)} %copy-done.2, bf16[768,256]{1,0:T(8,128)(2,1)S(1)} %copy-done, bf16[768,256]{1,0:T(8,128)(2,1)S(1)} %copy-done.1, bf16[64,432]{1,0:T(8,128)(2,1)S(1)} %copy-done.4, ...), custom_call_target="tpu_custom_call" | custom-call | tf_op jit(solution)/shard_map/pallas_call | solution.py:198
  144.9 3.3 %collective-permute-start.5 = (f32[8,64,128]{2,1,0:T(8,128)S(1)}, f32[8,64,128]{2,1,0:T(8,128)S(1)}, u32[]{:S(2)}, u32[]{:S(2)}) collective-permute-start(f32[8,64,128]{2,1,0:T(8,128)S(1)} %get-tuple-element.10), channel_id=1, source_target_pairs={{0,256},{128,384},{256,0},{384,128},{1,257},{129,385},{257,1},{385... | collective-permute-start | bytes 786440 | tf_op jit(solution)/shard_map/ppermute | solution.py:309
  148.2 1.9 collective-permute-start.6
  150.2 5.1 %collective-permute-start.4 = (f32[8,64,128]{2,1,0:T(8,128)S(1)}, f32[8,64,128]{2,1,0:T(8,128)S(1)}, u32[]{:S(2)}, u32[]{:S(2)}) collective-permute-start(f32[8,64,128]{2,1,0:T(8,128)S(1)} %get-tuple-element.12), channel_id=1, source_target_pairs={{0,128},{128,256},{256,384},{384,0},{1,129},{129,257},{257,385},{3... | collective-permute-start | bytes 786440 | tf_op jit(solution)/shard_map/ppermute | solution.py:309
  155.3 2.2 %collective-permute-done.5 = f32[8,64,128]{2,1,0:T(8,128)S(1)} collective-permute-done((f32[8,64,128]{2,1,0:T(8,128)S(1)}, f32[8,64,128]{2,1,0:T(8,128)S(1)}, u32[]{:S(2)}, u32[]{:S(2)}) %collective-permute-start.5) | collective-permute-done | bytes 262176 | tf_op jit(solution)/shard_map/ppermute | solution.py:309
  157.5 4.6 %collective-permute-done.6 = f32[8,64,128]{2,1,0:T(8,128)S(1)} collective-permute-done((f32[8,64,128]{2,1,0:T(8,128)S(1)}, f32[8,64,128]{2,1,0:T(8,128)S(1)}, u32[]{:S(2)}, u32[]{:S(2)}) %collective-permute-start.6) | collective-permute-done | bytes 262176 | tf_op jit(solution)/shard_map/ppermute | solution.py:309
  162.2 4.0 %collective-permute-start.7 = (f32[4,64,128]{2,1,0:T(8,128)S(1)}, f32[4,64,128]{2,1,0:T(8,128)S(1)}, u32[]{:S(2)}, u32[]{:S(2)}) collective-permute-start(f32[4,64,128]{2,1,0:T(8,128)S(1)} %slice.29), channel_id=1, source_target_pairs={{0,78},{2,76},{4,74},{6,72},{8,70},{10,68},{12,66},{14,64},{64,14}... | collective-permute-start | bytes 393224 | tf_op jit(solution)/shard_map/ppermute | solution.py:306
  166.2 8.0 %collective-permute-done.7 = f32[4,64,128]{2,1,0:T(8,128)S(1)} collective-permute-done((f32[4,64,128]{2,1,0:T(8,128)S(1)}, f32[4,64,128]{2,1,0:T(8,128)S(1)}, u32[]{:S(2)}, u32[]{:S(2)}) %collective-permute-start.7) | collective-permute-done | bytes 131104 | tf_op jit(solution)/shard_map/ppermute | solution.py:306
  175.0 16.9 %all-to-all-done.1 = f32[64,4,8,128]{3,2,1,0:T(8,128)} async-done(((f32[64,4,8,128]{3,2,1,0:T(8,128)}), f32[64,4,8,128]{3,2,1,0:T(8,128)}, u32[]{:S(2)}, u32[]{:S(2)}) %all-to-all-start.1) | async-done | bytes 1048608 | tf_op jit(solution)/shard_map/all_to_all | solution.py:303
  191.9 2.0 %shard_map.107 = f32[4,2,4,8,8,128]{5,4,3,2,1,0:T(8,128)} custom-call(s32[1]{0:T(128)} %bitcast.half, f32[4,8,2,4,8,128]{5,4,3,2,1,0:T(8,128)} %bitcast.8.blocks), custom_call_target="tpu_custom_call" | custom-call | bytes 2097152 | tf_op jit(solution)/shard_map/pallas_call | solution.py:267
  (25 shorter events, 2.8 us)
Async XLA Ops:
  0.6 2.6 %copy-start.7 = (f32[4,8192]{1,0:T(4,128)S(1)}, f32[4,8192]{1,0:T(4,128)}, u32[]{:S(2)}) copy-start(f32[4,8192]{1,0:T(4,128)} %param.11) | copy-start | bytes 393220
  3.2 23.3 %collective-permute-start = (f32[4,8192]{1,0:T(4,128)S(1)}, f32[4,8192]{1,0:T(4,128)S(1)}, u32[]{:S(2)}, u32[]{:S(2)}) collective-permute-start(f32[4,8192]{1,0:T(4,128)S(1)} %copy-done.7), channel_id=1, source_target_pairs={{0,78},{2,76},{4,74},{6,72},{8,70},{10,68},{12,66},{14,64},{64,14}... | collective-permute-start | bytes 393224 | tf_op jit(solution)/shard_map/ppermute | solution.py:306
  14.6 105.8 %all-to-all-start = ((f32[64,2,4,8,128]{4,3,2,1,0:T(8,128)}), f32[64,2,4,8,128]{4,3,2,1,0:T(8,128)S(1)}, u32[]{:S(2)}, u32[]{:S(2)}) async-start(f32[64,2,4,8,128]{4,3,2,1,0:T(8,128)} %bitcast.34), calls=%async_computation | async-start | bytes 4194304 | tf_op jit(solution)/shard_map/all_to_all | solution.py:303
  25.8 19.7 %copy-start = (bf16[768,256]{1,0:T(8,128)(2,1)S(1)}, bf16[768,256]{1,0:T(8,128)(2,1)}, u32[]{:S(2)}) copy-start(bf16[768,256]{1,0:T(8,128)(2,1)} %constant.27.clone.forward) | copy-start | bytes 1179652
  25.8 19.7 %copy-start.2 = (f32[2,72,128]{2,1,0:T(8,128)S(1)}, f32[2,72,128]{2,1,0:T(8,128)}, u32[]{:S(2)}) copy-start(f32[2,72,128]{2,1,0:T(8,128)} %constant.29.clone.turn) | copy-start | bytes 221188
  25.8 19.7 %copy-start.3 = (bf16[144,192]{1,0:T(8,128)(2,1)S(1)}, bf16[144,192]{1,0:T(8,128)(2,1)}, u32[]{:S(2)}) copy-start(bf16[144,192]{1,0:T(8,128)(2,1)} %constant.24.clone.first) | copy-start | bytes 165892
  26.6 11.5 %collective-permute-start.2 = (f32[8,64,128]{2,1,0:T(8,128)S(1)}, f32[8,64,128]{2,1,0:T(8,128)S(1)}, u32[]{:S(2)}, u32[]{:S(2)}) collective-permute-start(f32[8,64,128]{2,1,0:T(8,128)S(1)} %bitcast.38), channel_id=1, source_target_pairs={{0,256},{128,384},{256,0},{384,128},{1,257},{129,385},{257,1},{385... | collective-permute-start | bytes 786440 | tf_op jit(solution)/shard_map/ppermute | solution.py:309
  30.0 11.3 %collective-permute-start.1 = (f32[8,64,128]{2,1,0:T(8,128)S(1)}, f32[8,64,128]{2,1,0:T(8,128)S(1)}, u32[]{:S(2)}, u32[]{:S(2)}) collective-permute-start(f32[8,64,128]{2,1,0:T(8,128)S(1)} %bitcast.39), channel_id=1, source_target_pairs={{0,128},{128,256},{256,384},{384,0},{1,129},{129,257},{257,385},{3... | collective-permute-start | bytes 786440 | tf_op jit(solution)/shard_map/ppermute | solution.py:309
  34.0 10.5 %collective-permute-start.3 = (f32[8,64,128]{2,1,0:T(8,128)S(1)}, f32[8,64,128]{2,1,0:T(8,128)}, u32[]{:S(2)}, u32[]{:S(2)}) collective-permute-start(f32[8,64,128]{2,1,0:T(8,128)S(1)} %bitcast.40), channel_id=1, source_target_pairs={{0,384},{128,0},{256,128},{384,256},{1,385},{129,1},{257,129},{385... | collective-permute-start | bytes 786440 | tf_op jit(solution)/shard_map/ppermute | solution.py:309
  45.5 74.9 %copy-start.1 = (bf16[768,256]{1,0:T(8,128)(2,1)S(1)}, bf16[768,256]{1,0:T(8,128)(2,1)}, u32[]{:S(2)}) copy-start(bf16[768,256]{1,0:T(8,128)(2,1)} %constant.28.clone.inverse) | copy-start | bytes 1179652
  45.5 74.8 %copy-start.5 = (bf16[64,432]{1,0:T(8,128)(2,1)S(1)}, bf16[64,432]{1,0:T(8,128)(2,1)}, u32[]{:S(2)}) copy-start(bf16[64,432]{1,0:T(8,128)(2,1)} %constant.25.clone.last) | copy-start | bytes 165892
  47.9 1.4 copy-start.6
  120.4 17.7 %copy-start.4 = (bf16[64,432]{1,0:T(8,128)(2,1)S(1)}, bf16[64,432]{1,0:T(8,128)(2,1)}, u32[]{:S(2)}) copy-start(bf16[64,432]{1,0:T(8,128)(2,1)} %constant.26.clone.last) | copy-start | bytes 165892
  127.9 64.0 %all-to-all-start.1 = ((f32[64,4,8,128]{3,2,1,0:T(8,128)}), f32[64,4,8,128]{3,2,1,0:T(8,128)}, u32[]{:S(2)}, u32[]{:S(2)}) async-start(f32[64,4,8,128]{3,2,1,0:T(8,128)} %get-tuple-element.8), calls=%async_computation.1 | async-start | bytes 2097152 | tf_op jit(solution)/shard_map/all_to_all | solution.py:303
  144.9 12.6 %collective-permute-start.5 = (f32[8,64,128]{2,1,0:T(8,128)S(1)}, f32[8,64,128]{2,1,0:T(8,128)S(1)}, u32[]{:S(2)}, u32[]{:S(2)}) collective-permute-start(f32[8,64,128]{2,1,0:T(8,128)S(1)} %get-tuple-element.10), channel_id=1, source_target_pairs={{0,256},{128,384},{256,0},{384,128},{1,257},{129,385},{257,1},{385... | collective-permute-start | bytes 786440 | tf_op jit(solution)/shard_map/ppermute | solution.py:309
  148.2 13.9 %collective-permute-start.6 = (f32[8,64,128]{2,1,0:T(8,128)S(1)}, f32[8,64,128]{2,1,0:T(8,128)S(1)}, u32[]{:S(2)}, u32[]{:S(2)}) collective-permute-start(f32[8,64,128]{2,1,0:T(8,128)S(1)} %get-tuple-element.11), channel_id=1, source_target_pairs={{0,384},{128,0},{256,128},{384,256},{1,385},{129,1},{257,129},{385... | collective-permute-start | bytes 786440 | tf_op jit(solution)/shard_map/ppermute | solution.py:309
  150.2 12.0 %collective-permute-start.4 = (f32[8,64,128]{2,1,0:T(8,128)S(1)}, f32[8,64,128]{2,1,0:T(8,128)S(1)}, u32[]{:S(2)}, u32[]{:S(2)}) collective-permute-start(f32[8,64,128]{2,1,0:T(8,128)S(1)} %get-tuple-element.12), channel_id=1, source_target_pairs={{0,128},{128,256},{256,384},{384,0},{1,129},{129,257},{257,385},{3... | collective-permute-start | bytes 786440 | tf_op jit(solution)/shard_map/ppermute | solution.py:309
  162.2 12.0 %collective-permute-start.7 = (f32[4,64,128]{2,1,0:T(8,128)S(1)}, f32[4,64,128]{2,1,0:T(8,128)S(1)}, u32[]{:S(2)}, u32[]{:S(2)}) collective-permute-start(f32[4,64,128]{2,1,0:T(8,128)S(1)} %slice.29), channel_id=1, source_target_pairs={{0,78},{2,76},{4,74},{6,72},{8,70},{10,68},{12,66},{14,64},{64,14}... | collective-permute-start | bytes 393224 | tf_op jit(solution)/shard_map/ppermute | solution.py:306

commit v9 on v8

--- a/solution.py
+++ b/solution.py
@@ -102,18 +102,34 @@
     return jnp.concatenate([flat[row(r, block), :] for r in range(rows)], axis=1)
 
 
+def pairs_to_wide(block):
+    a, count, rows, m = block.shape
+    flat, all_rows = block.reshape(a * count * rows, m), count * rows
+    return jnp.concatenate(
+        [flat[pl.ds(r, a, stride=all_rows), :] for r in range(all_rows)], axis=1
+    )
+
+
 def filter_kernel(first, turn, forward, filters, spec):
     wide = jnp.concatenate([filters[r] for r in range(filters.shape[0])], axis=1)
     spec[...] = forward_spectrum(wide, first, turn, forward)
 
 
-def input_grad_kernel(at, first, turn, forward, inverse, last, grad, filter_spec, spec, out):
-    spec[...] = forward_spectrum(rows_to_wide(grad), first, turn, forward)
-    wide = inverse_signal(correlate(spec[...], filter_spec[...]), inverse, turn, last)
-    a, rows, m = out.shape
-    flat = out.reshape(a * rows, m)
-    for r in range(rows):
-        flat[row(r, out), :] = wide[:, r * INNER : (r + 1) * INNER]
+def input_grad_kernel(at, first, turn, forward, inverse, last, grad, *refs):
+    *filter_specs, spec, out = refs
+    a, count, rows, m = out.shape
+    wide = pairs_to_wide(grad)
+    value = forward_spectrum(wide, first, turn, forward)
+    size = rows * HALF
+    for i in range(count):
+        spec[i] = value[i * size : (i + 1) * size]
+    other = jnp.concatenate([v[...] for v in filter_specs], axis=0)
+    wide = inverse_signal(correlate(value, other), inverse, turn, last)
+    flat = out.reshape(a * count * rows, m)
+    for i in range(count):
+        for r in range(rows):
+            at_row = (i * rows + r) * INNER
+            flat[pl.ds(i * rows + r, a, stride=count * rows), :] = wide[:, at_row : at_row + INNER]
 
 
 def filter_grad_kernel(at, first, turn, forward, inverse, last, tokens, grad_spec, out):
@@ -156,15 +172,16 @@
     spec_shape = (None, r * HALF, 2 * m)
     grid_spec = pltpu.PrefetchScalarGridSpec(
         num_scalar_prefetch=1,
-        grid=(count,),
+        grid=(count // 2,),
         in_specs=specs
         + [
-            pl.BlockSpec((a, None, None, r, m), lambda i, at: (0, 0, i, 0, 0)),
-            pl.BlockSpec(spec_shape, lambda i, at: ((at[0] - i) & (count - 1), 0, 0)),
+            pl.BlockSpec((a, None, 2, r, m), lambda i, at: (0, 0, i, 0, 0)),
+            pl.BlockSpec(spec_shape, lambda i, at: ((at[0] - 2 * i) & (count - 1), 0, 0)),
+            pl.BlockSpec(spec_shape, lambda i, at: ((at[0] - 2 * i - 1) & (count - 1), 0, 0)),
         ],
         out_specs=[
-            pl.BlockSpec(spec_shape, lambda i, at: (i, 0, 0)),
-            pl.BlockSpec((a, None, r, m), lambda i, at: (0, i, 0, 0)),
+            pl.BlockSpec((2, r * HALF, 2 * m), lambda i, at: (i, 0, 0)),
+            pl.BlockSpec((a, 2, r, m), lambda i, at: (0, i, 0, 0)),
         ],
     )
     return pl.pallas_call(
@@ -176,7 +193,7 @@
         ],
         cost_estimate=cost(2 * 10**9, 8 * both.size),
         compiler_params=LIMIT,
-    )(at_x, *operands, both, filter_spec)
+    )(at_x, *operands, both, filter_spec, filter_spec)
 
 
 def filter_grad_part(at_x, both, grad_spec, tables):

time: 195 us -> 194 us (level)
  no operation moved by 1% of the time
where the time goes in v9:
time: 194 us; the launch traced here: 193 us
  waiting for transfers between devices  112 us (58%)
  starting transfers between devices  56.2 us (29%)
  Pallas kernels  19.7 us (10%)
  local copies, waits for them, and re-layouts  3.3 us (2%)
    all_to_all x2, waiting for transfers between devices, exchange(): return lax.all_to_all(blocks, ('y', 'zl', 'c'), 0, 0, tiled=True)  88.1 us
    all_to_all x2, starting transfers between devices, exchange(): return lax.all_to_all(blocks, ('y', 'zl', 'c'), 0, 0, tiled=True)  21.3 us
    ppermute x6, starting transfers between devices, along_x(): return lax.ppermute(v, 'x', [(i, (i + s) % x) for i in range(x)])  19.6 us
    ppermute x2, starting transfers between devices, facing(): lax.ppermute(v, ('zh', 'zl'), [(i, h * z - 1 - i) for i in range(h * z)])  15.4 us
    ppermute x6, waiting for transfers between devices, along_x(): return lax.ppermute(v, 'x', [(i, (i + s) % x) for i in range(x)])  15.3 us
    ppermute x2, waiting for transfers between devices, facing(): lax.ppermute(v, ('zh', 'zl'), [(i, h * z - 1 - i) for i in range(h * z)])  8.6 us
    pallas_call x1, Pallas kernels, filter_grad_part(): pl.pallas_call(filter_grad_kernel, grid_spec=grid_spec, out_shape=jax.Sha...  6.8 us
    pallas_call x1, Pallas kernels, input_grad_part(): pl.pallas_call(input_grad_kernel, grid_spec=grid_spec, out_shape=[jax.Sha...  6.04 us
  transfers between devices with their start and end apart: 10, of which 9 were waited for; matrix products, arithmetic and copies ran while one was open for 1% of the time, Pallas kernels for 5%

profile of v9, /device:TPU:6, one launch (start us, length us, event | category | flops | bytes accessed | tf_op | source)
XLA Modules:
  0.0 193.4 jit_solution(7429943136311770615)
XLA Ops:
  0.6 2.5 %shard_map.104 = f32[4,8,2,2,4,8,128]{6,5,4,3,2,1,0:T(8,128)} custom-call(s32[1]{0:T(128)} %bitcast.half, f32[4,2,4,8,8,128]{5,4,3,2,1,0:T(8,128)} %bitcast.35, f32[4,2,4,8,8,128]{5,4,3,2,1,0:T(8,128)} %bitcast.36), custom_call_target="tpu_custom_call" | custom-call | bytes 4194304 | tf_op jit(solution)/shard_map/pallas_call | solution.py:284
  3.2 11.4 %collective-permute-start = (f32[4,8192]{1,0:T(4,128)S(1)}, f32[4,8192]{1,0:T(4,128)S(1)}, u32[]{:S(2)}, u32[]{:S(2)}) collective-permute-start(f32[4,8192]{1,0:T(4,128)S(1)} %copy-done.8), channel_id=1, source_target_pairs={{0,78},{2,76},{4,74},{6,72},{8,70},{10,68},{12,66},{14,64},{64,14}... | collective-permute-start | bytes 393224 | tf_op jit(solution)/shard_map/ppermute | solution.py:323
  14.6 11.2 %all-to-all-start = ((f32[64,2,4,8,128]{4,3,2,1,0:T(8,128)}), f32[64,2,4,8,128]{4,3,2,1,0:T(8,128)S(1)}, u32[]{:S(2)}, u32[]{:S(2)}) async-start(f32[64,2,4,8,128]{4,3,2,1,0:T(8,128)} %bitcast.34), calls=%async_computation | async-start | bytes 4194304 | tf_op jit(solution)/shard_map/all_to_all | solution.py:320
  26.6 3.3 %collective-permute-start.2 = (f32[8,64,128]{2,1,0:T(8,128)S(1)}, f32[8,64,128]{2,1,0:T(8,128)S(1)}, u32[]{:S(2)}, u32[]{:S(2)}) collective-permute-start(f32[8,64,128]{2,1,0:T(8,128)S(1)} %bitcast.38), channel_id=1, source_target_pairs={{0,256},{128,384},{256,0},{384,128},{1,257},{129,385},{257,1},{385... | collective-permute-start | bytes 786440 | tf_op jit(solution)/shard_map/ppermute | solution.py:326
  30.0 4.0 %collective-permute-start.1 = (f32[8,64,128]{2,1,0:T(8,128)S(1)}, f32[8,64,128]{2,1,0:T(8,128)S(1)}, u32[]{:S(2)}, u32[]{:S(2)}) collective-permute-start(f32[8,64,128]{2,1,0:T(8,128)S(1)} %bitcast.39), channel_id=1, source_target_pairs={{0,128},{128,256},{256,384},{384,0},{1,129},{129,257},{257,385},{3... | collective-permute-start | bytes 786440 | tf_op jit(solution)/shard_map/ppermute | solution.py:326
  34.0 1.9 collective-permute-start.3
  35.9 2.2 %collective-permute-done.2 = f32[8,64,128]{2,1,0:T(8,128)S(1)} collective-permute-done((f32[8,64,128]{2,1,0:T(8,128)S(1)}, f32[8,64,128]{2,1,0:T(8,128)S(1)}, u32[]{:S(2)}, u32[]{:S(2)}) %collective-permute-start.2) | collective-permute-done | bytes 262176 | tf_op jit(solution)/shard_map/ppermute | solution.py:326
  38.1 3.2 %collective-permute-done.1 = f32[8,64,128]{2,1,0:T(8,128)S(1)} collective-permute-done((f32[8,64,128]{2,1,0:T(8,128)S(1)}, f32[8,64,128]{2,1,0:T(8,128)S(1)}, u32[]{:S(2)}, u32[]{:S(2)}) %collective-permute-start.1) | collective-permute-done | bytes 262176 | tf_op jit(solution)/shard_map/ppermute | solution.py:326
  41.3 3.2 %collective-permute-done.3 = f32[8,64,128]{2,1,0:T(8,128)} collective-permute-done((f32[8,64,128]{2,1,0:T(8,128)S(1)}, f32[8,64,128]{2,1,0:T(8,128)}, u32[]{:S(2)}, u32[]{:S(2)}) %collective-permute-start.3) | collective-permute-done | bytes 262176 | tf_op jit(solution)/shard_map/ppermute | solution.py:326
  45.5 2.3 %shard_map.105.refs_0_.refs_1_ = f32[4,576,256]{2,1,0:T(8,128)S(1)} custom-call(bf16[144,192]{1,0:T(8,128)(2,1)S(1)} %copy-done.5, f32[2,72,128]{2,1,0:T(8,128)S(1)} %copy-done.4, bf16[768,256]{1,0:T(8,128)(2,1)S(1)} %copy-done.1, f32[4,8,64,128]{3,2,1,0:T(8,128)S(1)} %pad_maximum_fusion.filters), custom_call_target="tpu_custom_call" | custom-call | flops 83000000512 | bytes 2097152 | tf_op jit(solution)/shard_map/pallas_call | solution.py:157
  47.9 1.4 copy-done
  49.3 71.1 %all-to-all-done.grad.tokens = f32[64,2,4,8,128]{4,3,2,1,0:T(8,128)S(1)} async-done(((f32[64,2,4,8,128]{4,3,2,1,0:T(8,128)}), f32[64,2,4,8,128]{4,3,2,1,0:T(8,128)S(1)}, u32[]{:S(2)}, u32[]{:S(2)}) %all-to-all-start) | async-done | bytes 2097184 | tf_op jit(solution)/shard_map/all_to_all | solution.py:320
  120.4 6.0 %shard_map.106 = (f32[4,576,256]{2,1,0:T(8,128)}, f32[64,4,8,128]{3,2,1,0:T(8,128)S(1)}) custom-call(s32[1]{0:T(128)} %bitcast.1.at, bf16[144,192]{1,0:T(8,128)(2,1)S(1)} %copy-done.5, f32[2,72,128]{2,1,0:T(8,128)S(1)} %copy-done.4, bf16[768,256]{1,0:T(8,128)(2,1)S(1)} %copy-done.1, bf16[768,256]{1,0:T(8,128)(2,1)S(1)} %copy-done.2, ...), custom_call_target="tpu_custom_call" | custom-call | flops 2000000000 | bytes 4194304 | tf_op jit(solution)/shard_map/pallas_call | solution.py:187
  127.4 10.1 %all-to-all-start.1 = ((f32[64,4,8,128]{3,2,1,0:T(8,128)}), f32[64,4,8,128]{3,2,1,0:T(8,128)}, u32[]{:S(2)}, u32[]{:S(2)}) async-start(f32[64,4,8,128]{3,2,1,0:T(8,128)} %copy-done.3), calls=%async_computation.1 | async-start | bytes 2097152 | tf_op jit(solution)/shard_map/all_to_all | solution.py:320
  137.5 6.8 %shard_map.108 = f32[4,8,64,128]{3,2,1,0:T(8,128)S(1)} custom-call(s32[1]{0:T(128)} %bitcast.1.at, bf16[144,192]{1,0:T(8,128)(2,1)S(1)} %copy-done.5, f32[2,72,128]{2,1,0:T(8,128)S(1)} %copy-done.4, bf16[768,256]{1,0:T(8,128)(2,1)S(1)} %copy-done.1, bf16[768,256]{1,0:T(8,128)(2,1)S(1)} %copy-done.2, bf16[64,432]{1,0:T(8,128)(2,1)S(1)} %copy-done.6, ...), custom_call_target="tpu_custom_call" | custom-call | tf_op jit(solution)/shard_map/pallas_call | solution.py:215
  144.4 3.3 %collective-permute-start.5 = (f32[8,64,128]{2,1,0:T(8,128)S(1)}, f32[8,64,128]{2,1,0:T(8,128)S(1)}, u32[]{:S(2)}, u32[]{:S(2)}) collective-permute-start(f32[8,64,128]{2,1,0:T(8,128)S(1)} %get-tuple-element.10), channel_id=1, source_target_pairs={{0,256},{128,384},{256,0},{384,128},{1,257},{129,385},{257,1},{385... | collective-permute-start | bytes 786440 | tf_op jit(solution)/shard_map/ppermute | solution.py:326
  147.7 1.9 collective-permute-start.6
  149.6 5.1 %collective-permute-start.4 = (f32[8,64,128]{2,1,0:T(8,128)S(1)}, f32[8,64,128]{2,1,0:T(8,128)S(1)}, u32[]{:S(2)}, u32[]{:S(2)}) collective-permute-start(f32[8,64,128]{2,1,0:T(8,128)S(1)} %get-tuple-element.12), channel_id=1, source_target_pairs={{0,128},{128,256},{256,384},{384,0},{1,129},{129,257},{257,385},{3... | collective-permute-start | bytes 786440 | tf_op jit(solution)/shard_map/ppermute | solution.py:326
  154.8 2.2 %collective-permute-done.5 = f32[8,64,128]{2,1,0:T(8,128)S(1)} collective-permute-done((f32[8,64,128]{2,1,0:T(8,128)S(1)}, f32[8,64,128]{2,1,0:T(8,128)S(1)}, u32[]{:S(2)}, u32[]{:S(2)}) %collective-permute-start.5) | collective-permute-done | bytes 262176 | tf_op jit(solution)/shard_map/ppermute | solution.py:326
  157.0 4.6 %collective-permute-done.6 = f32[8,64,128]{2,1,0:T(8,128)S(1)} collective-permute-done((f32[8,64,128]{2,1,0:T(8,128)S(1)}, f32[8,64,128]{2,1,0:T(8,128)S(1)}, u32[]{:S(2)}, u32[]{:S(2)}) %collective-permute-start.6) | collective-permute-done | bytes 262176 | tf_op jit(solution)/shard_map/ppermute | solution.py:326
  161.7 4.0 %collective-permute-start.7 = (f32[4,64,128]{2,1,0:T(8,128)S(1)}, f32[4,64,128]{2,1,0:T(8,128)S(1)}, u32[]{:S(2)}, u32[]{:S(2)}) collective-permute-start(f32[4,64,128]{2,1,0:T(8,128)S(1)} %slice.29), channel_id=1, source_target_pairs={{0,78},{2,76},{4,74},{6,72},{8,70},{10,68},{12,66},{14,64},{64,14}... | collective-permute-start | bytes 393224 | tf_op jit(solution)/shard_map/ppermute | solution.py:323
  165.7 7.9 %collective-permute-done.7 = f32[4,64,128]{2,1,0:T(8,128)S(1)} collective-permute-done((f32[4,64,128]{2,1,0:T(8,128)S(1)}, f32[4,64,128]{2,1,0:T(8,128)S(1)}, u32[]{:S(2)}, u32[]{:S(2)}) %collective-permute-start.7) | collective-permute-done | bytes 131104 | tf_op jit(solution)/shard_map/ppermute | solution.py:323
  174.3 17.1 %all-to-all-done.1 = f32[64,4,8,128]{3,2,1,0:T(8,128)} async-done(((f32[64,4,8,128]{3,2,1,0:T(8,128)}), f32[64,4,8,128]{3,2,1,0:T(8,128)}, u32[]{:S(2)}, u32[]{:S(2)}) %all-to-all-start.1) | async-done | bytes 1048608 | tf_op jit(solution)/shard_map/all_to_all | solution.py:320
  191.4 2.0 %shard_map.107 = f32[4,2,4,8,8,128]{5,4,3,2,1,0:T(8,128)} custom-call(s32[1]{0:T(128)} %bitcast.half, f32[4,8,2,4,8,128]{5,4,3,2,1,0:T(8,128)} %bitcast.8.blocks), custom_call_target="tpu_custom_call" | custom-call | bytes 2097152 | tf_op jit(solution)/shard_map/pallas_call | solution.py:284
  (27 shorter events, 3.7 us)
Async XLA Ops:
  0.6 2.6 %copy-start.8 = (f32[4,8192]{1,0:T(4,128)S(1)}, f32[4,8192]{1,0:T(4,128)}, u32[]{:S(2)}) copy-start(f32[4,8192]{1,0:T(4,128)} %param.11) | copy-start | bytes 393220
  3.2 23.3 %collective-permute-start = (f32[4,8192]{1,0:T(4,128)S(1)}, f32[4,8192]{1,0:T(4,128)S(1)}, u32[]{:S(2)}, u32[]{:S(2)}) collective-permute-start(f32[4,8192]{1,0:T(4,128)S(1)} %copy-done.8), channel_id=1, source_target_pairs={{0,78},{2,76},{4,74},{6,72},{8,70},{10,68},{12,66},{14,64},{64,14}... | collective-permute-start | bytes 393224 | tf_op jit(solution)/shard_map/ppermute | solution.py:323
  14.6 105.8 %all-to-all-start = ((f32[64,2,4,8,128]{4,3,2,1,0:T(8,128)}), f32[64,2,4,8,128]{4,3,2,1,0:T(8,128)S(1)}, u32[]{:S(2)}, u32[]{:S(2)}) async-start(f32[64,2,4,8,128]{4,3,2,1,0:T(8,128)} %bitcast.34), calls=%async_computation | async-start | bytes 4194304 | tf_op jit(solution)/shard_map/all_to_all | solution.py:320
  25.8 19.7 %copy-start.1 = (bf16[768,256]{1,0:T(8,128)(2,1)S(1)}, bf16[768,256]{1,0:T(8,128)(2,1)}, u32[]{:S(2)}) copy-start(bf16[768,256]{1,0:T(8,128)(2,1)} %constant.27.clone.forward) | copy-start | bytes 1179652
  25.8 19.7 %copy-start.4 = (f32[2,72,128]{2,1,0:T(8,128)S(1)}, f32[2,72,128]{2,1,0:T(8,128)}, u32[]{:S(2)}) copy-start(f32[2,72,128]{2,1,0:T(8,128)} %constant.29.clone.turn) | copy-start | bytes 221188
  25.8 19.7 %copy-start.5 = (bf16[144,192]{1,0:T(8,128)(2,1)S(1)}, bf16[144,192]{1,0:T(8,128)(2,1)}, u32[]{:S(2)}) copy-start(bf16[144,192]{1,0:T(8,128)(2,1)} %constant.24.clone.first) | copy-start | bytes 165892
  26.6 11.5 %collective-permute-start.2 = (f32[8,64,128]{2,1,0:T(8,128)S(1)}, f32[8,64,128]{2,1,0:T(8,128)S(1)}, u32[]{:S(2)}, u32[]{:S(2)}) collective-permute-start(f32[8,64,128]{2,1,0:T(8,128)S(1)} %bitcast.38), channel_id=1, source_target_pairs={{0,256},{128,384},{256,0},{384,128},{1,257},{129,385},{257,1},{385... | collective-permute-start | bytes 786440 | tf_op jit(solution)/shard_map/ppermute | solution.py:326
  30.0 11.3 %collective-permute-start.1 = (f32[8,64,128]{2,1,0:T(8,128)S(1)}, f32[8,64,128]{2,1,0:T(8,128)S(1)}, u32[]{:S(2)}, u32[]{:S(2)}) collective-permute-start(f32[8,64,128]{2,1,0:T(8,128)S(1)} %bitcast.39), channel_id=1, source_target_pairs={{0,128},{128,256},{256,384},{384,0},{1,129},{129,257},{257,385},{3... | collective-permute-start | bytes 786440 | tf_op jit(solution)/shard_map/ppermute | solution.py:326
  34.0 10.5 %collective-permute-start.3 = (f32[8,64,128]{2,1,0:T(8,128)S(1)}, f32[8,64,128]{2,1,0:T(8,128)}, u32[]{:S(2)}, u32[]{:S(2)}) collective-permute-start(f32[8,64,128]{2,1,0:T(8,128)S(1)} %bitcast.40), channel_id=1, source_target_pairs={{0,384},{128,0},{256,128},{384,256},{1,385},{129,1},{257,129},{385... | collective-permute-start | bytes 786440 | tf_op jit(solution)/shard_map/ppermute | solution.py:326
  45.5 74.9 %copy-start.2 = (bf16[768,256]{1,0:T(8,128)(2,1)S(1)}, bf16[768,256]{1,0:T(8,128)(2,1)}, u32[]{:S(2)}) copy-start(bf16[768,256]{1,0:T(8,128)(2,1)} %constant.28.clone.inverse) | copy-start | bytes 1179652
  45.5 74.8 %copy-start.7 = (bf16[64,432]{1,0:T(8,128)(2,1)S(1)}, bf16[64,432]{1,0:T(8,128)(2,1)}, u32[]{:S(2)}) copy-start(bf16[64,432]{1,0:T(8,128)(2,1)} %constant.25.clone.last) | copy-start | bytes 165892
  47.9 1.4 copy-start
  120.4 17.1 %copy-start.6 = (bf16[64,432]{1,0:T(8,128)(2,1)S(1)}, bf16[64,432]{1,0:T(8,128)(2,1)}, u32[]{:S(2)}) copy-start(bf16[64,432]{1,0:T(8,128)(2,1)} %constant.26.clone.last) | copy-start | bytes 165892
  126.4 1.0 copy-start.3
  127.4 64.0 %all-to-all-start.1 = ((f32[64,4,8,128]{3,2,1,0:T(8,128)}), f32[64,4,8,128]{3,2,1,0:T(8,128)}, u32[]{:S(2)}, u32[]{:S(2)}) async-start(f32[64,4,8,128]{3,2,1,0:T(8,128)} %copy-done.3), calls=%async_computation.1 | async-start | bytes 2097152 | tf_op jit(solution)/shard_map/all_to_all | solution.py:320
  144.4 12.6 %collective-permute-start.5 = (f32[8,64,128]{2,1,0:T(8,128)S(1)}, f32[8,64,128]{2,1,0:T(8,128)S(1)}, u32[]{:S(2)}, u32[]{:S(2)}) collective-permute-start(f32[8,64,128]{2,1,0:T(8,128)S(1)} %get-tuple-element.10), channel_id=1, source_target_pairs={{0,256},{128,384},{256,0},{384,128},{1,257},{129,385},{257,1},{385... | collective-permute-start | bytes 786440 | tf_op jit(solution)/shard_map/ppermute | solution.py:326
  147.7 13.9 %collective-permute-start.6 = (f32[8,64,128]{2,1,0:T(8,128)S(1)}, f32[8,64,128]{2,1,0:T(8,128)S(1)}, u32[]{:S(2)}, u32[]{:S(2)}) collective-permute-start(f32[8,64,128]{2,1,0:T(8,128)S(1)} %get-tuple-element.11), channel_id=1, source_target_pairs={{0,384},{128,0},{256,128},{384,256},{1,385},{129,1},{257,129},{385... | collective-permute-start | bytes 786440 | tf_op jit(solution)/shard_map/ppermute | solution.py:326
  149.6 12.0 %collective-permute-start.4 = (f32[8,64,128]{2,1,0:T(8,128)S(1)}, f32[8,64,128]{2,1,0:T(8,128)S(1)}, u32[]{:S(2)}, u32[]{:S(2)}) collective-permute-start(f32[8,64,128]{2,1,0:T(8,128)S(1)} %get-tuple-element.12), channel_id=1, source_target_pairs={{0,128},{128,256},{256,384},{384,0},{1,129},{129,257},{257,385},{3... | collective-permute-start | bytes 786440 | tf_op jit(solution)/shard_map/ppermute | solution.py:326
  161.7 11.9 %collective-permute-start.7 = (f32[4,64,128]{2,1,0:T(8,128)S(1)}, f32[4,64,128]{2,1,0:T(8,128)S(1)}, u32[]{:S(2)}, u32[]{:S(2)}) collective-permute-start(f32[4,64,128]{2,1,0:T(8,128)S(1)} %slice.29), channel_id=1, source_target_pairs={{0,78},{2,76},{4,74},{6,72},{8,70},{10,68},{12,66},{14,64},{64,14}... | collective-permute-start | bytes 393224 | tf_op jit(solution)/shard_map/ppermute | solution.py:323
